TPU v7x, 32 devices: a whole 2x2x4 slice. The times are simulated.
32 devices in a mesh: role: 2 (over y), dp: 16 (over z, x, core).
Axes of the slice: x: 2, y: 2, z: 4, core: 2. Of those that a mesh axis runs over, the one named last changes fastest.
Arguments:
- frames: bfloat16 [2, 2, 4096, 1024], P('role', None, 'dp'), may hold values from -6 to 6
- cotangent: bfloat16 [2, 2, 4096, 1024], P('role', None, 'dp'), may hold values from -6 to 6
- inner_weight: bfloat16 [2, 1024, 3072], P(None, 'dp'), may hold values from -0.1875 to 0.1875
- outer_weight: bfloat16 [2, 1024, 1024], P(None, 'dp'), may hold values from -0.5 to 0.5
- expand_weight: bfloat16 [2, 1024, 4096], P(None, 'dp'), may hold values from -0.1875 to 0.1875
- shrink_weight: bfloat16 [2, 4096, 1024], P(None, 'dp'), may hold values from -0.09375 to 0.09375
- causal_gain: bfloat16 [2, 1024], P(None, 'dp'), may hold values from 0.099609375 to 1.8984375
- causal_shift: bfloat16 [2, 1024], P(None, 'dp'), may hold values from -2 to 2
- section_scale: bfloat16 [7, 2, 1024], P(None, None, 'dp'), may hold values from 0.099609375 to 1.8984375
- section_shift: bfloat16 [7, 2, 1024], P(None, None, 'dp'), may hold values from -2 to 2
- prompt_lengths: int32 [2, 16, 4], P(None, 'dp'), may hold values from 1 to 128, 256 in all within a row
- target_lengths: int32 [2, 16, 4], P(None, 'dp'), may hold values from 1 to 128, 256 in all within a row
- sections: int32 [2, 16, 4], P(None, 'dp'), may hold values from 0 to 6
Outputs:
- mixed: bfloat16 [2, 2, 4096, 1024], P('role', None, 'dp')
- frames_grad: bfloat16 [2, 2, 4096, 1024], P('role', None, 'dp')
- inner_grad: float32 [2, 1024, 3072], P(None, 'dp')
- outer_grad: float32 [2, 1024, 1024], P(None, 'dp')
- expand_grad: float32 [2, 1024, 4096], P(None, 'dp')
- shrink_grad: float32 [2, 4096, 1024], P(None, 'dp')
- causal_gain_grad: float32 [2, 1024], P(None, 'dp')
- causal_shift_grad: float32 [2, 1024], P(None, 'dp')
- section_scale_grad: float32 [7, 2, 1024], P(None, None, 'dp')
- section_shift_grad: float32 [7, 2, 1024], P(None, None, 'dp')
Inputs may be any that keep to these rules, and one draw needn't show every extreme that they name: `prompt_lengths`: each row of 4 lengths sums to 256. `target_lengths`: each row of 4 lengths sums to 256.
All inputs are finite; a program needn't handle non-finite values.
Results may differ from a plain program's by a relative error of at most 0.018.
Values may be sent and summed in bfloat16 or wider, within the bound.
A program may use at most 320 MiB of HBM per device.

v0:
```python
import jax
import jax.numpy as jnp
from jax import lax
from jax.sharding import PartitionSpec as P

HEADS = 16
HD = 64


highest = lax.Precision.HIGHEST


def shifted_2(x, axis, by):
    peers = lax.axis_size(axis)
    pairs = [(i, i + by) for i in range(peers) if 0 <= i + by < peers]
    return lax.ppermute(x, axis, pairs)


def normalize(hidden):
    average = jnp.mean(hidden, axis=-1, keepdims=True)
    centred = hidden - average
    spread = jnp.mean(centred * centred, axis=-1, keepdims=True)
    return centred * lax.rsqrt(spread + 1e-05)


def affine_norm(hidden, picker, scale_column, shift_column):
    scale_rows = jnp.dot(picker, scale_column, precision=highest)
    shift_rows = jnp.dot(picker, shift_column, precision=highest)
    return scale_rows * normalize(hidden) + shift_rows


def norm_with_back(hidden, picker, scale_column, shift_column):

    def apply_norm(state, scales, shifts):
        return affine_norm(state, picker, scales, shifts)

    return jax.vjp(apply_norm, hidden, scale_column, shift_column)


def exact_gelu(inputs):
    return jax.nn.gelu(inputs, approximate=False)


def frame_tags(lengths, offsets, total_rows):
    places = jnp.arange(total_rows, dtype=jnp.int32)
    finish = jnp.cumsum(lengths)
    segment = jnp.sum((places[:, None] >= finish[None, :]).astype(jnp.int32), axis=1)
    member = segment[:, None] == jnp.arange(lengths.shape[0], dtype=jnp.int32)[None, :]
    shifted = offsets - (finish - lengths)
    position = places + jnp.sum(jnp.where(member, shifted[None, :], 0), axis=1)
    return (segment, position, member)


def fetch_forward(project, restore, expand, shrink, scale_table, shift_table):
    return (
        lax.all_gather(project, "dp", axis=0, tiled=True),
        lax.all_gather(restore, "dp", axis=0, tiled=True),
        lax.all_gather(expand, "dp", axis=0, tiled=True),
        lax.all_gather(shrink, "dp", axis=0, tiled=True),
        lax.all_gather(scale_table, "dp", axis=2, tiled=True),
        lax.all_gather(shift_table, "dp", axis=2, tiled=True),
    )


def fetch_backward(project, restore, expand, shrink, scale_table, shift_table):
    return (
        lax.all_gather(project, "dp", axis=0, tiled=True),
        lax.all_gather(restore, "dp", axis=0, tiled=True),
        lax.all_gather(expand, "dp", axis=0, tiled=True),
        lax.all_gather(shrink, "dp", axis=0, tiled=True),
        lax.all_gather(scale_table, "dp", axis=2, tiled=True),
        lax.all_gather(shift_table, "dp", axis=2, tiled=True),
    )


def scatter_each(grads):
    return (
        lax.psum_scatter(grads[0], "dp", scatter_dimension=0, tiled=True),
        lax.psum_scatter(grads[1], "dp", scatter_dimension=0, tiled=True),
        lax.psum_scatter(grads[2], "dp", scatter_dimension=0, tiled=True),
        lax.psum_scatter(grads[3], "dp", scatter_dimension=0, tiled=True),
        lax.psum_scatter(grads[4], "dp", scatter_dimension=2, tiled=True),
        lax.psum_scatter(grads[5], "dp", scatter_dimension=2, tiled=True),
    )


def score_block(queries, key_rows, allowed):
    scores = jnp.einsum(
        "qhd,khd->hqk", queries, key_rows, preferred_element_type=jnp.float32
    ) * HD ** (-0.5)
    return jnp.where(allowed[None], scores, -1e30)


def attend_forward(normed_low, project, allowed):
    total_rows = normed_low.shape[0]
    packed = jnp.dot(normed_low, project, preferred_element_type=jnp.float32).astype(jnp.bfloat16)
    packed = packed.reshape(total_rows, 3, HEADS, HD)
    queries = packed[:, 0]
    own_keys = packed[:, 1]
    own_values = packed[:, 2]
    far_keys, far_values = shifted_2((own_keys, own_values), "role", 1)
    key_rows = jnp.concatenate([far_keys, own_keys], axis=0)
    value_rows = jnp.concatenate([far_values, own_values], axis=0)
    scores = score_block(queries, key_rows, allowed)
    highest_score = jnp.max(scores, axis=-1, keepdims=True)
    exponent = jnp.exp(scores - highest_score)
    totals = jnp.sum(exponent, axis=-1, keepdims=True)
    softened = exponent / totals
    log_total = highest_score + jnp.log(totals)
    mixture = jnp.einsum(
        "hqk,khd->qhd",
        softened.astype(jnp.bfloat16),
        value_rows,
        preferred_element_type=jnp.float32,
    )
    mixture = mixture.astype(jnp.bfloat16).reshape(total_rows, HEADS * HD)
    return (mixture, (queries, key_rows, value_rows, log_total))


def attend_backward(grad_mixture, kept, allowed, normed_low, project):
    queries, key_rows, value_rows, log_total = kept
    total_rows = queries.shape[0]
    scores = score_block(queries, key_rows, allowed)
    softened = jnp.exp(scores - log_total)
    soft_low = softened.astype(jnp.bfloat16)
    grad_heads = grad_mixture.reshape(total_rows, HEADS, HD)
    grad_values = jnp.einsum(
        "hqk,qhd->khd", soft_low, grad_heads, preferred_element_type=jnp.float32
    )
    grad_soft = jnp.einsum(
        "qhd,khd->hqk", grad_heads, value_rows, preferred_element_type=jnp.float32
    )
    inner_sum = jnp.sum(softened * grad_soft, axis=-1, keepdims=True)
    grad_scores = (softened * (grad_soft - inner_sum)).astype(jnp.bfloat16)
    grad_queries = jnp.einsum(
        "hqk,khd->qhd", grad_scores, key_rows, preferred_element_type=jnp.float32
    ) * HD ** (-0.5)
    grad_keys = jnp.einsum(
        "hqk,qhd->khd", grad_scores, queries, preferred_element_type=jnp.float32
    ) * HD ** (-0.5)
    returned_keys, returned_values = (
        shifted_2(grad_keys[:total_rows].astype(jnp.bfloat16), "role", -1).astype(jnp.float32),
        shifted_2(grad_values[:total_rows].astype(jnp.bfloat16), "role", -1).astype(jnp.float32),
    )
    own_keys = grad_keys[total_rows:] + returned_keys
    own_values = grad_values[total_rows:] + returned_values
    grad_packed = jnp.stack([grad_queries, own_keys, own_values], axis=1).astype(jnp.bfloat16)
    grad_packed = grad_packed.reshape(total_rows, 3 * HEADS * HD)
    grad_project = jnp.dot(normed_low.T, grad_packed, preferred_element_type=jnp.float32)
    grad_normed = jnp.dot(grad_packed, project.T, preferred_element_type=jnp.float32)
    return (grad_project, grad_normed)


def layer_forward(hidden, full_set, picker, allowed):
    project, restore, expand, shrink, scale_table, shift_table = full_set
    scale_wide = scale_table.astype(jnp.float32)
    shift_wide = shift_table.astype(jnp.float32)
    first_norm, first_back = norm_with_back(hidden, picker, scale_wide[:, 0], shift_wide[:, 0])
    first_low = first_norm.astype(jnp.bfloat16)
    mixture, kept = attend_forward(first_low, project, allowed)
    middle = hidden + jnp.dot(mixture, restore, preferred_element_type=jnp.float32)
    second_norm, second_back = norm_with_back(middle, picker, scale_wide[:, 1], shift_wide[:, 1])
    second_low = second_norm.astype(jnp.bfloat16)
    upper = jnp.dot(second_low, expand, preferred_element_type=jnp.float32)
    lifted, gelu_back = jax.vjp(exact_gelu, upper)
    lifted_low = lifted.astype(jnp.bfloat16)
    result = middle + jnp.dot(lifted_low, shrink, preferred_element_type=jnp.float32)
    return (
        result,
        (first_back, first_low, mixture, kept, second_back, second_low, gelu_back, lifted_low),
    )


def layer_backward(grad_out, full_set, saved, allowed):
    project, restore, expand, shrink, scale_table, shift_table = full_set
    first_back, first_low, mixture, kept, second_back, second_low, gelu_back, lifted_low = saved
    grad_low = grad_out.astype(jnp.bfloat16)
    grad_shrink = jnp.dot(lifted_low.T, grad_low, preferred_element_type=jnp.float32)
    grad_lifted = jnp.dot(grad_low, shrink.T, preferred_element_type=jnp.float32)
    grad_upper = gelu_back(grad_lifted)[0].astype(jnp.bfloat16)
    grad_expand = jnp.dot(second_low.T, grad_upper, preferred_element_type=jnp.float32)
    grad_second = jnp.dot(grad_upper, expand.T, preferred_element_type=jnp.float32)
    grad_middle_norm, grad_scale_two, grad_shift_two = second_back(grad_second)
    grad_middle = grad_out + grad_middle_norm
    middle_low = grad_middle.astype(jnp.bfloat16)
    grad_restore = jnp.dot(mixture.T, middle_low, preferred_element_type=jnp.float32)
    grad_mixture = jnp.dot(middle_low, restore.T, preferred_element_type=jnp.float32).astype(
        jnp.bfloat16
    )
    grad_project, grad_first = attend_backward(grad_mixture, kept, allowed, first_low, project)
    grad_hidden_norm, grad_scale_one, grad_shift_one = first_back(grad_first)
    grad_hidden = grad_middle + grad_hidden_norm
    grad_scales = jnp.stack([grad_scale_one, grad_scale_two], axis=1)
    grad_shifts = jnp.stack([grad_shift_one, grad_shift_two], axis=1)
    return (
        grad_hidden,
        (grad_project, grad_restore, grad_expand, grad_shrink, grad_scales, grad_shifts),
    )


def body(
    frames,
    cotangent,
    inner_weight,
    outer_weight,
    expand_weight,
    shrink_weight,
    causal_gain,
    causal_shift,
    section_scale,
    section_shift,
    prompt_lengths,
    target_lengths,
    sections,
):
    role_index = lax.axis_index("role")
    is_target = role_index == 1
    micro_count = frames.shape[1]
    frame_rows = frames.shape[2]
    layer_tables = [(causal_gain[None], causal_shift[None]), (section_scale, section_shift)]
    shard_sets = []
    for layer_index in range(2):
        shard_sets.append(
            (
                inner_weight[layer_index],
                outer_weight[layer_index],
                expand_weight[layer_index],
                shrink_weight[layer_index],
                layer_tables[layer_index][0],
                layer_tables[layer_index][1],
            )
        )
    mixed_rows = []
    input_rows = []
    shard_totals = [None, None]
    for micro_step in range(micro_count):
        prompt_row = prompt_lengths[micro_step, 0]
        target_row = target_lengths[micro_step, 0]
        section_row = sections[micro_step, 0]
        prompt_segment, prompt_position, prompt_member = frame_tags(
            prompt_row, jnp.zeros_like(prompt_row), frame_rows
        )
        target_segment, target_position, target_member = frame_tags(
            target_row, prompt_row, frame_rows
        )
        own_segment = jnp.where(is_target, target_segment, prompt_segment)
        own_position = jnp.where(is_target, target_position, prompt_position)
        own_member = jnp.where(is_target, target_member, prompt_member)
        same_far = (own_segment[:, None] == prompt_segment[None, :]) & is_target
        same_own = own_segment[:, None] == own_segment[None, :]
        causal_own = same_own & (own_position[None, :] <= own_position[:, None])
        allowed_sets = [
            jnp.concatenate([same_far, causal_own], axis=1),
            jnp.concatenate([same_far, same_own], axis=1),
        ]
        section_frame = jnp.sum(jnp.where(own_member, section_row[None, :], 0), axis=1)
        section_picker = (
            section_frame[:, None] == jnp.arange(section_scale.shape[0], dtype=jnp.int32)[None, :]
        ).astype(jnp.float32)
        pickers = [jnp.ones((frame_rows, 1), jnp.float32), section_picker]
        hidden = frames[0, micro_step].astype(jnp.float32)
        kept_layers = []
        for layer_index in range(2):
            shard_set = shard_sets[layer_index]
            full_set = fetch_forward(
                shard_set[0], shard_set[1], shard_set[2], shard_set[3], shard_set[4], shard_set[5]
            )
            hidden, saved = layer_forward(
                hidden, full_set, pickers[layer_index], allowed_sets[layer_index]
            )
            kept_layers.append((full_set, saved))
        mixed_rows.append(hidden.astype(jnp.bfloat16))
        grad_hidden = cotangent[0, micro_step].astype(jnp.float32)
        for layer_index in (1, 0):
            full_set, saved = kept_layers[layer_index]
            shard_set = shard_sets[layer_index]
            full_set = fetch_backward(
                shard_set[0], shard_set[1], shard_set[2], shard_set[3], shard_set[4], shard_set[5]
            )
            grad_hidden, grads = layer_backward(
                grad_hidden, full_set, saved, allowed_sets[layer_index]
            )
            shards = scatter_each(grads)
            if shard_totals[layer_index] is None:
                shard_totals[layer_index] = shards
            else:
                shard_totals[layer_index] = jax.tree.map(jnp.add, shard_totals[layer_index], shards)
        input_rows.append(grad_hidden.astype(jnp.bfloat16))
    first_set = shard_totals[0]
    second_set = shard_totals[1]
    summed = (
        lax.psum(first_set[0].astype(jnp.bfloat16), "role").astype(jnp.float32),
        lax.psum(first_set[1].astype(jnp.bfloat16), "role").astype(jnp.float32),
        lax.psum(first_set[2].astype(jnp.bfloat16), "role").astype(jnp.float32),
        lax.psum(first_set[3].astype(jnp.bfloat16), "role").astype(jnp.float32),
        lax.psum(first_set[4].astype(jnp.bfloat16), "role").astype(jnp.float32),
        lax.psum(first_set[5].astype(jnp.bfloat16), "role").astype(jnp.float32),
        lax.psum(second_set[0].astype(jnp.bfloat16), "role").astype(jnp.float32),
        lax.psum(second_set[1].astype(jnp.bfloat16), "role").astype(jnp.float32),
        lax.psum(second_set[2].astype(jnp.bfloat16), "role").astype(jnp.float32),
        lax.psum(second_set[3].astype(jnp.bfloat16), "role").astype(jnp.float32),
        lax.psum(second_set[4].astype(jnp.bfloat16), "role").astype(jnp.float32),
        lax.psum(second_set[5].astype(jnp.bfloat16), "role").astype(jnp.float32),
    )
    mixed = jnp.stack(mixed_rows, axis=0)[None]
    frames_grad = jnp.stack(input_rows, axis=0)[None]
    inner_grad = jnp.stack([summed[0], summed[6]], axis=0)
    outer_grad = jnp.stack([summed[1], summed[7]], axis=0)
    expand_grad = jnp.stack([summed[2], summed[8]], axis=0)
    shrink_grad = jnp.stack([summed[3], summed[9]], axis=0)
    return (
        mixed,
        frames_grad,
        inner_grad,
        outer_grad,
        expand_grad,
        shrink_grad,
        summed[4][0],
        summed[5][0],
        summed[10],
        summed[11],
    )


def solution(mesh):
    placed = (
        P("role", None, "dp", None),
        P("role", None, "dp", None),
        P(None, "dp", None),
        P(None, "dp", None),
        P(None, "dp", None),
        P(None, "dp", None),
        P(None, "dp"),
        P(None, "dp"),
        P(None, None, "dp"),
        P(None, None, "dp"),
        P(None, "dp", None),
        P(None, "dp", None),
        P(None, "dp", None),
    )
    return jax.shard_map(
        body,
        mesh=mesh,
        in_specs=placed,
        out_specs=(
            P("role", None, "dp", None),
            P("role", None, "dp", None),
            P(None, "dp", None),
            P(None, "dp", None),
            P(None, "dp", None),
            P(None, "dp", None),
            P(None, "dp"),
            P(None, "dp"),
            P(None, None, "dp"),
            P(None, None, "dp"),
        ),
        check_vma=False,
    )
```

profile of v0, /device:TPU:0, one launch (start us, length us, event | category | flops | bytes accessed | tf_op | source)
XLA Modules:
  0.0 2126.4 jit_solution(18243364698282841242)
XLA Ops:
  18.6 26.2 %all_gather.30 = bf16[7,2,1024]{0,1,2:T(2,128)(2,1)S(1)} all-gather(bf16[7,2,64]{0,1,2:T(2,128)(2,1)S(1)} %copy.80), channel_id=1, replica_groups=mesh['role'=2,'dp'=16] {'dp'}, dimensions={2}, use_global_device_ids=true | all-gather | bytes 30464 | tf_op jit(solution)/shard_map/all_gather | solution.py:60
  52.3 17.7 all-gather.10
  70.1 18.4 all-gather.11
  88.8 19.6 all_gather.31
  144.1 25.0 %collective-permute-done = bf16[256,16,64]{0,2,1:T(8,128)(2,1)S(1)} collective-permute-done((bf16[256,16,64]{0,2,1:T(8,128)(2,1)S(1)}, bf16[256,16,64]{0,2,1:T(8,128)(2,1)S(1)}, u32[]{:S(2)}, u32[]{:S(2)}) %collective-permute-start) | collective-permute-done | bytes 524320 | tf_op jit(solution)/shard_map/ppermute | solution.py:16
  187.3 10.5 all-gather.25.cloned.1.call-done
  197.7 16.2 multiply_convert_fusion.5
  214.0 59.6 %all-gather.27.cloned.1.call-done = bf16[1,4096,1024]{2,1,0:T(8,128)(2,1)} async-done(((bf16[1,256,1024]{2,1,0:T(8,128)(2,1)}), bf16[1,4096,1024]{2,1,0:T(8,128)(2,1)}) %all-gather.27.cloned.1.call-update) | async-done | bytes 8388624 | tf_op jit(solution)/shard_map/all_gather | solution.py:59
  281.5 54.4 %all-gather.29.cloned.1.call-done = bf16[1,1024,3072]{2,1,0:T(8,128)(2,1)} async-done(((bf16[1,64,3072]{2,1,0:T(8,128)(2,1)}), bf16[1,1024,3072]{2,1,0:T(8,128)(2,1)}) %all-gather.29.cloned.1.call-update) | async-done | bytes 6291472 | tf_op jit(solution)/shard_map/all_gather | solution.py:56
  351.2 16.4 multiply_convert_fusion.7
  397.3 56.3 %all-gather.33.cloned.1.call-done = bf16[1,1024,4096]{2,1,0:T(8,128)(2,1)} async-done(((bf16[1,64,4096]{2,1,0:T(8,128)(2,1)}), bf16[1,1024,4096]{2,1,0:T(8,128)(2,1)}) %all-gather.33.cloned.1.call-update) | async-done | bytes 8388624 | tf_op jit(solution)/shard_map/all_gather | solution.py:58
  453.6 15.7 multiply_convert_fusion.4
  469.4 59.6 %all-gather.35.cloned.1.call-done = bf16[1,4096,1024]{2,1,0:T(8,128)(2,1)} async-done(((bf16[1,256,1024]{2,1,0:T(8,128)(2,1)}), bf16[1,4096,1024]{2,1,0:T(8,128)(2,1)}) %all-gather.35.cloned.1.call-update) | async-done | bytes 8388624 | tf_op jit(solution)/shard_map/all_gather | solution.py:59
  529.0 11.8 add_convert_fusion.1
  557.9 12.5 multiply_convert_fusion.6
  570.4 10.9 add_convert_fusion.3
  669.8 11.1 add_convert_fusion
  687.6 11.3 add_convert_fusion.2
  806.3 10.7 convolution_add_fusion.2
  822.2 10.4 convolution_add_fusion
  852.4 10.2 convolution_add_fusion.1
  911.7 11.5 reduce-scatter.23.cloned.1.call-done
  925.1 135.9 %reduce-scatter.21.cloned.1.call-done = f32[64,3072]{1,0:T(8,128)} async-done(((f32[1024,3072]{1,0:T(8,128)}), f32[64,3072]{1,0:T(8,128)}) %reduce-scatter.21.cloned.1.call-update) | async-done | bytes 786448 | tf_op jit(solution)/shard_map/reduce_scatter | solution.py:78
  1063.0 180.0 %reduce-scatter.31.cloned.1.call-done = f32[64,4096]{1,0:T(8,128)} async-done(((f32[1024,4096]{1,0:T(8,128)}), f32[64,4096]{1,0:T(8,128)}) %reduce-scatter.31.cloned.1.call-update) | async-done | bytes 1048592 | tf_op jit(solution)/shard_map/reduce_scatter | solution.py:80
  1245.0 179.5 %reduce-scatter.35.cloned.1.call-done = f32[256,1024]{1,0:T(8,128)} async-done(((f32[4096,1024]{1,0:T(8,128)}), f32[256,1024]{1,0:T(8,128)}) %reduce-scatter.35.cloned.1.call-update) | async-done | bytes 1048592 | tf_op jit(solution)/shard_map/reduce_scatter | solution.py:81
  1426.7 179.5 %reduce-scatter.29.cloned.1.call-done = f32[64,4096]{1,0:T(8,128)} async-done(((f32[1024,4096]{1,0:T(8,128)}), f32[64,4096]{1,0:T(8,128)}) %reduce-scatter.29.cloned.1.call-update) | async-done | bytes 1048592 | tf_op jit(solution)/shard_map/reduce_scatter | solution.py:80
  1608.2 179.5 %reduce-scatter.33.cloned.1.call-done = f32[256,1024]{1,0:T(8,128)} async-done(((f32[4096,1024]{1,0:T(8,128)}), f32[256,1024]{1,0:T(8,128)}) %reduce-scatter.33.cloned.1.call-update) | async-done | bytes 1048592 | tf_op jit(solution)/shard_map/reduce_scatter | solution.py:81
  1803.4 42.6 %reduce-scatter.41.cloned.1.call-done = f32[64,14]{1,0:T(8,128)} async-done(((f32[1024,14]{1,0:T(8,128)}), f32[64,14]{1,0:T(8,128)}) %reduce-scatter.41.cloned.1.call-update) | async-done | bytes 3600
  1846.9 57.8 %reduce-scatter.43.cloned.1.call-done = f32[64,14]{1,0:T(8,128)} async-done(((f32[1024,14]{1,0:T(8,128)}), f32[64,14]{1,0:T(8,128)}) %reduce-scatter.43.cloned.1.call-update) | async-done | bytes 3600
  1911.6 51.4 %reduce-scatter.39.cloned.1.call-done = f32[64,2]{1,0:T(8,128)} async-done(((f32[1024,2]{1,0:T(8,128)}), f32[64,2]{1,0:T(8,128)}) %reduce-scatter.39.cloned.1.call-update) | async-done | bytes 528
  1963.9 57.8 %reduce-scatter.37.cloned.1.call-done = f32[64,2]{1,0:T(8,128)} async-done(((f32[1024,2]{1,0:T(8,128)}), f32[64,2]{1,0:T(8,128)}) %reduce-scatter.37.cloned.1.call-update) | async-done | bytes 528
  2029.9 81.1 %all-reduce.4.cloned.1.call-done = (bf16[1,64,3072]{2,1,0:T(8,128)(2,1)}, bf16[1,64,3072]{2,1,0:T(8,128)(2,1)}, bf16[1,64,1024]{2,1,0:T(8,128)(2,1)}, bf16[1,64,...) async-done(((bf16[1,64,3072]{2,1,0:T(8,128)(2,1)}, ...) | async-done | bytes 3145744 | tf_op jit(solution)/shard_map/psum | solution.py:298
  (732 shorter events, 467.4 us)
Async XLA Ops:
  7.2 104.3 %all-gather.21.cloned.1.call-start = ((), (), s32[]{:S(2)}) async-start(), calls=%async_computation.12 | async-start | bytes 6684672 | tf_op jit(solution)/shard_map/all_gather | solution.py:56
  9.4 163.5 %all-gather.23.cloned.1.call-start = ((), (), s32[]{:S(2)}) async-start(), calls=%async_computation.13 | async-start | bytes 2228224 | tf_op jit(solution)/shard_map/all_gather | solution.py:57
  11.2 186.6 %all-gather.25.cloned.1.call-start = ((), (), s32[]{:S(2)}) async-start(), calls=%async_computation.14 | async-start | bytes 8912896 | tf_op jit(solution)/shard_map/all_gather | solution.py:58
  13.5 260.1 %all-gather.27.cloned.1.call-start = ((), (), s32[]{:S(2)}) async-start(), calls=%async_computation.15 | async-start | bytes 8912896 | tf_op jit(solution)/shard_map/all_gather | solution.py:59
  14.6 321.3 %all-gather.29.cloned.1.call-start = ((), (), s32[]{:S(2)}) async-start(), calls=%async_computation.16 | async-start | bytes 6684672 | tf_op jit(solution)/shard_map/all_gather | solution.py:56
  15.2 377.9 %all-gather.31.cloned.1.call-start = ((), (), s32[]{:S(2)}) async-start(), calls=%async_computation.17 | async-start | bytes 2228224 | tf_op jit(solution)/shard_map/all_gather | solution.py:57
  15.8 437.9 %all-gather.33.cloned.1.call-start = ((), (), s32[]{:S(2)}) async-start(), calls=%async_computation.18 | async-start | bytes 8912896 | tf_op jit(solution)/shard_map/all_gather | solution.py:58
  16.5 512.5 %all-gather.35.cloned.1.call-start = ((), (), s32[]{:S(2)}) async-start(), calls=%async_computation.19 | async-start | bytes 8912896 | tf_op jit(solution)/shard_map/all_gather | solution.py:59
  17.3 891.2 %reduce-scatter.27.cloned.1.call-start = ((), (), s32[]{:S(2)}) async-start(), calls=%async_computation.23 | async-start | bytes 4456448 | tf_op jit(solution)/shard_map/reduce_scatter | solution.py:79
  133.1 48.0 %collective-permute-start.4 = (bf16[256,16,64]{0,2,1:T(8,128)(2,1)}, bf16[256,16,64]{0,2,1:T(8,128)(2,1)}, u32[]{:S(2)}, u32[]{:S(2)}) collective-permute-start(bf16[256,16,64]{0,2,1:T(8,128)(2,1)} %get-tuple-element.104), channel_id=1, source_target_pairs={{0,16},{1,17},{2,18},{3,19},{4,20},{5,21},{6,22},{7,23},{8,24},{9,... | collective-permute-start | bytes 1572872 | tf_op jit(solution)/shard_map/ppermute | solution.py:16
  135.2 40.6 %collective-permute-start.5 = (bf16[256,16,64]{0,2,1:T(8,128)(2,1)}, bf16[256,16,64]{0,2,1:T(8,128)(2,1)}, u32[]{:S(2)}, u32[]{:S(2)}) collective-permute-start(bf16[256,16,64]{0,2,1:T(8,128)(2,1)} %get-tuple-element.105), channel_id=1, source_target_pairs={{0,16},{1,17},{2,18},{3,19},{4,20},{5,21},{6,22},{7,23},{8,24},{9,... | collective-permute-start | bytes 1572872 | tf_op jit(solution)/shard_map/ppermute | solution.py:16
  137.3 31.8 %collective-permute-start = (bf16[256,16,64]{0,2,1:T(8,128)(2,1)S(1)}, bf16[256,16,64]{0,2,1:T(8,128)(2,1)S(1)}, u32[]{:S(2)}, u32[]{:S(2)}) collective-permute-start(bf16[256,16,64]{0,2,1:T(8,128)(2,1)S(1)} %get-tuple-element.100), channel_id=1, source_target_pairs={{0,16},{1,17},{2,18},{3,19},{4,20},{5,21},{6,22},{7,23},{8,24},{9,... | collective-permute-start | bytes 1572872 | tf_op jit(solution)/shard_map/ppermute | solution.py:16
  344.4 43.2 %collective-permute-start.6 = (bf16[256,16,64]{0,2,1:T(8,128)(2,1)}, bf16[256,16,64]{0,2,1:T(8,128)(2,1)}, u32[]{:S(2)}, u32[]{:S(2)}) collective-permute-start(bf16[256,16,64]{0,2,1:T(8,128)(2,1)} %get-tuple-element.102), channel_id=1, source_target_pairs={{0,16},{1,17},{2,18},{3,19},{4,20},{5,21},{6,22},{7,23},{8,24},{9,... | collective-permute-start | bytes 1572872 | tf_op jit(solution)/shard_map/ppermute | solution.py:16
  348.8 33.5 %collective-permute-start.7 = (bf16[256,16,64]{0,2,1:T(8,128)(2,1)}, bf16[256,16,64]{0,2,1:T(8,128)(2,1)}, u32[]{:S(2)}, u32[]{:S(2)}) collective-permute-start(bf16[256,16,64]{0,2,1:T(8,128)(2,1)} %get-tuple-element.103), channel_id=1, source_target_pairs={{0,16},{1,17},{2,18},{3,19},{4,20},{5,21},{6,22},{7,23},{8,24},{9,... | collective-permute-start | bytes 1572872 | tf_op jit(solution)/shard_map/ppermute | solution.py:16
  378.2 171.5 %collective-permute-start.2 = (bf16[256,16,64]{0,2,1:T(8,128)(2,1)}, bf16[256,16,64]{0,2,1:T(8,128)(2,1)}, u32[]{:S(2)}, u32[]{:S(2)}) collective-permute-start(bf16[256,16,64]{0,2,1:T(8,128)(2,1)} %get-tuple-element.98), channel_id=1, source_target_pairs={{0,16},{1,17},{2,18},{3,19},{4,20},{5,21},{6,22},{7,23},{8,24},{9,... | collective-permute-start | bytes 1572872 | tf_op jit(solution)/shard_map/ppermute | solution.py:16
  380.3 163.6 %collective-permute-start.3 = (bf16[256,16,64]{0,2,1:T(8,128)(2,1)}, bf16[256,16,64]{0,2,1:T(8,128)(2,1)}, u32[]{:S(2)}, u32[]{:S(2)}) collective-permute-start(bf16[256,16,64]{0,2,1:T(8,128)(2,1)} %get-tuple-element.99), channel_id=1, source_target_pairs={{0,16},{1,17},{2,18},{3,19},{4,20},{5,21},{6,22},{7,23},{8,24},{9,... | collective-permute-start | bytes 1572872 | tf_op jit(solution)/shard_map/ppermute | solution.py:16
  607.8 53.7 %collective-permute-start.9 = (bf16[256,16,64]{0,2,1:T(8,128)(2,1)}, bf16[256,16,64]{0,2,1:T(8,128)(2,1)}, u32[]{:S(2)}, u32[]{:S(2)}) collective-permute-start(bf16[256,16,64]{0,2,1:T(8,128)(2,1)} %slice.410), channel_id=1, source_target_pairs={{16,0},{17,1},{18,2},{19,3},{20,4},{21,5},{22,6},{23,7},{24,8},{25... | collective-permute-start | bytes 1572872 | tf_op jit(solution)/shard_map/ppermute | solution.py:16
  615.8 35.9 %collective-permute-start.13 = (bf16[256,16,64]{0,2,1:T(8,128)(2,1)}, bf16[256,16,64]{0,2,1:T(8,128)(2,1)}, u32[]{:S(2)}, u32[]{:S(2)}) collective-permute-start(bf16[256,16,64]{0,2,1:T(8,128)(2,1)} %slice.406), channel_id=1, source_target_pairs={{16,0},{17,1},{18,2},{19,3},{20,4},{21,5},{22,6},{23,7},{24,8},{25... | collective-permute-start | bytes 1572872 | tf_op jit(solution)/shard_map/ppermute | solution.py:16
  619.8 290.2 %reduce-scatter.25.cloned.1.call-start = ((), (), s32[]{:S(2)}) async-start(), calls=%async_computation.22 | async-start | bytes 4456448 | tf_op jit(solution)/shard_map/reduce_scatter | solution.py:79
  711.3 211.9 %reduce-scatter.23.cloned.1.call-start = ((), (), s32[]{:S(2)}) async-start(), calls=%async_computation.21 | async-start | bytes 13369344 | tf_op jit(solution)/shard_map/reduce_scatter | solution.py:78
  721.7 339.3 %reduce-scatter.21.cloned.1.call-start = ((), (), s32[]{:S(2)}) async-start(), calls=%async_computation.20 | async-start | bytes 13369344 | tf_op jit(solution)/shard_map/reduce_scatter | solution.py:78
  736.0 42.6 %collective-permute-start.15 = (bf16[256,16,64]{0,2,1:T(8,128)(2,1)S(1)}, bf16[256,16,64]{0,2,1:T(8,128)(2,1)}, u32[]{:S(2)}, u32[]{:S(2)}) collective-permute-start(bf16[256,16,64]{0,2,1:T(8,128)(2,1)S(1)} %slice.404), channel_id=1, source_target_pairs={{16,0},{17,1},{18,2},{19,3},{20,4},{21,5},{22,6},{23,7},{24,8},{25... | collective-permute-start | bytes 1572872 | tf_op jit(solution)/shard_map/ppermute | solution.py:16
  742.9 34.0 %collective-permute-start.11 = (bf16[256,16,64]{0,2,1:T(8,128)(2,1)}, bf16[256,16,64]{0,2,1:T(8,128)(2,1)}, u32[]{:S(2)}, u32[]{:S(2)}) collective-permute-start(bf16[256,16,64]{0,2,1:T(8,128)(2,1)} %slice.408), channel_id=1, source_target_pairs={{16,0},{17,1},{18,2},{19,3},{20,4},{21,5},{22,6},{23,7},{24,8},{25... | collective-permute-start | bytes 1572872 | tf_op jit(solution)/shard_map/ppermute | solution.py:16
  800.8 442.1 %reduce-scatter.31.cloned.1.call-start = ((), (), s32[]{:S(2)}) async-start(), calls=%async_computation.25 | async-start | bytes 17825792 | tf_op jit(solution)/shard_map/reduce_scatter | solution.py:80
  817.0 607.6 %reduce-scatter.35.cloned.1.call-start = ((), (), s32[]{:S(2)}) async-start(), calls=%async_computation.27 | async-start | bytes 17825792 | tf_op jit(solution)/shard_map/reduce_scatter | solution.py:81
  832.7 773.5 %reduce-scatter.29.cloned.1.call-start = ((), (), s32[]{:S(2)}) async-start(), calls=%async_computation.24 | async-start | bytes 17825792 | tf_op jit(solution)/shard_map/reduce_scatter | solution.py:80
  847.8 939.9 %reduce-scatter.33.cloned.1.call-start = ((), (), s32[]{:S(2)}) async-start(), calls=%async_computation.26 | async-start | bytes 17825792 | tf_op jit(solution)/shard_map/reduce_scatter | solution.py:81
  862.7 983.3 %reduce-scatter.41.cloned.1.call-start = ((), (), s32[]{:S(2)}) async-start(), calls=%async_computation.30 | async-start | bytes 557056
  889.2 1015.5 %reduce-scatter.43.cloned.1.call-start = ((), (), s32[]{:S(2)}) async-start(), calls=%async_computation.31 | async-start | bytes 557056
  891.4 1071.7 %reduce-scatter.39.cloned.1.call-start = ((), (), s32[]{:S(2)}) async-start(), calls=%async_computation.29 | async-start | bytes 557056
  906.8 1114.9 %reduce-scatter.37.cloned.1.call-start = ((), (), s32[]{:S(2)}) async-start(), calls=%async_computation.28 | async-start | bytes 557056
  907.9 1203.1 %all-reduce.4.cloned.1.call-start = ((), (), s32[]{:S(2)}) async-start(), calls=%async_computation.32 | async-start | bytes 6291456 | tf_op jit(solution)/shard_map/psum | solution.py:298
  (202 other events, 5745.8 us)
Sparse Core Ops, SparseCore 0:
  10.9 67.0 all-gather.20
  80.7 40.5 all-gather.22
  124.0 73.6 all-gather.24
  200.3 73.2 all-gather.26
  275.7 60.0 all-gather.28
  337.9 39.8 all-gather.30
  379.9 73.6 all-gather.32
  455.8 73.1 all-gather.34
  620.0 73.3 reduce-scatter.26
  711.5 73.7 reduce-scatter.24
  789.3 133.8 reduce-scatter.22
  927.1 133.9 reduce-scatter.20
  1065.2 177.7 reduce-scatter.30
  1246.9 177.5 reduce-scatter.34
  1428.5 177.5 reduce-scatter.28
  1610.1 177.5 reduce-scatter.32
  1791.1 54.7 reduce-scatter.40
  1849.8 54.8 reduce-scatter.42
  1908.2 54.7 reduce-scatter.38
  1966.8 54.8 reduce-scatter.36
  2025.0 85.9 all-reduce.3
where the time goes:
time: 2140 us; the launch traced here: 2130 us
  waiting for transfers between devices  1440 us (67%)
  matrix products  410 us (19%)
  blocking collectives  86.9 us (4%)
  other arithmetic  73.8 us (3%)
  local copies, waits for them, and re-layouts  68.6 us (3%)
  starting transfers between devices  34.3 us (2%)
    reduce_scatter x2, waiting for transfers between devices, scatter_each(): lax.psum_scatter(grads[2], 'dp', scatter_dimension=0, tiled=True)  359 us
    reduce_scatter x2, waiting for transfers between devices, scatter_each(): lax.psum_scatter(grads[3], 'dp', scatter_dimension=0, tiled=True)  359 us
    unnamed x25, waiting for transfers between devices  212 us
    reduce_scatter x2, waiting for transfers between devices, scatter_each(): lax.psum_scatter(grads[0], 'dp', scatter_dimension=0, tiled=True)  147 us
    all_gather x2, waiting for transfers between devices, fetch_forward(): lax.all_gather(shrink, 'dp', axis=0, tiled=True)  119 us
    psum x1, waiting for transfers between devices, body(): lax.psum(second_set[0].astype(jnp.bfloat16), 'role').astype(jnp.float32)  81.1 us
    all_gather x2, waiting for transfers between devices, fetch_forward(): lax.all_gather(expand, 'dp', axis=0, tiled=True)  66.8 us
    dot_general x4, matrix products, layer_forward(): upper = jnp.dot(second_low, expand, preferred_element_type=jnp.float32)  60.9 us
  transfers between devices with their start and end apart: 37, of which 20 were waited for; matrix products, arithmetic and copies ran while one was open for 22% of the time, Pallas kernels for 0%

commit v1 on v0

v1 whole, which is shorter than its diff:
```python
import functools

import jax
import jax.numpy as jnp
from jax import lax
from jax.experimental import pallas as pl
from jax.experimental.pallas import tpu as pltpu
from jax.sharding import PartitionSpec as P

HEADS = 16
HD = 64
MESH = pl.DeviceIdType.MESH
SLOTS = 4
F32 = jnp.float32
BF16 = jnp.bfloat16


class Place:
    def __init__(self, outer_count):
        self.outers = outer_count
        self.role = lax.axis_index("role")
        dp = lax.axis_index("dp")
        self.core = dp % 2
        self.pair = (dp // 2) % 2
        self.outer = dp // 4
        self.dp = dp

    def at(self, role, outer, pair, core):
        return (role, (outer * 2 + pair) * 2 + core)

    def sibling(self):
        return self.at(self.role, self.outer, self.pair, 1 - self.core)

    def across(self):
        return self.at(self.role, self.outer, 1 - self.pair, self.core)

    def other_role(self):
        return self.at(1 - self.role, self.outer, self.pair, self.core)

    def along(self, by):
        return self.at(self.role, (self.outer + by) % self.outers, self.pair, self.core)

    def greet(self):
        barrier = pltpu.get_barrier_semaphore()
        peers = [self.sibling(), self.across(), self.other_role()]
        peers += [self.along(by) for by in range(1, self.outers)]
        for peer in peers:
            pl.semaphore_signal(barrier, inc=1, device_id=peer, device_id_type=MESH)
        pl.semaphore_wait(barrier, len(peers))


def remote(src, dst, send, recv, peer):
    return pltpu.make_async_remote_copy(
        src_ref=src, dst_ref=dst, send_sem=send, recv_sem=recv, device_id=peer, device_id_type=MESH
    )


def gather_kernel(count, outers, split, part_ref, full_ref, own_sem, zs, zr, xs, xr, us, ur, vs, vr, cs, cr):
    me = Place(outers)
    width = part_ref.shape[-1]
    main = width - split
    main_cols = pl.ds(pl.multiple_of(me.role * split, 128), main)
    give_cols = pl.ds(pl.multiple_of(me.role * main, 128), split)
    take_cols = pl.ds(pl.multiple_of((1 - me.role) * main, 128), split)
    me.greet()

    def own(k):
        return pltpu.make_async_copy(part_ref.at[k], full_ref.at[k, me.outer, me.pair, me.core], own_sem.at[k % SLOTS])

    def z_copy(k, by):
        s = k % SLOTS
        return remote(
            part_ref.at[k, :, main_cols],
            full_ref.at[k, me.outer, me.pair, me.core, :, main_cols],
            zs.at[s, by - 1], zr.at[s, by - 1], me.along(by),
        )

    def z_wait(k, by):
        s = k % SLOTS
        dst = full_ref.at[k, (me.outer - by + outers) % outers, me.pair, me.core, :, main_cols]
        remote(dst, dst, zs.at[s, by - 1], zr.at[s, by - 1], me.along(by)).wait_recv()

    def x_copy(k, pair):
        s = k % SLOTS
        ref = full_ref.at[k, :, pair, me.core, :, main_cols]
        return remote(ref, ref, xs.at[s], xr.at[s], me.across())

    def u_copy(k, by, cols):
        s = k % (2 * SLOTS)
        ref = full_ref.at[k, (me.outer - by + outers) % outers, me.pair, me.core, :, cols]
        return remote(ref, ref, us.at[s, by - 1], ur.at[s, by - 1], me.other_role())

    def v_copy(k, cols):
        s = k % SLOTS
        ref = full_ref.at[k, :, 1 - me.pair, me.core, :, cols]
        return remote(ref, ref, vs.at[s], vr.at[s], me.other_role())

    def c_copy(k, core):
        s = k % SLOTS
        ref = full_ref.at[k, :, :, core]
        return remote(ref, ref, cs.at[s], cr.at[s], me.sibling())

    def step(t, _):
        @pl.when(t < count)
        def _():
            own(t).start()
            for by in range(1, outers):
                z_copy(t, by).start()

        @pl.when((t >= 1) & (t < count + 1))
        def _():
            k = t - 1
            own(k).wait()
            for by in range(1, outers):
                z_wait(k, by)
            x_copy(k, me.pair).start()
            for by in range(1, outers):
                u_copy(k, by, give_cols).start()

        @pl.when((t >= 2) & (t < count + 2))
        def _():
            k = t - 2
            x_copy(k, 1 - me.pair).wait_recv()
            v_copy(k, give_cols).start()

        @pl.when((t >= 3) & (t < count + 3))
        def _():
            k = t - 3
            for by in range(1, outers):
                u_copy(k, by, take_cols).wait_recv()
            v_copy(k, take_cols).wait_recv()
            c_copy(k, me.core).start()
            for by in range(1, outers):
                z_copy(k, by).wait_send()
                u_copy(k, by, give_cols).wait_send()
            x_copy(k, me.pair).wait_send()
            v_copy(k, give_cols).wait_send()

        @pl.when(t >= 4)
        def _():
            k = t - 4
            c_copy(k, 1 - me.core).wait_recv()
            c_copy(k, me.core).wait_send()

        return 0

    lax.fori_loop(0, count + 4, step, 0)


def gather_all(parts, outers, split, collective_id):
    count, rows, width = parts.shape
    dma = pltpu.SemaphoreType.DMA
    many = outers - 1
    return pl.pallas_call(
        functools.partial(gather_kernel, count, outers, split),
        out_shape=jax.ShapeDtypeStruct((count, outers, 2, 2, rows, width), parts.dtype),
        in_specs=[pl.BlockSpec(memory_space=pl.ANY)],
        out_specs=pl.BlockSpec(memory_space=pl.ANY),
        scratch_shapes=[
            dma((SLOTS,)),
            dma((SLOTS, many)), dma((SLOTS, many)),
            dma((SLOTS,)), dma((SLOTS,)),
            dma((2 * SLOTS, many)), dma((2 * SLOTS, many)),
            dma((SLOTS,)), dma((SLOTS,)),
            dma((SLOTS,)), dma((SLOTS,)),
        ],
        compiler_params=pltpu.CompilerParams(collective_id=collective_id, has_side_effects=True),
        name="gather_weights",
    )(parts)


def reduce_kernel(
    count, outers, split, grad_ref, out_ref,
    own_buf, core_buf, role_buf, pair_buf, outer_buf, last_buf, sum_buf, low_buf, end_buf, fin_buf,
    own_sem, cs, cr, ys, yr, xs, xr, zs, zr, es, er, fs,
):
    me = Place(outers)
    width = grad_ref.shape[-1]
    main = width - split
    rows = grad_ref.shape[-2]
    main_cols = pl.ds(pl.multiple_of(me.role * split, 128), main)
    keep_cols = pl.ds(pl.multiple_of(me.role * main, 128), split)
    give_cols = pl.ds(pl.multiple_of((1 - me.role) * main, 128), split)
    me.greet()

    def own(k):
        return pltpu.make_async_copy(grad_ref.at[k, :, :, me.core], own_buf.at[k % SLOTS], own_sem.at[k % SLOTS])

    def c_copy(k):
        s = k % SLOTS
        return remote(grad_ref.at[k, :, :, 1 - me.core], core_buf.at[s], cs.at[s], cr.at[s], me.sibling())

    def y_copy(k):
        s = k % SLOTS
        return remote(sum_buf.at[s, :, :, :, give_cols], role_buf.at[s], ys.at[s], yr.at[s], me.other_role())

    def x_copy(k):
        s = k % SLOTS
        return remote(sum_buf.at[s, :, 1 - me.pair, :, main_cols], pair_buf.at[s], xs.at[s], xr.at[s], me.across())

    def z_copy(k, by):
        s = k % SLOTS
        return remote(
            low_buf.at[s, (me.outer + by) % outers], outer_buf.at[s, by - 1], zs.at[s, by - 1], zr.at[s, by - 1], me.along(by)
        )

    def e_copy(k):
        s = k % SLOTS
        return remote(end_buf.at[s], last_buf.at[s], es.at[s], er.at[s], me.other_role())

    def f_copy(k):
        s = k % SLOTS
        return pltpu.make_async_copy(fin_buf.at[s], out_ref.at[k], fs.at[s])

    def step(t, _):
        @pl.when(t < count)
        def _():
            own(t).start()
            c_copy(t).start()

        @pl.when((t >= 1) & (t < count + 1))
        def _():
            k = t - 1
            s = k % SLOTS
            own(k).wait()
            c_copy(k).wait()
            for o in range(outers):
                for p in range(2):
                    sum_buf[s, o, p] = (own_buf[s, o, p].astype(F32) + core_buf[s, o, p].astype(F32)).astype(BF16)
            y_copy(k).start()

        @pl.when((t >= 2) & (t < count + 2))
        def _():
            k = t - 2
            s = k % SLOTS
            y_copy(k).wait()
            for o in range(outers):
                for p in range(2):
                    had = sum_buf[s, o, p, :, keep_cols].astype(F32)
                    sum_buf[s, o, p, :, keep_cols] = (had + role_buf[s, o, p].astype(F32)).astype(BF16)
            x_copy(k).start()

        @pl.when((t >= 3) & (t < count + 3))
        def _():
            k = t - 3
            s = k % SLOTS
            x_copy(k).wait()
            for o in range(outers):
                had = sum_buf[s, o, me.pair, :, main_cols].astype(F32)
                low_buf[s, o] = (had + pair_buf[s, o].astype(F32)).astype(BF16)
            for by in range(1, outers):
                z_copy(k, by).start()

        @pl.when((t >= 4) & (t < count + 4))
        def _():
            k = t - 4
            s = k % SLOTS
            for by in range(1, outers):
                z_copy(k, by).wait()
            total = low_buf[s, me.outer].astype(F32)
            for by in range(1, outers):
                total = total + outer_buf[s, by - 1].astype(F32)
            end_buf[s] = total.astype(BF16)
            e_copy(k).start()

        @pl.when((t >= 5) & (t < count + 5))
        def _():
            k = t - 5
            s = k % SLOTS
            e_copy(k).wait()

            @pl.when(k >= SLOTS)
            def _():
                f_copy(k - SLOTS).wait()

            mid = main - split
            mine = end_buf[s].astype(F32)
            theirs = last_buf[s].astype(F32)

            @pl.when(me.role == 0)
            def _():
                fin_buf[s, :, :split] = mine[:, :split]
                fin_buf[s, :, split:main] = mine[:, split:] + theirs[:, :mid]
                fin_buf[s, :, main:] = theirs[:, mid:]

            @pl.when(me.role == 1)
            def _():
                fin_buf[s, :, :split] = theirs[:, :split]
                fin_buf[s, :, split:main] = theirs[:, split:] + mine[:, :mid]
                fin_buf[s, :, main:] = mine[:, mid:]

            f_copy(k).start()

        return 0

    lax.fori_loop(0, count + 5, step, 0)
    for k in range(count - SLOTS, count):
        f_copy(k).wait()


def reduce_all(grads, split, collective_id):
    count, outers, _, _, rows, width = grads.shape
    dma = pltpu.SemaphoreType.DMA
    many = outers - 1
    main = width - split
    return pl.pallas_call(
        functools.partial(reduce_kernel, count, outers, split),
        out_shape=jax.ShapeDtypeStruct((count, rows, width), F32),
        in_specs=[pl.BlockSpec(memory_space=pl.ANY)],
        out_specs=pl.BlockSpec(memory_space=pl.ANY),
        scratch_shapes=[
            pltpu.VMEM((SLOTS, outers, 2, rows, width), BF16),
            pltpu.VMEM((SLOTS, outers, 2, rows, width), BF16),
            pltpu.VMEM((SLOTS, outers, 2, rows, split), BF16),
            pltpu.VMEM((SLOTS, outers, rows, main), BF16),
            pltpu.VMEM((SLOTS, many, rows, main), BF16),
            pltpu.VMEM((SLOTS, rows, main), BF16),
            pltpu.VMEM((SLOTS, outers, 2, rows, width), BF16),
            pltpu.VMEM((SLOTS, outers, rows, main), BF16),
            pltpu.VMEM((SLOTS, rows, main), BF16),
            pltpu.VMEM((SLOTS, rows, width), F32),
            dma((SLOTS,)),
            dma((SLOTS,)), dma((SLOTS,)),
            dma((SLOTS,)), dma((SLOTS,)),
            dma((SLOTS,)), dma((SLOTS,)),
            dma((SLOTS, many)), dma((SLOTS, many)),
            dma((SLOTS,)), dma((SLOTS,)),
            dma((SLOTS,)),
        ],
        compiler_params=pltpu.CompilerParams(
            collective_id=collective_id, has_side_effects=True, vmem_limit_bytes=40 * 2**20
        ),
        name="reduce_gradients",
    )(grads)


def frame_tags(lengths, offsets, total_rows):
    places = jnp.arange(total_rows, dtype=jnp.int32)
    segs = lengths.shape[0]
    upto = jnp.arange(segs)[:, None] >= jnp.arange(segs)[None, :]
    finish = jnp.sum(jnp.where(upto, lengths[None, :], 0), axis=1)
    segment = jnp.sum((places[:, None] >= finish[None, :]).astype(jnp.int32), axis=1)
    member = segment[:, None] == jnp.arange(segs, dtype=jnp.int32)[None, :]
    shifted = offsets - (finish - lengths)
    position = places + jnp.sum(jnp.where(member, shifted[None, :], 0), axis=1)
    return (segment, position, member)


def dot(a, b):
    return jnp.dot(a, b, preferred_element_type=F32)


def dot_t(a, b):
    return lax.dot_general(a, b, (((1,), (1,)), ((), ())), preferred_element_type=F32)


def t_dot(a, b):
    return lax.dot_general(a, b, (((0,), (0,)), ((), ())), preferred_element_type=F32)


def normalize(hidden):
    average = jnp.mean(hidden, axis=-1, keepdims=True)
    centred = hidden - average
    spread = jnp.mean(centred * centred, axis=-1, keepdims=True)
    inverse = lax.rsqrt(spread + 1e-05)
    return centred * inverse, inverse


def norm_backward(grad, scale, unit, inverse):
    inner = grad * scale
    return inverse * (
        inner - jnp.mean(inner, axis=-1, keepdims=True) - unit * jnp.mean(inner * unit, axis=-1, keepdims=True)
    )


def attend(queries, keys, values, allowed):
    scores = jnp.einsum("gqhd,gkhd->ghqk", queries, keys, preferred_element_type=F32) * HD**-0.5
    scores = jnp.where(allowed[:, None], scores, -1e30)
    top = jnp.max(scores, axis=-1, keepdims=True)
    exponent = jnp.exp(scores - top)
    totals = jnp.sum(exponent, axis=-1, keepdims=True)
    soft = exponent / totals
    mixture = jnp.einsum("ghqk,gkhd->gqhd", soft.astype(BF16), values, preferred_element_type=F32)
    return mixture.astype(BF16), top + jnp.log(totals)


def attend_back(grad, queries, keys, values, allowed, lse):
    scores = jnp.einsum("gqhd,gkhd->ghqk", queries, keys, preferred_element_type=F32) * HD**-0.5
    soft = jnp.exp(jnp.where(allowed[:, None], scores, -1e30) - lse)
    grad_values = jnp.einsum("ghqk,gqhd->gkhd", soft.astype(BF16), grad, preferred_element_type=F32)
    grad_soft = jnp.einsum("gqhd,gkhd->ghqk", grad, values, preferred_element_type=F32)
    inner = jnp.sum(soft * grad_soft, axis=-1, keepdims=True)
    grad_scores = (soft * (grad_soft - inner)).astype(BF16)
    grad_queries = jnp.einsum("ghqk,gkhd->gqhd", grad_scores, keys, preferred_element_type=F32) * HD**-0.5
    grad_keys = jnp.einsum("ghqk,gqhd->gkhd", grad_scores, queries, preferred_element_type=F32) * HD**-0.5
    return grad_queries, grad_keys, grad_values


def gelu_parts(upper):
    cumulative = 0.5 * (1.0 + lax.erf(upper * 0.7071067811865476))
    density = jnp.exp(-0.5 * upper * upper) * 0.3989422804014327
    return upper * cumulative, cumulative + upper * density


def layer_forward(hidden, weights, tables, allowed, micro):
    count = hidden.shape[0]
    rows = count // micro
    pieces = (weights.shape[0] - 4) // 2
    scale_a, shift_a, scale_f, shift_f = tables
    unit_a, inverse_a = normalize(hidden)
    attn_in = (scale_a * unit_a + shift_a).astype(BF16)
    queries, keys, values = (
        dot(attn_in, weights[i]).astype(BF16).reshape(micro, rows, HEADS, HD) for i in range(3)
    )
    far_keys, far_values = lax.ppermute((keys, values), "role", [(0, 1)])
    keys = jnp.concatenate([far_keys, keys], axis=1)
    values = jnp.concatenate([far_values, values], axis=1)
    mixture, lse = attend(queries, keys, values, allowed)
    mixture = mixture.reshape(count, -1)
    middle = hidden + dot(mixture, weights[3])
    unit_f, inverse_f = normalize(middle)
    ffn_in = (scale_f * unit_f + shift_f).astype(BF16)
    result = middle
    lifted, slopes = [], []
    for j in range(pieces):
        up, slope = gelu_parts(dot(ffn_in, weights[4 + j]))
        lifted.append(up.astype(BF16))
        slopes.append(slope.astype(BF16))
        result = result + dot(lifted[j], weights[4 + pieces + j])
    kept = (unit_a, inverse_a, attn_in, queries, keys, values, lse, mixture, unit_f, inverse_f, ffn_in, lifted, slopes)
    return result, kept


def layer_backward(grad, weights, tables, allowed, kept, table_sums):
    unit_a, inverse_a, attn_in, queries, keys, values, lse, mixture, unit_f, inverse_f, ffn_in, lifted, slopes = kept
    scale_a, _, scale_f, _ = tables
    pieces = (weights.shape[0] - 4) // 2
    micro, rows = queries.shape[:2]
    count = micro * rows
    low = grad.astype(BF16)
    shrink_grads, expand_grads = [], []
    grad_ffn = 0.0
    for j in range(pieces):
        shrink_grads.append(t_dot(lifted[j], low).astype(BF16))
        grad_upper = (dot_t(low, weights[4 + pieces + j]) * slopes[j].astype(F32)).astype(BF16)
        expand_grads.append(t_dot(ffn_in, grad_upper).astype(BF16))
        grad_ffn = grad_ffn + dot_t(grad_upper, weights[4 + j])
    table_f = (table_sums(grad_ffn * unit_f), table_sums(grad_ffn))
    grad_middle = grad + norm_backward(grad_ffn, scale_f, unit_f, inverse_f)
    middle_low = grad_middle.astype(BF16)
    outer_grad = t_dot(mixture, middle_low).astype(BF16)
    grad_mixture = dot_t(middle_low, weights[3]).astype(BF16).reshape(micro, rows, HEADS, HD)
    grad_queries, grad_keys, grad_values = attend_back(grad_mixture, queries, keys, values, allowed, lse)
    back_keys, back_values = lax.ppermute(
        (grad_keys[:, :rows].astype(BF16), grad_values[:, :rows].astype(BF16)), "role", [(1, 0)]
    )
    grad_keys = grad_keys[:, rows:] + back_keys.astype(F32)
    grad_values = grad_values[:, rows:] + back_values.astype(F32)
    inner_grads = []
    grad_attn = 0.0
    for i, part in enumerate((grad_queries, grad_keys, grad_values)):
        part = part.astype(BF16).reshape(count, -1)
        inner_grads.append(t_dot(attn_in, part).astype(BF16))
        grad_attn = grad_attn + dot_t(part, weights[i])
    table_a = (table_sums(grad_attn * unit_a), table_sums(grad_attn))
    grad_hidden = grad_middle + norm_backward(grad_attn, scale_a, unit_a, inverse_a)
    tables_grad = (table_a[0], table_a[1], table_f[0], table_f[1])
    return grad_hidden, jnp.stack(inner_grads + [outer_grad] + expand_grads + shrink_grads), tables_grad


def body(
    frames, cotangent, inner_weight, outer_weight, expand_weight, shrink_weight, causal_gain, causal_shift,
    section_scale, section_shift, prompt_lengths, target_lengths, sections,
):
    is_target = lax.axis_index("role") == 1
    _, micro, rows, width = frames.shape
    shard = inner_weight.shape[1]
    devices = width // shard
    outers = devices // 4
    pieces = expand_weight.shape[2] // width
    layers = inner_weight.shape[0]
    count = micro * rows
    segs = section_scale.shape[0]

    parts = jnp.concatenate(
        [
            inner_weight.reshape(layers, shard, 3, width).transpose(0, 2, 1, 3),
            outer_weight[:, None],
            expand_weight.reshape(layers, shard, devices, pieces, shard).transpose(0, 3, 1, 2, 4).reshape(layers, pieces, shard, width),
            shrink_weight.reshape(layers, pieces, shard, width),
        ],
        axis=1,
    )
    per_layer = parts.shape[1]
    full = gather_all(parts.reshape(layers * per_layer, shard, width), outers, 3 * width // 8, 0)
    full = full.reshape(layers, per_layer, width, width)

    small = jnp.concatenate(
        [causal_gain, causal_shift, section_scale.reshape(2 * segs, -1), section_shift.reshape(2 * segs, -1)], axis=0
    )
    small = lax.all_gather(small, "dp", axis=1, tiled=True).astype(F32)
    scales = small[4 : 4 + 2 * segs].reshape(segs, 2, width)
    shifts = small[4 + 2 * segs :].reshape(segs, 2, width)

    allowed_sets = [[], []]
    section_frames = []
    for m in range(micro):
        prompt_row, target_row, section_row = prompt_lengths[m, 0], target_lengths[m, 0], sections[m, 0]
        prompt_segment, prompt_position, prompt_member = frame_tags(prompt_row, jnp.zeros_like(prompt_row), rows)
        target_segment, target_position, target_member = frame_tags(target_row, prompt_row, rows)
        own_segment = jnp.where(is_target, target_segment, prompt_segment)
        own_position = jnp.where(is_target, target_position, prompt_position)
        own_member = jnp.where(is_target, target_member, prompt_member)
        same_far = (own_segment[:, None] == prompt_segment[None, :]) & is_target
        same_own = own_segment[:, None] == own_segment[None, :]
        causal_own = same_own & (own_position[None, :] <= own_position[:, None])
        allowed_sets[0].append(jnp.concatenate([same_far, causal_own], axis=1))
        allowed_sets[1].append(jnp.concatenate([same_far, same_own], axis=1))
        section_frames.append(jnp.sum(jnp.where(own_member, section_row[None, :], 0), axis=1))
    allowed_sets = [jnp.stack(a) for a in allowed_sets]
    section_frame = jnp.concatenate(section_frames)
    picker = section_frame[:, None] == jnp.arange(segs, dtype=jnp.int32)[None, :]

    def rows_of(table):
        return jnp.sum(jnp.where(picker[:, :, None], table[None], 0.0), axis=1)

    def all_sum(values):
        return jnp.sum(values, axis=0, keepdims=True)

    def section_sum(values):
        return jnp.dot(picker.T.astype(F32), values, precision=lax.Precision.HIGHEST)

    tables = [
        (small[0:1], small[2:3], small[1:2], small[3:4]),
        (rows_of(scales[:, 0]), rows_of(shifts[:, 0]), rows_of(scales[:, 1]), rows_of(shifts[:, 1])),
    ]
    hidden = frames[0].reshape(count, width).astype(F32)
    kept = [None, None]
    for layer in range(2):
        hidden, kept[layer] = layer_forward(hidden, full[layer], tables[layer], allowed_sets[layer], micro)
    mixed = hidden.astype(BF16).reshape(1, micro, rows, width)
    grad = cotangent[0].reshape(count, width).astype(F32)
    weight_grads = [None, None]
    table_grads = [None, None]
    sums = [all_sum, section_sum]
    for layer in (1, 0):
        grad, weight_grads[layer], table_grads[layer] = layer_backward(
            grad, full[layer], tables[layer], allowed_sets[layer], kept[layer], sums[layer]
        )
    frames_grad = grad.astype(BF16).reshape(1, micro, rows, width)

    small_grads = jnp.concatenate(
        [
            table_grads[0][0], table_grads[0][2], table_grads[0][1], table_grads[0][3],
            jnp.stack([table_grads[1][0], table_grads[1][2]], axis=1).reshape(2 * segs, width),
            jnp.stack([table_grads[1][1], table_grads[1][3]], axis=1).reshape(2 * segs, width),
        ],
        axis=0,
    )
    small_grads = lax.psum(lax.psum_scatter(small_grads, "dp", scatter_dimension=1, tiled=True), "role")

    stacked = jnp.concatenate(weight_grads, axis=0).reshape(layers * per_layer, outers, 2, 2, shard, width)
    owned = reduce_all(stacked, width // 4, 1).reshape(layers, per_layer, shard, width)
    inner_grad = owned[:, :3].transpose(0, 2, 1, 3).reshape(layers, shard, 3 * width)
    outer_grad = owned[:, 3]
    expand_grad = (
        owned[:, 4 : 4 + pieces].reshape(layers, pieces, shard, devices, shard).transpose(0, 2, 3, 1, 4).reshape(layers, shard, -1)
    )
    shrink_grad = owned[:, 4 + pieces :].reshape(layers, pieces * shard, width)
    return (
        mixed, frames_grad, inner_grad, outer_grad, expand_grad, shrink_grad,
        small_grads[0:2], small_grads[2:4],
        small_grads[4 : 4 + 2 * segs].reshape(segs, 2, shard),
        small_grads[4 + 2 * segs :].reshape(segs, 2, shard),
    )


def solution(mesh):
    rows = P("role", None, "dp", None)
    second = P(None, "dp", None)
    placed = (rows, rows, second, second, second, second, P(None, "dp"), P(None, "dp"), P(None, None, "dp"), P(None, None, "dp"), second, second, second)
    given = (rows, rows, second, second, second, second, P(None, "dp"), P(None, "dp"), P(None, None, "dp"), P(None, None, "dp"))
    return jax.shard_map(body, mesh=mesh, in_specs=placed, out_specs=given, check_vma=False)
```

time: 2140 us -> 1150 us (0.54)
  waiting for transfers between devices: 1440 us -> 119 us
  Pallas kernels: 0 us -> 427 us
  matrix products: 410 us -> 238 us
  local copies, waits for them, and re-layouts: 68.6 us -> 231 us
  blocking collectives: 86.9 us -> 31.5 us
    reduce_scatter x8 -> x0, waiting for transfers between devices: 866 us -> none  [the longest x2 359 us: scatter_each(): lax.psum_scatter(grads[2], 'dp', scatter_dimension=0, tiled=True)]
    pallas_call x0 -> x2, Pallas kernels: none -> 427 us  [the longest x1 229 us: reduce_all(): pl.pallas_call(functools.partial(reduce_kernel, count, outers, split), ou...]
    all_gather x8 -> x0, waiting for transfers between devices: 240 us -> none  [the longest x2 119 us: fetch_forward(): lax.all_gather(shrink, 'dp', axis=0, tiled=True)]
    dot_general x96 -> x88, matrix products: 410 us -> 238 us  [the longest x24 58.4 us: t_dot(): lax.dot_general(a, b, (((0,), (0,)), ((), ())), preferred_element_type=F32)]
    unnamed x25 -> x2, waiting for transfers between devices: 212 us -> 52.8 us
    reshape x0 -> x31, local copies, waits for them, and re-layouts: none -> 81.7 us  [the longest x12 40.4 us: layer_forward(): dot(attn_in, weights[i]).astype(BF16).reshape(micro, rows, HEADS, HD)]
    psum x1 -> x0, waiting for transfers between devices: 81.1 us -> none  [body(): lax.psum(second_set[0].astype(jnp.bfloat16), 'role').astype(jnp.float32)]
    all_gather x4 -> x1, blocking collectives: 81.9 us -> 23.4 us  [body(): small = lax.all_gather(small, 'dp', axis=1, tiled=True).astype(F32)]
  transfers between devices with their start and end apart: 37 -> 9, of which waited for: 20 -> 5; matrix products, arithmetic and copies ran while one was open for 22% -> 14% of each run, Pallas kernels for 0% -> 0%
where the time goes in v1:
time: 1150 us; the launch traced here: 1140 us
  Pallas kernels  427 us (37%)
  matrix products  238 us (21%)
  local copies, waits for them, and re-layouts  231 us (20%)
  waiting for transfers between devices  119 us (10%)
  other arithmetic  61.4 us (5%)
  blocking collectives  31.5 us (3%)
  starting transfers between devices  17.5 us (2%)
  between operations  16.2 us (1%)
    pallas_call x1, Pallas kernels, reduce_all(): pl.pallas_call(functools.partial(reduce_kernel, count, outers, split), ou...  229 us
    pallas_call x1, Pallas kernels, gather_all(): pl.pallas_call(functools.partial(gather_kernel, count, outers, split), ou...  198 us
    unnamed x356, local copies, waits for them, and re-layouts  92.5 us
    dot_general x24, matrix products, t_dot(): lax.dot_general(a, b, (((0,), (0,)), ((), ())), preferred_element_type=F32)  58.4 us
    ppermute x4, waiting for transfers between devices, layer_backward(): lax.ppermute((grad_keys[:, :rows].astype(BF16), grad_values[:, :rows].ast...  53.8 us
    dot_general x24, matrix products, dot(): return jnp.dot(a, b, preferred_element_type=F32)  53.6 us
    unnamed x2, waiting for transfers between devices  52.8 us
    dot_general x24, matrix products, dot_t(): lax.dot_general(a, b, (((1,), (1,)), ((), ())), preferred_element_type=F32)  45.8 us
  transfers between devices with their start and end apart: 9, of which 5 were waited for; matrix products, arithmetic and copies ran while one was open for 14% of the time, Pallas kernels for 0%

profile of v1, /device:TPU:0, one launch (start us, length us, event | category | flops | bytes accessed | tf_op | source)
XLA Modules:
  0.0 1141.6 jit_solution(12784097014198249294)
XLA Ops:
  9.3 23.4 %all-gather = bf16[16,64,32]{1,2,0:T(8,128)(2,1)S(1)} all-gather(bf16[1,64,32]{1,2,0:T(8,128)(2,1)S(1)} %maximum_bitcast_fusion), channel_id=1, replica_groups=mesh['role'=2,'dp'=16] {'dp'}, dimensions={0}, use_global_device_ids=true | all-gather | bytes 69632 | tf_op jit(solution)/shard_map/all_gather | solution.py:501
  32.9 5.0 reshape.664
  47.2 197.9 %gather_weights.1 = bf16[24,4,2,2,64,1024]{5,4,3,2,1,0:T(8,128)(2,1)} custom-call(bf16[24,64,1024]{2,1,0:T(8,128)(2,1)} %bitcast.396), custom_call_target="tpu_custom_call" | custom-call | tf_op jit(solution)/shard_map/gather_weights/pallas_call | solution.py:154
  245.7 7.4 fusion.132
  262.4 5.0 collective-permute-start.1
  267.4 4.1 convolution_convert_fusion.31
  280.1 25.9 %fusion.131 = (bf16[1,4,2,2,64,1024]{5,4,3,2,1,0:T(8,128)(2,1)}, bf16[1,4,2,2,64,1024]{5,4,3,2,1,0:T(8,128)(2,1)}, bf16[1,4,2,2,64,1024]{5,4,3,2,1,0:T(8,128)(2,...) fusion(bf16[24,4,2,2,64,1024]{5,4,3,2,1,0:T(8,128)(2,1)} %gathe, ...), kind=kLoop, calls=%fused_computation.352 | loop fusion | bytes 79691776 | tf_op jit(solution)/shard_map/slice | solution.py:426
  307.2 4.1 convolution_convert_fusion.30
  320.8 10.2 select_reduce_fusion.3
  331.0 4.6 fusion.140
  341.3 7.1 fusion.88
  397.1 4.5 convolution_convert_fusion.28
  412.1 5.1 fusion.143
  421.3 12.4 %collective-permute-done.2 = bf16[2,256,16,64]{1,3,2,0:T(8,128)(2,1)} collective-permute-done((bf16[2,256,16,64]{1,3,2,0:T(8,128)(2,1)}, bf16[2,256,16,64]{1,3,2,0:T(8,128)(2,1)}, u32[]{:S(2)}, u32[]{:S(2)}) %collective-permute-start.2) | collective-permute-done | bytes 1048608 | tf_op jit(solution)/shard_map/ppermute | solution.py:415
  433.7 6.6 fusion.89
  483.8 8.7 fusion.12
  492.5 12.5 %multiply_reduce_fusion.1 = (f32[2,16,256]{2,1,0:T(8,128)S(1)}, f32[2,16,256,512]{3,2,1,0:T(8,128)}) fusion(f32[2,16,256,512]{3,2,1,0:T(8,128)} %copy-done.2, f32[2,16,256]{2,1,0:T(8,128)S(1)} %log_add_fusion.1, bf16[2,256,16,64]{1,3,2,0:T(8,128)(2,1)S(1)} %copy.214, bf16[2,256,16,64]{1,3,2,0:T(8,128)(2,1)S(1)} %copy-done.40, ...), kind=kOutput, calls=%fused_computation.4 | convolution fusion | flops 553639936 | bytes 36765696 | tf_op jit(solution)/shard_map/gqhd,gkhd->ghqk/dot_general | solution.py:391
  505.0 12.2 %multiply_convert_fusion.1 = bf16[2,16,256,512]{3,2,1,0:T(8,128)(2,1)S(1)} fusion(f32[2,16,256,512]{3,2,1,0:T(8,128)} %get-tuple-element.126, f32[2,16,256,512]{3,2,1,0:T(8,128)} %copy-done.2, f32[2,16,256]{2,1,0:T(8,128)S(1)} %get-tuple-element.125, f32[2,16,256]{2,1,0:T(8,128)S(1)} %log_add_fusion.1), kind=kLoop, calls=%fused_computation.3 | loop fusion | flops 16777216 | bytes 42008576 | tf_op jit(solution)/shard_map/convert_element_type | solution.py:393
  518.8 4.2 fusion.90
  566.2 19.6 %collective-permute-done.5 = bf16[2,256,16,64]{1,3,2,0:T(8,128)(2,1)S(1)} collective-permute-done((bf16[2,256,16,64]{1,3,2,0:T(8,128)(2,1)S(1)}, bf16[2,256,16,64]{1,3,2,0:T(8,128)(2,1)S(1)}, u32[]{:S(2)}, u32[]{:S(2)}) %collective-permute-start.5) | collective-permute-done | bytes 1048608 | tf_op jit(solution)/shard_map/ppermute | solution.py:454
  587.5 19.4 %collective-permute-done.4 = bf16[2,256,16,64]{1,3,2,0:T(8,128)(2,1)S(1)} collective-permute-done((bf16[2,256,16,64]{1,3,2,0:T(8,128)(2,1)S(1)}, bf16[2,256,16,64]{1,3,2,0:T(8,128)(2,1)S(1)}, u32[]{:S(2)}, u32[]{:S(2)}) %collective-permute-start.4) | collective-permute-done | bytes 1048608 | tf_op jit(solution)/shard_map/ppermute | solution.py:454
  670.5 7.3 fusion.15
  682.3 12.5 %multiply_reduce_fusion = (f32[2,16,256]{2,1,0:T(8,128)S(1)}, f32[2,16,256,512]{3,2,1,0:T(8,128)}) fusion(f32[2,16,256,512]{3,2,1,0:T(8,128)} %copy-done.1, f32[2,16,256]{2,1,0:T(8,128)S(1)} %copy-done.116, bf16[2,256,16,64]{1,3,2,0:T(8,128)(2,1)S(1)} %copy.221, bf16[2,256,16,64]{1,3,2,0:T(8,128)(2,1)S(1)} %copy-done.38, ...), kind=kOutput, calls=%fused_computation.1 | convolution fusion | flops 553639936 | bytes 36765696 | tf_op jit(solution)/shard_map/gqhd,gkhd->ghqk/dot_general | solution.py:391
  694.8 11.8 %multiply_convert_fusion = bf16[2,16,256,512]{3,2,1,0:T(8,128)(2,1)S(1)} fusion(f32[2,16,256,512]{3,2,1,0:T(8,128)} %get-tuple-element.130, f32[2,16,256,512]{3,2,1,0:T(8,128)} %copy-done.1, f32[2,16,256]{2,1,0:T(8,128)S(1)} %get-tuple-element.129, f32[2,16,256]{2,1,0:T(8,128)S(1)} %copy-done.116), kind=kLoop, calls=%fused_computation | loop fusion | flops 16777216 | bytes 42008576 | tf_op jit(solution)/shard_map/convert_element_type | solution.py:393
  708.3 4.6 fusion.91
  727.6 14.8 %collective-permute-done.6 = bf16[2,256,16,64]{1,3,2,0:T(8,128)(2,1)} collective-permute-done((bf16[2,256,16,64]{1,3,2,0:T(8,128)(2,1)}, bf16[2,256,16,64]{1,3,2,0:T(8,128)(2,1)}, u32[]{:S(2)}, u32[]{:S(2)}) %collective-permute-start.6) | collective-permute-done | bytes 1048608 | tf_op jit(solution)/shard_map/ppermute | solution.py:454
  805.8 229.1 %reduce_gradients.1 = f32[24,64,1024]{2,1,0:T(8,128)S(1)} custom-call(bf16[24,4,2,2,64,1024]{5,4,3,2,1,0:T(8,128)(2,1)} %constant_dynamic-update-slice_fusion.grad_ref), custom_call_target="tpu_custom_call" | custom-call | tf_op jit(solution)/shard_map/reduce_gradients/pallas_call | solution.py:306
  1047.5 4.5 reshape.690
  1052.0 6.9 copy.276
  1058.9 5.6 reshape.691
  1071.1 52.8 %reduce-scatter.4.cloned.1.call-done = f32[64,32]{1,0:T(8,128)} async-done(((f32[1024,32]{1,0:T(8,128)}), f32[64,32]{1,0:T(8,128)}) %reduce-scatter.4.cloned.1.call-update) | async-done | bytes 8208
  1124.7 8.1 psum.7
  (565 shorter events, 367.4 us)
Async XLA Ops:
  7.2 1116.7 %reduce-scatter.4.cloned.1.call-start = ((), (), s32[]{:S(2)}) async-start(), calls=%async_computation.1 | async-start | bytes 557056
  47.2 197.9 %copy-start.8 = (bf16[1,2,256,1024]{3,2,1,0:T(8,128)(2,1)S(1)}, bf16[1,2,256,1024]{3,2,1,0:T(8,128)(2,1)}, u32[]{:S(2)}) copy-start(bf16[1,2,256,1024]{3,2,1,0:T(8,128)(2,1)} %param.13) | copy-start | bytes 3145732
  245.1 8.0 copy-start.129
  245.1 107.9 %copy-start.123 = (f32[1,1024]{1,0:T(1,128)}, f32[1,1024]{1,0:T(1,128)S(1)}, u32[]{:S(2)}) copy-start(f32[1,1024]{1,0:T(1,128)S(1)} %get-tuple-element.62) | copy-start | bytes 12292
  262.4 68.5 %collective-permute-start.1 = (bf16[2,256,16,64]{1,3,2,0:T(8,128)(2,1)}, bf16[2,256,16,64]{1,3,2,0:T(8,128)(2,1)}, u32[]{:S(2)}, u32[]{:S(2)}) collective-permute-start(bf16[2,256,16,64]{1,3,2,0:T(8,128)(2,1)} %copy.196), channel_id=1, source_target_pairs={{0,16},{1,17},{2,18},{3,19},{4,20},{5,21},{6,22},{7,23},{8,24},{9,... | collective-permute-start | bytes 3145736 | tf_op jit(solution)/shard_map/ppermute | solution.py:415
  277.1 62.5 %collective-permute-start = (bf16[2,256,16,64]{1,3,2,0:T(8,128)(2,1)}, bf16[2,256,16,64]{1,3,2,0:T(8,128)(2,1)}, u32[]{:S(2)}, u32[]{:S(2)}) collective-permute-start(bf16[2,256,16,64]{1,3,2,0:T(8,128)(2,1)} %copy.192), channel_id=1, source_target_pairs={{0,16},{1,17},{2,18},{3,19},{4,20},{5,21},{6,22},{7,23},{8,24},{9,... | collective-permute-start | bytes 3145736 | tf_op jit(solution)/shard_map/ppermute | solution.py:415
  280.1 26.0 %copy-start.139 = (s32[2,1,4]{2,1,0:T(1,128)S(1)}, s32[2,1,4]{2,1,0:T(1,128)}, u32[]{:S(2)}) copy-start(s32[2,1,4]{2,1,0:T(1,128)} %param.25) | copy-start | bytes 100
  306.0 47.8 %copy-start.18 = (bf16[1,4,2,2,64,1024]{5,4,3,2,1,0:T(8,128)(2,1)}, bf16[1,4,2,2,64,1024]{5,4,3,2,1,0:T(8,128)(2,1)S(1)}, u32[]{:S(2)}) copy-start(bf16[1,4,2,2,64,1024]{5,4,3,2,1,0:T(8,128)(2,1)S(1)} %get-tuple-element.49) | copy-start | bytes 6291460
  320.7 10.2 copy-start.34
  320.7 10.2 copy-start.43
  352.6 16.1 %copy-start.3 = (f32[512,1024]{1,0:T(8,128)}, f32[512,1024]{1,0:T(8,128)S(1)}, u32[]{:S(2)}) copy-start(f32[512,1024]{1,0:T(8,128)S(1)} %get-tuple-element.105) | copy-start | bytes 6291460
  353.7 7.4 copy-start.107
  355.1 13.6 %copy-start.94 = (f32[512,1024]{1,0:T(8,128)}, f32[512,1024]{1,0:T(8,128)S(1)}, u32[]{:S(2)}) copy-start(f32[512,1024]{1,0:T(8,128)S(1)} %fusion.148) | copy-start | bytes 6291460
  372.6 13.8 %copy-start.99 = (bf16[512,1024]{1,0:T(8,128)(2,1)}, bf16[512,1024]{1,0:T(8,128)(2,1)S(1)}, u32[]{:S(2)}) copy-start(bf16[512,1024]{1,0:T(8,128)(2,1)S(1)} %add_convert_fusion.2) | copy-start | bytes 3145732
  383.5 28.7 %collective-permute-start.3 = (bf16[2,256,16,64]{1,3,2,0:T(8,128)(2,1)}, bf16[2,256,16,64]{1,3,2,0:T(8,128)(2,1)}, u32[]{:S(2)}, u32[]{:S(2)}) collective-permute-start(bf16[2,256,16,64]{1,3,2,0:T(8,128)(2,1)} %copy.205), channel_id=1, source_target_pairs={{0,16},{1,17},{2,18},{3,19},{4,20},{5,21},{6,22},{7,23},{8,24},{9,... | collective-permute-start | bytes 3145736 | tf_op jit(solution)/shard_map/ppermute | solution.py:415
  397.1 15.1 %copy-start.36 = (bf16[2,256,16,64]{1,3,2,0:T(8,128)(2,1)}, bf16[2,256,16,64]{1,3,2,0:T(8,128)(2,1)S(1)}, u32[]{:S(2)}) copy-start(bf16[2,256,16,64]{1,3,2,0:T(8,128)(2,1)S(1)} %copy.207) | copy-start | bytes 3145732
  405.6 6.5 copy-start.118
  409.2 24.5 %collective-permute-start.2 = (bf16[2,256,16,64]{1,3,2,0:T(8,128)(2,1)}, bf16[2,256,16,64]{1,3,2,0:T(8,128)(2,1)}, u32[]{:S(2)}, u32[]{:S(2)}) collective-permute-start(bf16[2,256,16,64]{1,3,2,0:T(8,128)(2,1)} %copy.201), channel_id=1, source_target_pairs={{0,16},{1,17},{2,18},{3,19},{4,20},{5,21},{6,22},{7,23},{8,24},{9,... | collective-permute-start | bytes 3145736 | tf_op jit(solution)/shard_map/ppermute | solution.py:415
  417.2 16.5 %copy-start.2 = (f32[2,16,256,512]{3,2,1,0:T(8,128)}, f32[2,16,256,512]{3,2,1,0:T(8,128)S(1)}, u32[]{:S(2)}) copy-start(f32[2,16,256,512]{3,2,1,0:T(8,128)S(1)} %get-tuple-element.115) | copy-start | bytes 50331652
  417.2 16.5 %copy-start.39 = (bf16[2,256,16,64]{1,3,2,0:T(8,128)(2,1)S(1)}, bf16[2,256,16,64]{1,3,2,0:T(8,128)(2,1)}, u32[]{:S(2)}) copy-start(bf16[2,256,16,64]{1,3,2,0:T(8,128)(2,1)} %copy.201) | copy-start | bytes 3145732
  444.5 30.7 %copy-start.5 = (f32[512,1024]{1,0:T(8,128)}, f32[512,1024]{1,0:T(8,128)S(1)}, u32[]{:S(2)}) copy-start(f32[512,1024]{1,0:T(8,128)S(1)} %get-tuple-element.117) | copy-start | bytes 6291460
  447.5 8.6 copy-start.101
  457.4 11.9 %copy-start.97 = (f32[512,1024]{1,0:T(8,128)}, f32[512,1024]{1,0:T(8,128)S(1)}, u32[]{:S(2)}) copy-start(f32[512,1024]{1,0:T(8,128)S(1)} %fusion.152) | copy-start | bytes 6291460
  483.8 8.7 copy-start.40
  505.0 12.2 %copy-start.37 = (bf16[2,256,16,64]{1,3,2,0:T(8,128)(2,1)S(1)}, bf16[2,256,16,64]{1,3,2,0:T(8,128)(2,1)}, u32[]{:S(2)}) copy-start(bf16[2,256,16,64]{1,3,2,0:T(8,128)(2,1)} %copy-done.36) | copy-start | bytes 3145732
  557.8 28.0 %collective-permute-start.5 = (bf16[2,256,16,64]{1,3,2,0:T(8,128)(2,1)S(1)}, bf16[2,256,16,64]{1,3,2,0:T(8,128)(2,1)S(1)}, u32[]{:S(2)}, u32[]{:S(2)}) collective-permute-start(bf16[2,256,16,64]{1,3,2,0:T(8,128)(2,1)S(1)} %slice.369), channel_id=1, source_target_pairs={{16,0},{17,1},{18,2},{19,3},{20,4},{21,5},{22,6},{23,7},{24,8},{25... | collective-permute-start | bytes 3145736 | tf_op jit(solution)/shard_map/ppermute | solution.py:454
  559.2 47.6 %collective-permute-start.4 = (bf16[2,256,16,64]{1,3,2,0:T(8,128)(2,1)S(1)}, bf16[2,256,16,64]{1,3,2,0:T(8,128)(2,1)S(1)}, u32[]{:S(2)}, u32[]{:S(2)}) collective-permute-start(bf16[2,256,16,64]{1,3,2,0:T(8,128)(2,1)S(1)} %slice.370), channel_id=1, source_target_pairs={{16,0},{17,1},{18,2},{19,3},{20,4},{21,5},{22,6},{23,7},{24,8},{25... | collective-permute-start | bytes 3145736 | tf_op jit(solution)/shard_map/ppermute | solution.py:454
  615.3 42.0 %copy-start.114 = (bf16[512,1024]{1,0:T(8,128)(2,1)}, bf16[512,1024]{1,0:T(8,128)(2,1)S(1)}, u32[]{:S(2)}) copy-start(bf16[512,1024]{1,0:T(8,128)(2,1)S(1)} %get-tuple-element.32) | copy-start | bytes 3145732
  681.0 67.9 %collective-permute-start.7 = (bf16[2,256,16,64]{1,3,2,0:T(8,128)(2,1)}, bf16[2,256,16,64]{1,3,2,0:T(8,128)(2,1)}, u32[]{:S(2)}, u32[]{:S(2)}) collective-permute-start(bf16[2,256,16,64]{1,3,2,0:T(8,128)(2,1)} %slice.367), channel_id=1, source_target_pairs={{16,0},{17,1},{18,2},{19,3},{20,4},{21,5},{22,6},{23,7},{24,8},{25... | collective-permute-start | bytes 3145736 | tf_op jit(solution)/shard_map/ppermute | solution.py:454
  694.8 11.8 %copy-start.35 = (bf16[2,256,16,64]{1,3,2,0:T(8,128)(2,1)S(1)}, bf16[2,256,16,64]{1,3,2,0:T(8,128)(2,1)}, u32[]{:S(2)}) copy-start(bf16[2,256,16,64]{1,3,2,0:T(8,128)(2,1)} %copy.198) | copy-start | bytes 3145732
  715.4 27.0 %collective-permute-start.6 = (bf16[2,256,16,64]{1,3,2,0:T(8,128)(2,1)}, bf16[2,256,16,64]{1,3,2,0:T(8,128)(2,1)}, u32[]{:S(2)}, u32[]{:S(2)}) collective-permute-start(bf16[2,256,16,64]{1,3,2,0:T(8,128)(2,1)} %slice.368), channel_id=1, source_target_pairs={{16,0},{17,1},{18,2},{19,3},{20,4},{21,5},{22,6},{23,7},{24,8},{25... | collective-permute-start | bytes 3145736 | tf_op jit(solution)/shard_map/ppermute | solution.py:454
  1058.9 7.0 copy-start.24
  (136 other events, 339.6 us)
Sparse Core Ops, SparseCore 0:
  1066.0 57.7 reduce-scatter.3

commit v2 on v0

v2 whole, which is shorter than its diff:
```python
import functools

import jax
import jax.numpy as jnp
from jax import lax
from jax.experimental import pallas as pl
from jax.experimental.pallas import tpu as pltpu
from jax.sharding import PartitionSpec as P

HEADS = 16
HD = 64
MESH = pl.DeviceIdType.MESH
SLOTS = 4
F32 = jnp.float32
BF16 = jnp.bfloat16


class Place:
    def __init__(self, outer_count):
        self.outers = outer_count
        self.role = lax.axis_index("role")
        dp = lax.axis_index("dp")
        self.core = dp % 2
        self.pair = (dp // 2) % 2
        self.outer = dp // 4
        self.dp = dp

    def at(self, role, outer, pair, core):
        return (role, (outer * 2 + pair) * 2 + core)

    def sibling(self):
        return self.at(self.role, self.outer, self.pair, 1 - self.core)

    def across(self):
        return self.at(self.role, self.outer, 1 - self.pair, self.core)

    def other_role(self):
        return self.at(1 - self.role, self.outer, self.pair, self.core)

    def along(self, by):
        return self.at(self.role, (self.outer + by) % self.outers, self.pair, self.core)

    def around(self, by):
        return (self.role, (self.dp + by) % (4 * self.outers))

    def greet(self):
        barrier = pltpu.get_barrier_semaphore()
        pl.semaphore_signal(barrier, inc=1, device_id=self.other_role(), device_id_type=MESH)

        def greet_one(i, carry):
            pl.semaphore_signal(barrier, inc=1, device_id=self.around(i + 1), device_id_type=MESH)
            return carry

        lax.fori_loop(0, 4 * self.outers - 1, greet_one, 0)
        pl.semaphore_wait(barrier, 4 * self.outers)


def remote(src, dst, send, recv, peer):
    return pltpu.make_async_remote_copy(
        src_ref=src, dst_ref=dst, send_sem=send, recv_sem=recv, device_id=peer, device_id_type=MESH
    )


def frame_tags(lengths, offsets, total_rows):
    places = jnp.arange(total_rows, dtype=jnp.int32)
    segs = lengths.shape[0]
    upto = jnp.arange(segs)[:, None] >= jnp.arange(segs)[None, :]
    finish = jnp.sum(jnp.where(upto, lengths[None, :], 0), axis=1)
    segment = jnp.sum((places[:, None] >= finish[None, :]).astype(jnp.int32), axis=1)
    member = segment[:, None] == jnp.arange(segs, dtype=jnp.int32)[None, :]
    shifted = offsets - (finish - lengths)
    position = places + jnp.sum(jnp.where(member, shifted[None, :], 0), axis=1)
    return (segment, position, member)


def dot(a, b):
    return jnp.dot(a, b, preferred_element_type=F32)


def dot_t(a, b):
    return lax.dot_general(a, b, (((1,), (1,)), ((), ())), preferred_element_type=F32)


def t_dot(a, b):
    return lax.dot_general(a, b, (((0,), (0,)), ((), ())), preferred_element_type=F32)


def normalize(hidden):
    average = jnp.mean(hidden, axis=-1, keepdims=True)
    centred = hidden - average
    spread = jnp.mean(centred * centred, axis=-1, keepdims=True)
    inverse = lax.rsqrt(spread + 1e-05)
    return centred * inverse, inverse


def norm_backward(grad, scale, unit, inverse):
    inner = grad * scale
    return inverse * (
        inner - jnp.mean(inner, axis=-1, keepdims=True) - unit * jnp.mean(inner * unit, axis=-1, keepdims=True)
    )


def gelu_parts(upper):
    cumulative = 0.5 * (1.0 + lax.erf(upper * 0.7071067811865476))
    density = jnp.exp(-0.5 * upper * upper) * 0.3989422804014327
    return upper * cumulative, cumulative + upper * density


class Gather:
    lag = 4

    def __init__(self, me, part_ref, full_ref, split, sems):
        self.me, self.part, self.full, self.split = me, part_ref, full_ref, split
        self.own_sem, self.zs, self.zr, self.xs, self.xr, self.us, self.ur, self.vs, self.vr, self.cs, self.cr = sems
        self.half = part_ref.shape[-1] // 2
        self.main = self.half - split
        self.steps = 2 * part_ref.shape[0]

    @staticmethod
    def semaphores(many):
        dma = pltpu.SemaphoreType.DMA
        return [
            dma((SLOTS,)),
            dma((SLOTS, many)), dma((SLOTS, many)),
            dma((SLOTS,)), dma((SLOTS,)),
            dma((2 * SLOTS, many)), dma((2 * SLOTS, many)),
            dma((SLOTS,)), dma((SLOTS,)),
            dma((SLOTS,)), dma((SLOTS,)),
        ]

    def cols(self, h, offset, size):
        return pl.ds(pl.multiple_of((h % 2) * self.half + offset, 128), size)

    def main_cols(self, h):
        return self.cols(h, self.me.role * self.split, self.main)

    def give_cols(self, h):
        return self.cols(h, self.me.role * self.main, self.split)

    def take_cols(self, h):
        return self.cols(h, (1 - self.me.role) * self.main, self.split)

    def before(self, by):
        return (self.me.outer - by + self.me.outers) % self.me.outers

    def own(self, h):
        me, cols = self.me, self.cols(h, 0, self.half)
        return pltpu.make_async_copy(
            self.part.at[h // 2, :, cols], self.full.at[h // 2, me.outer, me.pair, me.core, :, cols], self.own_sem.at[h % SLOTS]
        )

    def z_copy(self, h, by):
        me, cols, s = self.me, self.main_cols(h), h % SLOTS
        return remote(
            self.part.at[h // 2, :, cols],
            self.full.at[h // 2, me.outer, me.pair, me.core, :, cols],
            self.zs.at[s, by - 1], self.zr.at[s, by - 1], me.along(by),
        )

    def z_wait(self, h, by):
        me, s = self.me, h % SLOTS
        dst = self.full.at[h // 2, self.before(by), me.pair, me.core, :, self.main_cols(h)]
        remote(dst, dst, self.zs.at[s, by - 1], self.zr.at[s, by - 1], me.along(by)).wait_recv()

    def x_copy(self, h, pair):
        me, s = self.me, h % SLOTS
        ref = self.full.at[h // 2, :, pair, me.core, :, self.main_cols(h)]
        return remote(ref, ref, self.xs.at[s], self.xr.at[s], me.across())

    def u_copy(self, h, by, cols):
        me, s = self.me, h % (2 * SLOTS)
        ref = self.full.at[h // 2, self.before(by), me.pair, me.core, :, cols]
        return remote(ref, ref, self.us.at[s, by - 1], self.ur.at[s, by - 1], me.other_role())

    def v_copy(self, h, cols):
        me, s = self.me, h % SLOTS
        ref = self.full.at[h // 2, :, 1 - me.pair, me.core, :, cols]
        return remote(ref, ref, self.vs.at[s], self.vr.at[s], me.other_role())

    def c_copy(self, h, core):
        s = h % SLOTS
        ref = self.full.at[h // 2, :, :, core, :, self.cols(h, 0, self.half)]
        return remote(ref, ref, self.cs.at[s], self.cr.at[s], self.me.sibling())

    def step(self, t):
        me, count = self.me, self.steps
        others = range(1, me.outers)

        @pl.when(t < count)
        def _():
            self.own(t).start()
            for by in others:
                self.z_copy(t, by).start()

        @pl.when((t >= 1) & (t < count + 1))
        def _():
            h = t - 1
            self.own(h).wait()
            for by in others:
                self.z_wait(h, by)
            self.x_copy(h, me.pair).start()
            for by in others:
                self.u_copy(h, by, self.give_cols(h)).start()

        @pl.when((t >= 2) & (t < count + 2))
        def _():
            h = t - 2
            self.x_copy(h, 1 - me.pair).wait_recv()
            self.v_copy(h, self.give_cols(h)).start()

        @pl.when((t >= 3) & (t < count + 3))
        def _():
            h = t - 3
            for by in others:
                self.u_copy(h, by, self.take_cols(h)).wait_recv()
            self.v_copy(h, self.take_cols(h)).wait_recv()
            self.c_copy(h, me.core).start()
            for by in others:
                self.z_copy(h, by).wait_send()
                self.u_copy(h, by, self.give_cols(h)).wait_send()
            self.x_copy(h, me.pair).wait_send()
            self.v_copy(h, self.give_cols(h)).wait_send()

        @pl.when((t >= 4) & (t < count + 4))
        def _():
            h = t - 4
            self.c_copy(h, 1 - me.core).wait_recv()
            self.c_copy(h, me.core).wait_send()


def loop(count, action):
    def one(i, carry):
        action(i)
        return carry

    lax.fori_loop(0, count, one, 0)


def tile(i, size):
    return pl.ds(pl.multiple_of(i * size, size), size)


WIDE = 256


def forward_kernel(
    layers, outers, split,
    part_ref, frames_ref, piece_ref, pick_ref, bias_ref,
    full_ref, saved_ref, hidden_ref, probs_ref, mixed_ref, table_ref,
    tab_in, h_buf, a_buf, qkv_buf, far_buf, mix_buf, f_buf, lift_buf, slope_buf, w_buf, p_buf,
    ts, tr, w_sem, save_sem, h_sem, p_sem, out_sem, ks, kr, *gather_sems,
):
    me = Place(outers)
    devices = 4 * outers
    rows_all, width = frames_ref.shape
    per_layer = part_ref.shape[0] // layers
    pieces = (per_layer - 4) // 2
    micro = bias_ref.shape[1]
    rows = rows_all // micro
    pairs = width // 128
    gather = Gather(me, part_ref, full_ref, split, gather_sems)
    me.greet()

    def piece_copy(by):
        return remote(piece_ref, tab_in.at[me.dp], ts.at[by - 1], tr.at[by - 1], me.around(by))

    def piece_wait(by):
        here = tab_in.at[(me.dp - by + devices) % devices]
        remote(here, here, ts.at[by - 1], tr.at[by - 1], me.around(by)).wait_recv()

    loop(devices - 1, lambda i: piece_copy(i + 1).start())
    tab_in[me.dp] = piece_ref[...]

    @pl.when(me.role == 0)
    def _():
        far_buf[...] = jnp.zeros_like(far_buf)

    loop(6, gather.step)
    loop(devices - 1, lambda i: piece_wait(i + 1))
    loop(devices - 1, lambda i: piece_copy(i + 1).wait_send())
    per = 128 * devices // width
    for group in range(width // 128):
        total = tab_in[group * per]
        for i in range(1, per):
            total = total + tab_in[group * per + i]
        table_ref[:, group * 128 : group * 128 + 128] = total

    def load_rows(i):
        r = tile(i, 64)
        h_buf[0, r, :] = frames_ref[r, :].astype(F32)

    loop(rows_all // 64, load_rows)

    def load(k):
        return pltpu.make_async_copy(full_ref.at[k], w_buf.at[k % 2], w_sem.at[k % 2])

    def matmul(in_ref, k, finish):
        load(k).wait()

        def columns(n):
            cols = tile(n, WIDE)
            w = w_buf[k % 2, :, :, :, :, cols].reshape(width, WIDE)
            finish(cols, dot(in_ref[...], w))

        loop(width // WIDE, columns)

    def norm(index, src, dst_ref, l):
        def some(i):
            r = tile(i, 64)
            unit, _ = normalize(h_buf[src, r, :])
            scale = dot(pick_ref[l * 4 + 2 * index, r, :], table_ref[...])
            shift = dot(pick_ref[l * 4 + 2 * index + 1, r, :], table_ref[...])
            dst_ref[r, :] = (scale * unit + shift).astype(BF16)

        loop(rows_all // 64, some)

    def layer(l):
        base = l * per_layer

        def save(ref, slot):
            return pltpu.make_async_copy(ref, saved_ref.at[l, slot], save_sem.at[slot])

        def save_hidden(which):
            return pltpu.make_async_copy(h_buf.at[which], hidden_ref.at[l, which], h_sem.at[which])

        load(base).start()
        save_hidden(0).start()
        norm(0, 0, a_buf, l)
        save(a_buf, 0).start()

        def project(i):
            def keep(cols, value):
                qkv_buf[i, :, cols] = value.astype(BF16)

            matmul(a_buf, base + i, keep)
            gather.step(2 * (base + i) + 6)
            gather.step(2 * (base + i) + 7)
            load(base + i + 1).start()
            save(qkv_buf.at[i], 1 + i).start()

        loop(3, project)

        def far_copy():
            return remote(qkv_buf.at[pl.ds(1, 2)], far_buf.at[l], ks.at[l], kr.at[l], me.other_role())

        @pl.when(me.role == 0)
        def _():
            far_copy().start()

        @pl.when(me.role == 1)
        def _():
            far_copy().wait_recv()

        save(far_buf.at[l, 0], 4).start()
        save(far_buf.at[l, 1], 5).start()

        def save_probs(it):
            return pltpu.make_async_copy(p_buf.at[it % 2], probs_ref.at[l, it], p_sem.at[it % 2])

        def attend(it):
            m, p = it // pairs, it % pairs
            r, cols = tile(m, rows), tile(p, 128)
            first = lax.broadcasted_iota(jnp.int32, (rows, 128), 1) < HD
            q = qkv_buf[0, r, cols].astype(F32) * HD**-0.5
            both = jnp.concatenate([jnp.where(first, q, 0.0).astype(BF16), jnp.where(first, 0.0, q).astype(BF16)], axis=0)
            keys = jnp.concatenate([far_buf[l, 0, r, cols], qkv_buf[1, r, cols]], axis=0)
            values = jnp.concatenate([far_buf[l, 1, r, cols], qkv_buf[2, r, cols]], axis=0)
            bias = bias_ref[l, m].astype(F32)
            scores = dot_t(keys, both) + jnp.concatenate([bias, bias], axis=1)
            exponent = jnp.exp(scores - jnp.max(scores, axis=0, keepdims=True))
            soft = (exponent * (1.0 / jnp.sum(exponent, axis=0, keepdims=True))).astype(BF16)

            @pl.when(it >= 2)
            def _():
                save_probs(it - 2).wait()

            p_buf[it % 2] = soft
            save_probs(it).start()
            out = t_dot(values, soft)
            out = jnp.concatenate([out[:HD, :rows], out[HD:, rows:]], axis=0)
            mix_buf[r, cols] = out.T.astype(BF16)

        segment = micro * pairs // 4

        def attend_some(s):
            loop(segment, lambda i: attend(s * segment + i))
            gather.step(2 * base + 12 + s)

        loop(4, attend_some)
        save_probs(micro * pairs - 2).wait()
        save_probs(micro * pairs - 1).wait()
        save(mix_buf, 6).start()
        load(base + 4).start()

        def keep_middle(cols, value):
            h_buf[1, :, cols] = h_buf[0, :, cols] + value

        matmul(mix_buf, base + 3, keep_middle)
        save_hidden(1).start()
        save_hidden(0).wait()
        norm(1, 1, f_buf, l)
        save(f_buf, 7).start()
        h_buf[0] = h_buf[1]

        def feed(j):
            load(base + 5 + 2 * j).start()

            def raise_columns(cols, value):
                up, slope = gelu_parts(value)
                lift_buf[:, cols] = up.astype(BF16)
                slope_buf[:, cols] = slope.astype(BF16)

            matmul(f_buf, base + 4 + 2 * j, raise_columns)
            lift_save = pltpu.make_async_copy(lift_buf, saved_ref.at[l, 8 + j], save_sem.at[8])
            slope_save = pltpu.make_async_copy(slope_buf, saved_ref.at[l, 8 + pieces + j], save_sem.at[9])
            lift_save.start()
            slope_save.start()
            gather.step(2 * base + 16 + 4 * j)
            gather.step(2 * base + 17 + 4 * j)

            @pl.when(j < pieces - 1)
            def _():
                load(base + 6 + 2 * j).start()

            def add(cols, value):
                h_buf[0, :, cols] += value

            matmul(lift_buf, base + 5 + 2 * j, add)

            @pl.when(j < pieces - 1)
            def _():
                gather.step(2 * base + 18 + 4 * j)
                gather.step(2 * base + 19 + 4 * j)

            lift_save.wait()
            slope_save.wait()

        loop(pieces, feed)
        save_hidden(1).wait()
        save(a_buf, 0).wait()
        for i in range(3):
            save(qkv_buf.at[i], 1 + i).wait()
        save(far_buf.at[l, 0], 4).wait()
        save(far_buf.at[l, 1], 5).wait()
        save(mix_buf, 6).wait()
        save(f_buf, 7).wait()

        @pl.when(me.role == 0)
        def _():
            far_copy().wait_send()

    loop(layers, layer)

    def store_rows(i):
        r = tile(i, 64)
        a_buf[r, :] = h_buf[0, r, :].astype(BF16)

    loop(rows_all // 64, store_rows)
    done = pltpu.make_async_copy(a_buf, mixed_ref, out_sem)
    done.start()
    done.wait()


def forward(parts, frames, piece, pick, bias, outers, layers, collective_id):
    count, shard, width = parts.shape
    rows_all = frames.shape[0]
    pieces = (count // layers - 4) // 2
    many = outers - 1
    dma = pltpu.SemaphoreType.DMA
    devices = 4 * outers
    split = width // 8
    micro = bias.shape[1]
    keys, rows = bias.shape[2:]
    pairs = width // 128
    any_space = pl.BlockSpec(memory_space=pl.ANY)
    vmem = pl.BlockSpec(memory_space=pltpu.VMEM)
    grid_rows = (rows_all, width)
    return pl.pallas_call(
        functools.partial(forward_kernel, layers, outers, split),
        out_shape=(
            jax.ShapeDtypeStruct((count, outers, 2, 2, shard, width), BF16),
            jax.ShapeDtypeStruct((layers, 8 + 2 * pieces) + grid_rows, BF16),
            jax.ShapeDtypeStruct((layers, 2) + grid_rows, F32),
            jax.ShapeDtypeStruct((layers, micro * pairs, keys, 2 * rows), BF16),
            jax.ShapeDtypeStruct(grid_rows, BF16),
            jax.ShapeDtypeStruct((piece.shape[0], width), BF16),
        ),
        in_specs=[any_space, vmem, vmem, vmem, vmem],
        out_specs=(any_space, any_space, any_space, any_space, any_space, vmem),
        scratch_shapes=[
            pltpu.VMEM((devices,) + piece.shape, BF16),
            pltpu.VMEM((2,) + grid_rows, F32),
            pltpu.VMEM(grid_rows, BF16),
            pltpu.VMEM((3,) + grid_rows, BF16),
            pltpu.VMEM((layers, 2) + grid_rows, BF16),
            pltpu.VMEM(grid_rows, BF16),
            pltpu.VMEM(grid_rows, BF16),
            pltpu.VMEM(grid_rows, BF16),
            pltpu.VMEM(grid_rows, BF16),
            pltpu.VMEM((2, outers, 2, 2, shard, width), BF16),
            pltpu.VMEM((2, keys, 2 * rows), BF16),
            dma((devices - 1,)), dma((devices - 1,)),
            dma((2,)), dma((10,)), dma((2,)), dma((2,)), dma(()), dma((layers,)), dma((layers,)),
        ]
        + Gather.semaphores(many),
        compiler_params=pltpu.CompilerParams(
            collective_id=collective_id, has_side_effects=True, vmem_limit_bytes=58 * 2**20
        ),
        name="gather_and_forward",
    )(parts, frames, piece, pick, bias)


class Reduce:
    lag = 5

    def __init__(self, me, grad_ref, out_ref, split, refs):
        self.me, self.grad, self.out, self.split = me, grad_ref, out_ref, split
        (
            self.own_buf, self.core_buf, self.role_buf, self.pair_buf, self.outer_buf, self.last_buf, self.sum_buf, self.low_buf,
            self.end_buf, self.fin_buf,
            self.own_sem, self.cs, self.cr, self.ys, self.yr, self.xs, self.xr, self.zs, self.zr, self.es, self.er, self.fs,
        ) = refs
        self.width = grad_ref.shape[-1]
        self.main = self.width - split
        self.steps = grad_ref.shape[0]

    @staticmethod
    def scratch(outers, rows, width, split):
        dma = pltpu.SemaphoreType.DMA
        many = outers - 1
        main = width - split
        return [
            pltpu.VMEM((2, outers, 2, rows, width), BF16),
            pltpu.VMEM((SLOTS, outers, 2, rows, width), BF16),
            pltpu.VMEM((SLOTS, outers, 2, rows, split), BF16),
            pltpu.VMEM((SLOTS, outers, rows, main), BF16),
            pltpu.VMEM((SLOTS, many, rows, main), BF16),
            pltpu.VMEM((SLOTS, rows, main), BF16),
            pltpu.VMEM((SLOTS, outers, 2, rows, width), BF16),
            pltpu.VMEM((SLOTS, outers, rows, main), BF16),
            pltpu.VMEM((SLOTS, rows, main), BF16),
            pltpu.VMEM((SLOTS, rows, width), F32),
            dma((2,)),
            dma((SLOTS,)), dma((SLOTS,)),
            dma((SLOTS,)), dma((SLOTS,)),
            dma((SLOTS,)), dma((SLOTS,)),
            dma((SLOTS, many)), dma((SLOTS, many)),
            dma((SLOTS,)), dma((SLOTS,)),
            dma((SLOTS,)),
        ]

    def cols(self, offset, size):
        return pl.ds(pl.multiple_of(offset, 128), size)

    def main_cols(self):
        return self.cols(self.me.role * self.split, self.main)

    def keep_cols(self):
        return self.cols(self.me.role * self.main, self.split)

    def give_cols(self):
        return self.cols((1 - self.me.role) * self.main, self.split)

    def own(self, k):
        s = lax.rem(k, 2)
        return pltpu.make_async_copy(self.grad.at[k, :, :, self.me.core], self.own_buf.at[s], self.own_sem.at[s])

    def c_copy(self, k):
        s = lax.rem(k, SLOTS)
        return remote(self.grad.at[k, :, :, 1 - self.me.core], self.core_buf.at[s], self.cs.at[s], self.cr.at[s], self.me.sibling())

    def y_copy(self, k):
        s = lax.rem(k, SLOTS)
        return remote(
            self.sum_buf.at[s, :, :, :, self.give_cols()], self.role_buf.at[s], self.ys.at[s], self.yr.at[s], self.me.other_role()
        )

    def x_copy(self, k):
        s = lax.rem(k, SLOTS)
        return remote(
            self.sum_buf.at[s, :, 1 - self.me.pair, :, self.main_cols()],
            self.pair_buf.at[s], self.xs.at[s], self.xr.at[s], self.me.across(),
        )

    def z_copy(self, k, by):
        s = lax.rem(k, SLOTS)
        me = self.me
        return remote(
            self.low_buf.at[s, lax.rem(me.outer + by, me.outers)], self.outer_buf.at[s, by - 1],
            self.zs.at[s, by - 1], self.zr.at[s, by - 1], me.along(by),
        )

    def e_copy(self, k):
        s = lax.rem(k, SLOTS)
        return remote(self.end_buf.at[s], self.last_buf.at[s], self.es.at[s], self.er.at[s], self.me.other_role())

    def f_copy(self, k):
        s = lax.rem(k, SLOTS)
        return pltpu.make_async_copy(self.fin_buf.at[s], self.out.at[k], self.fs.at[s])

    def step(self, t):
        me, count, split, main = self.me, self.steps, self.split, self.main
        others = range(1, me.outers)

        @pl.when((t >= 0) & (t < count))
        def _():
            self.own(t).start()
            self.c_copy(t).start()

        @pl.when((t >= 1) & (t < count + 1))
        def _():
            k = t - 1
            s = lax.rem(k, SLOTS)
            self.own(k).wait()
            self.c_copy(k).wait()

            def add(i):
                o, p = lax.div(i, 2), lax.rem(i, 2)
                self.sum_buf[s, o, p] = self.own_buf[lax.rem(k, 2), o, p] + self.core_buf[s, o, p]

            loop(2 * me.outers, add)
            self.y_copy(k).start()

        @pl.when((t >= 2) & (t < count + 2))
        def _():
            k = t - 2
            s = lax.rem(k, SLOTS)
            self.y_copy(k).wait()
            keep = self.keep_cols()

            def add(i):
                o, p = lax.div(i, 2), lax.rem(i, 2)
                self.sum_buf[s, o, p, :, keep] = self.sum_buf[s, o, p, :, keep] + self.role_buf[s, o, p]

            loop(2 * me.outers, add)
            self.x_copy(k).start()

        @pl.when((t >= 3) & (t < count + 3))
        def _():
            k = t - 3
            s = lax.rem(k, SLOTS)
            self.x_copy(k).wait()
            cols = self.main_cols()

            def add(o):
                self.low_buf[s, o] = self.sum_buf[s, o, me.pair, :, cols] + self.pair_buf[s, o]

            loop(me.outers, add)
            for by in others:
                self.z_copy(k, by).start()

        @pl.when((t >= 4) & (t < count + 4))
        def _():
            k = t - 4
            s = lax.rem(k, SLOTS)
            for by in others:
                self.z_copy(k, by).wait()
            total = self.low_buf[s, me.outer].astype(F32)
            for by in others:
                total = total + self.outer_buf[s, by - 1].astype(F32)
            self.end_buf[s] = total.astype(BF16)
            self.e_copy(k).start()

        @pl.when((t >= 5) & (t < count + 5))
        def _():
            k = t - 5
            s = lax.rem(k, SLOTS)
            self.e_copy(k).wait()

            @pl.when(k >= SLOTS)
            def _():
                self.f_copy(k - SLOTS).wait()

            mid = main - split
            mine = self.end_buf[s].astype(F32)
            theirs = self.last_buf[s].astype(F32)

            @pl.when(me.role == 0)
            def _():
                self.fin_buf[s, :, :split] = mine[:, :split]
                self.fin_buf[s, :, split:main] = mine[:, split:] + theirs[:, :mid]
                self.fin_buf[s, :, main:] = theirs[:, mid:]

            @pl.when(me.role == 1)
            def _():
                self.fin_buf[s, :, :split] = theirs[:, :split]
                self.fin_buf[s, :, split:main] = theirs[:, split:] + mine[:, :mid]
                self.fin_buf[s, :, main:] = mine[:, mid:]

            self.f_copy(k).start()

    def finish(self):
        for k in range(self.steps - SLOTS, self.steps):
            self.f_copy(k).wait()


def backward_kernel(
    layers, outers, split,
    full_ref, saved_ref, hidden_ref, probs_ref, cot_ref, table_ref, pick_ref, used_ref,
    grad_ref, out_ref, frames_grad_ref, table_out_ref,
    g_buf, acc_buf, h_buf, w_buf, low_buf, act_buf, give_buf, back_buf, p_buf, stage_buf, tab_sum, tab_in, tab_role, tab_back,
    act_sem, h_sem, w_sem, p_sem, stage_sem, ks, kr, ts, tr, rs_sem, rr_sem, out_sem, *reduce_refs,
):
    me = Place(outers)
    devices = 4 * outers
    rows_all, width = cot_ref.shape
    per_layer = full_ref.shape[0] // layers
    pieces = (per_layer - 4) // 2
    pairs = width // 128
    micro = probs_ref.shape[1] // pairs
    rows = rows_all // micro
    shard = grad_ref.shape[-2]
    tile_outers = WIDE // (4 * shard)
    block = 128
    reduce = Reduce(me, grad_ref, out_ref, split, reduce_refs)
    me.greet()

    def load_rows(i):
        r = tile(i, block)
        g_buf[r, :] = cot_ref[r, :].astype(F32)

    loop(rows_all // block, load_rows)
    tab_sum[...] = jnp.zeros_like(tab_sum)

    def get(l, item, slot):
        return pltpu.make_async_copy(saved_ref.at[l, item], act_buf.at[slot], act_sem.at[slot])

    def get_hidden(l, which):
        return pltpu.make_async_copy(hidden_ref.at[l, which], h_buf, h_sem)

    def get_w(k, slot):
        return pltpu.make_async_copy(full_ref.at[k], w_buf.at[slot], w_sem.at[slot])

    def send_stage(n):
        s = lax.rem(n, 2)
        return pltpu.make_async_copy(stage_buf.at[s], grad_ref.at[n], stage_sem.at[s])

    def produce(n, left, right):
        s = lax.rem(n, 2)

        def some(i):
            value = t_dot(left[:, tile(i, WIDE)], right[...]).astype(BF16)
            stage_buf[s, pl.ds(i * tile_outers, tile_outers)] = value.reshape(tile_outers, 2, 2, shard, width)

        loop(width // WIDE, some)
        send_stage(n).start()

        @pl.when(n >= 1)
        def _():
            send_stage(n - 1).wait()

    def through(left, slot, finish):
        def some(i):
            cols = tile(i, WIDE)
            finish(cols, dot_t(left[...], w_buf[slot, cols, :]))

        loop(width // WIDE, some)

    def lower(dst, src):
        def some(i):
            r = tile(i, block)
            dst[r, :] = src[r, :].astype(BF16)

        loop(rows_all // block, some)

    def norm_back(index, l):
        def some(i):
            r = tile(i, block)
            unit, inverse = normalize(h_buf[r, :])
            scale = dot(pick_ref[l * 4 + 2 * index, r, :], table_ref[...])
            grad = acc_buf[r, :]
            g_buf[r, :] = g_buf[r, :] + norm_backward(grad, scale, unit, inverse)
            for which, values in ((0, grad * unit), (1, grad)):
                picked = used_ref[l * 4 + 2 * index + which, :, r]
                high = values.astype(BF16)
                rest = (values - high.astype(F32)).astype(BF16)
                tab_sum[...] += dot(picked, high) + dot(picked, rest)

        loop(rows_all // block, some)

    def layer(turn):
        l = layers - 1 - turn
        base = l * per_layer
        n0 = turn * per_layer

        def service(index):
            reduce.step(n0 + index - 1)

        get(l, 7, 0).start()
        get(l, 8, 1).start()
        get(l, 8 + pieces, 3).start()
        get_w(base + 5, 0).start()
        get_hidden(l, 1).start()
        lower(low_buf, g_buf)
        acc_buf[...] = jnp.zeros_like(acc_buf)
        get(l, 7, 0).wait()

        def feed(j):
            s = lax.rem(j, 2)
            get_w(base + 4 + 2 * j, 1).start()
            get(l, 8 + j, 1 + s).wait()
            get(l, 8 + pieces + j, 3 + s).wait()

            @pl.when(j < pieces - 1)
            def _():
                get(l, 9 + j, 2 - s).start()
                get(l, 9 + pieces + j, 4 - s).start()

            produce(n0 + 2 * j, act_buf.at[1 + s], low_buf)
            get_w(base + 5 + 2 * j, 0).wait()

            def lift(cols, value):
                act_buf[5, :, cols] = (value * act_buf[3 + s, :, cols].astype(F32)).astype(BF16)

            through(low_buf, 0, lift)

            @pl.when(j < pieces - 1)
            def _():
                get_w(base + 7 + 2 * j, 0).start()

            service(j)
            produce(n0 + 2 * j + 1, act_buf.at[0], act_buf.at[5])
            get_w(base + 4 + 2 * j, 1).wait()

            def add(cols, value):
                acc_buf[:, cols] += value

            through(act_buf.at[5], 1, add)

        loop(pieces, feed)
        get_w(base + 3, 0).start()
        get(l, 6, 0).start()
        for i in range(5):
            get(l, 1 + i, 1 + i).start()

        def get_probs(it):
            s = lax.rem(it, 2)
            return pltpu.make_async_copy(probs_ref.at[l, it], p_buf.at[s], p_sem.at[s])

        get_probs(0).start()
        get_hidden(l, 1).wait()
        norm_back(1, l)
        lower(low_buf, g_buf)
        service(pieces)
        get(l, 6, 0).wait()
        produce(n0 + 2 * pieces, act_buf.at[0], low_buf)
        get_w(base + 3, 0).wait()

        def keep_mixture(cols, value):
            act_buf[6, :, cols] = value.astype(BF16)

        through(low_buf, 0, keep_mixture)
        get_w(base, 0).start()
        get(l, 0, 8).start()
        for i in range(5):
            get(l, 1 + i, 1 + i).wait()

        def attend(it):
            m, p = lax.div(it, pairs), lax.rem(it, pairs)
            r, cols = tile(m, rows), tile(p, 128)
            first = lax.broadcasted_iota(jnp.int32, (rows, 128), 1) < HD

            def both_of(x):
                return jnp.concatenate([jnp.where(first, x, 0.0).astype(BF16), jnp.where(first, 0.0, x).astype(BF16)], axis=0)

            queries = both_of(act_buf[1, r, cols].astype(F32) * HD**-0.5)
            out_grad = both_of(act_buf[6, r, cols].astype(F32))
            keys = jnp.concatenate([act_buf[4, r, cols], act_buf[2, r, cols]], axis=0)
            values = jnp.concatenate([act_buf[5, r, cols], act_buf[3, r, cols]], axis=0)
            get_probs(it).wait()

            @pl.when(it + 1 < micro * pairs)
            def _():
                get_probs(it + 1).start()

            soft_low = p_buf[lax.rem(it, 2)]
            soft = soft_low.astype(F32)
            grad_soft = dot_t(values, out_grad)
            inner = jnp.sum(soft * grad_soft, axis=0, keepdims=True)
            grad_scores = (soft * (grad_soft - inner)).astype(BF16)
            grad_values = dot(soft_low, out_grad)
            grad_keys = dot(grad_scores, queries)
            give_buf[0, r, cols] = grad_keys[:rows].astype(BF16)
            give_buf[1, r, cols] = grad_values[:rows].astype(BF16)
            h_buf[r, cols] = grad_keys[rows:]
            acc_buf[r, cols] = grad_values[rows:]
            out = t_dot(keys, grad_scores) * HD**-0.5
            out = jnp.concatenate([out[:HD, :rows], out[HD:, rows:]], axis=0)
            act_buf[7, r, cols] = out.T.astype(BF16)

        segment = micro * pairs // 4

        def attend_some(s):
            loop(segment, lambda i: attend(s * segment + i))
            service(pieces + 1 + s)

        loop(4, attend_some)

        def back_copy():
            return remote(give_buf, back_buf.at[l], ks.at[l], kr.at[l], me.other_role())

        @pl.when(me.role == 1)
        def _():
            back_copy().start()

        @pl.when(me.role == 0)
        def _():
            back_copy().wait_recv()

            def some(i):
                r = tile(i, block)
                act_buf[1, r, :] = (h_buf[r, :] + back_buf[l, 0, r, :].astype(F32)).astype(BF16)
                act_buf[2, r, :] = (acc_buf[r, :] + back_buf[l, 1, r, :].astype(F32)).astype(BF16)

            loop(rows_all // block, some)

        @pl.when(me.role == 1)
        def _():
            def some(i):
                r = tile(i, block)
                act_buf[1, r, :] = h_buf[r, :].astype(BF16)
                act_buf[2, r, :] = acc_buf[r, :].astype(BF16)

            loop(rows_all // block, some)

        get_hidden(l, 0).start()
        acc_buf[...] = jnp.zeros_like(acc_buf)
        get(l, 0, 8).wait()

        def project(i):
            s = lax.rem(i, 2)

            @pl.when(i < 2)
            def _():
                get_w(base + 1 + i, 1 - s).start()

            part = act_buf.at[jnp.where(i == 0, 7, i)]
            produce(n0 + 2 * pieces + 1 + i, act_buf.at[8], part)
            get_w(base + i, s).wait()

            def add(cols, value):
                acc_buf[:, cols] += value

            through(part, s, add)
            service(pieces + 5 + i)

        loop(3, project)
        get_hidden(l, 0).wait()
        norm_back(0, l)

        @pl.when(me.role == 1)
        def _():
            back_copy().wait_send()

    loop(layers, layer)
    lower(low_buf, g_buf)
    done = pltpu.make_async_copy(low_buf, frames_grad_ref, out_sem)
    done.start()

    per = 128 * devices // width
    for group in range(width // 128):
        tab_role[group] = tab_sum[:, group * 128 : group * 128 + 128]

    def tab_copy(by):
        to = lax.rem(me.dp + by, devices)
        return remote(tab_role.at[lax.div(to, per)], tab_in.at[me.dp], ts.at[by - 1], tr.at[by - 1], me.around(by))

    def tab_wait(by):
        here = tab_in.at[lax.rem(me.dp - by + devices, devices)]
        remote(here, here, ts.at[by - 1], tr.at[by - 1], me.around(by)).wait_recv()

    loop(devices - 1, lambda i: tab_copy(i + 1).start())
    tab_in[me.dp] = tab_role[lax.div(me.dp, per)]
    last = layers * per_layer - 1
    send_stage(last).wait()
    loop(2, lambda i: reduce.step(last + i))
    loop(devices - 1, lambda i: tab_wait(i + 1))
    loop(devices - 1, lambda i: tab_copy(i + 1).wait_send())
    total = tab_in[0]
    for i in range(1, devices):
        total = total + tab_in[i]
    tab_back[0] = total
    swap = remote(tab_back.at[0], tab_back.at[1], rs_sem, rr_sem, me.other_role())
    swap.start()
    loop(reduce.lag - 1, lambda i: reduce.step(last + 2 + i))
    swap.wait()
    table_out_ref[...] = tab_back[0] + tab_back[1]
    reduce.finish()
    done.wait()


def backward(full, saved, hidden, probs, cotangent, table, pick, used, outers, layers, shard, collective_id):
    count = full.shape[0]
    rows_all, width = cotangent.shape
    keys = probs.shape[2]
    small = table.shape[0]
    dma = pltpu.SemaphoreType.DMA
    devices = 4 * outers
    split = width // 4
    any_space = pl.BlockSpec(memory_space=pl.ANY)
    vmem = pl.BlockSpec(memory_space=pltpu.VMEM)
    grid_rows = (rows_all, width)
    return pl.pallas_call(
        functools.partial(backward_kernel, layers, outers, split),
        out_shape=(
            jax.ShapeDtypeStruct((count, outers, 2, 2, shard, width), BF16),
            jax.ShapeDtypeStruct((count, shard, width), F32),
            jax.ShapeDtypeStruct(grid_rows, BF16),
            jax.ShapeDtypeStruct((small, 128), F32),
        ),
        in_specs=[any_space, any_space, any_space, any_space, vmem, vmem, vmem, vmem],
        out_specs=(any_space, any_space, any_space, vmem),
        scratch_shapes=[
            pltpu.VMEM(grid_rows, F32),
            pltpu.VMEM(grid_rows, F32),
            pltpu.VMEM(grid_rows, F32),
            pltpu.VMEM((2, width, width), BF16),
            pltpu.VMEM(grid_rows, BF16),
            pltpu.VMEM((9,) + grid_rows, BF16),
            pltpu.VMEM((2,) + grid_rows, BF16),
            pltpu.VMEM((layers, 2) + grid_rows, BF16),
            pltpu.VMEM((2, keys, keys), BF16),
            pltpu.VMEM((2, outers, 2, 2, shard, width), BF16),
            pltpu.VMEM((small, width), F32),
            pltpu.VMEM((devices, small, 128), F32),
            pltpu.VMEM((width // 128, small, 128), F32),
            pltpu.VMEM((2, small, 128), F32),
            dma((9,)), dma(()), dma((2,)), dma((2,)), dma((2,)), dma((layers,)), dma((layers,)),
            dma((devices - 1,)), dma((devices - 1,)), dma(()), dma(()), dma(()),
        ]
        + Reduce.scratch(outers, shard, width, split),
        compiler_params=pltpu.CompilerParams(
            collective_id=collective_id, has_side_effects=True, vmem_limit_bytes=60 * 2**20
        ),
        name="backward_and_reduce",
    )(full, saved, hidden, probs, cotangent, table, pick, used)


def prepare(
    inner_weight, outer_weight, expand_weight, shrink_weight, causal_gain, causal_shift,
    section_scale, section_shift, prompt_lengths, target_lengths, sections, rows,
):
    is_target = lax.axis_index("role") == 1
    layers, shard, _ = inner_weight.shape
    width = outer_weight.shape[2]
    devices = width // shard
    pieces = expand_weight.shape[2] // width
    segs = section_scale.shape[0]
    micro = prompt_lengths.shape[0]
    outer = outer_weight[:, None]
    inner = inner_weight.reshape(layers, shard, 3, width).transpose(0, 2, 1, 3)
    expand = expand_weight.reshape(layers, shard, devices, pieces, shard).transpose(0, 3, 1, 2, 4)
    expand = expand.reshape(layers, pieces, 1, shard, width)
    shrink = shrink_weight.reshape(layers, pieces, 1, shard, width)
    feed = jnp.concatenate([expand, shrink], axis=2).reshape(layers, 2 * pieces, shard, width)
    parts = jnp.concatenate([inner, outer, feed], axis=1).reshape(-1, shard, width)

    small = jnp.concatenate(
        [causal_gain, causal_shift, section_scale.reshape(2 * segs, -1), section_shift.reshape(2 * segs, -1)], axis=0
    )
    per = 128 // shard
    spot = (lax.axis_index("dp") % per) * shard
    piece = lax.dynamic_update_slice(jnp.zeros((small.shape[0], 128), BF16), small, (0, spot))

    masks = [[], []]
    section_frames = []
    for m in range(micro):
        prompt_row, target_row, section_row = prompt_lengths[m, 0], target_lengths[m, 0], sections[m, 0]
        prompt_segment, prompt_position, prompt_member = frame_tags(prompt_row, jnp.zeros_like(prompt_row), rows)
        target_segment, target_position, target_member = frame_tags(target_row, prompt_row, rows)
        own_segment = jnp.where(is_target, target_segment, prompt_segment)
        own_position = jnp.where(is_target, target_position, prompt_position)
        own_member = jnp.where(is_target, target_member, prompt_member)
        same_far = (own_segment[None, :] == prompt_segment[:, None]) & is_target
        same_own = own_segment[None, :] == own_segment[:, None]
        causal_own = same_own & (own_position[:, None] <= own_position[None, :])
        masks[0].append(jnp.concatenate([same_far, causal_own], axis=0))
        masks[1].append(jnp.concatenate([same_far, same_own], axis=0))
        section_frames.append(jnp.sum(jnp.where(own_member, section_row[None, :], 0), axis=1))
    bias = jnp.where(jnp.stack([jnp.stack(one) for one in masks]), 0.0, -1e30).astype(BF16)
    section = jnp.concatenate(section_frames)
    none = jnp.zeros_like(section)
    first, second = 4 + 2 * section, 4 + 2 * segs + 2 * section
    used = jnp.stack([none, none + 2, none + 1, none + 3, first, second, first + 1, second + 1])
    return parts, piece, used, bias


def body(
    frames, cotangent, inner_weight, outer_weight, expand_weight, shrink_weight, causal_gain, causal_shift,
    section_scale, section_shift, prompt_lengths, target_lengths, sections,
):
    _, micro, rows, width = frames.shape
    layers, shard, _ = inner_weight.shape
    devices = width // shard
    outers = devices // 4
    pieces = expand_weight.shape[2] // width
    segs = section_scale.shape[0]
    parts, piece, used, bias = prepare(
        inner_weight, outer_weight, expand_weight, shrink_weight, causal_gain, causal_shift,
        section_scale, section_shift, prompt_lengths, target_lengths, sections, rows,
    )
    entries = jnp.arange(piece.shape[0], dtype=jnp.int32)
    pick = (used[:, :, None] == entries[None, None, :]).astype(BF16)
    pick_t = (used[:, None, :] == entries[None, :, None]).astype(BF16)
    full, saved, hidden, probs, mixed, table = forward(
        parts, frames.reshape(micro * rows, width), piece, pick, bias, outers, layers, 0
    )
    _, owned, frames_grad, small = backward(
        full.reshape(-1, width, width), saved, hidden, probs, cotangent.reshape(micro * rows, width),
        table, pick, pick_t, outers, layers, shard, 1,
    )
    owned = owned.reshape(layers, -1, shard, width)[::-1]
    feed = owned[:, : 2 * pieces].reshape(layers, pieces, 2, shard, width)
    inner_grad = owned[:, 2 * pieces + 1 :].transpose(0, 2, 1, 3).reshape(layers, shard, 3 * width)
    outer_grad = owned[:, 2 * pieces]
    expand_grad = feed[:, :, 1].reshape(layers, pieces, shard, devices, shard).transpose(0, 2, 3, 1, 4).reshape(layers, shard, -1)
    shrink_grad = feed[:, :, 0].reshape(layers, pieces * shard, width)
    per = 128 // shard
    spot = (lax.axis_index("dp") % per) * shard
    small = lax.dynamic_slice(small, (0, spot), (small.shape[0], shard))
    return (
        mixed.reshape(1, micro, rows, width), frames_grad.reshape(1, micro, rows, width),
        inner_grad, outer_grad, expand_grad, shrink_grad,
        small[0:2], small[2:4],
        small[4 : 4 + 2 * segs].reshape(segs, 2, shard),
        small[4 + 2 * segs :].reshape(segs, 2, shard),
    )


def solution(mesh):
    rows = P("role", None, "dp", None)
    second = P(None, "dp", None)
    placed = (rows, rows, second, second, second, second, P(None, "dp"), P(None, "dp"), P(None, None, "dp"), P(None, None, "dp"), second, second, second)
    given = (rows, rows, second, second, second, second, P(None, "dp"), P(None, "dp"), P(None, None, "dp"), P(None, None, "dp"))
    return jax.shard_map(body, mesh=mesh, in_specs=placed, out_specs=given, check_vma=False)
```

time: 2140 us -> 796 us (0.37)
  waiting for transfers between devices: 1440 us -> 0 us
  Pallas kernels: 0 us -> 739 us
  matrix products: 410 us -> 0 us
  blocking collectives: 86.9 us -> 0 us
  other arithmetic: 73.8 us -> 8.16 us
  starting transfers between devices: 34.3 us -> 0 us
    reduce_scatter x8 -> x0, waiting for transfers between devices: 866 us -> none  [the longest x2 359 us: scatter_each(): lax.psum_scatter(grads[2], 'dp', scatter_dimension=0, tiled=True)]
    pallas_call x0 -> x2, Pallas kernels: none -> 739 us  [the longest x1 380 us: forward(): pl.pallas_call(functools.partial(forward_kernel, layers, outers, split),...]
    dot_general x96 -> x0, matrix products: 410 us -> none  [the longest x4 60.9 us: layer_forward(): upper = jnp.dot(second_low, expand, preferred_element_type=jnp.float32)]
    all_gather x8 -> x0, waiting for transfers between devices: 240 us -> none  [the longest x2 119 us: fetch_forward(): lax.all_gather(shrink, 'dp', axis=0, tiled=True)]
    unnamed x25 -> x0, waiting for transfers between devices: 212 us -> none
    all_gather x4 -> x0, blocking collectives: 81.9 us -> none  [the longest x2 43.9 us: fetch_forward(): lax.all_gather(scale_table, 'dp', axis=2, tiled=True)]
    psum x1 -> x0, waiting for transfers between devices: 81.1 us -> none  [body(): lax.psum(second_set[0].astype(jnp.bfloat16), 'role').astype(jnp.float32)]
    ppermute x16 -> x0, waiting for transfers between devices: 35.7 us -> none  [shifted_2(): return lax.ppermute(x, axis, pairs)]
  transfers between devices with their start and end apart: 37 -> 0, of which waited for: 20 -> 0; matrix products, arithmetic and copies ran while one was open for 22% -> 0% of each run, Pallas kernels for 0% -> 0%
where the time goes in v2:
time: 796 us; the launch traced here: 795 us
  Pallas kernels  739 us (93%)
  local copies, waits for them, and re-layouts  47.3 us (6%)
  other arithmetic  8.16 us (1%)
    pallas_call x1, Pallas kernels, forward(): pl.pallas_call(functools.partial(forward_kernel, layers, outers, split),...  380 us
    pallas_call x1, Pallas kernels, backward(): pl.pallas_call(functools.partial(backward_kernel, layers, outers, split),...  358 us

profile of v2, /device:TPU:0, one launch (start us, length us, event | category | flops | bytes accessed | tf_op | source)
XLA Modules:
  0.0 795.1 jit_solution(16664801128914371868)
XLA Ops:
  0.6 5.0 reshape.271
  5.6 1.9 copy.42
  7.5 1.5 reshape.272
  9.0 1.4 pad_maximum_fusion.1
  10.4 0.2 copy.43
  10.6 2.8 reshape.270
  13.4 0.3 copy.44
  13.8 1.9 pad_maximum_fusion
  15.8 0.2 dynamic_update_slice.3.piece_ref
  16.9 1.5 fusion.pick_ref
  18.4 0.2 compare_and_fusion
  18.7 0.2 compare_and_fusion.2
  19.0 1.2 select_convert_fusion.bias_ref
  20.3 380.4 %gather_and_forward.1 = (bf16[24,4,2,2,64,1024]{5,4,3,2,1,0:T(8,128)(2,1)}, bf16[2,16,512,1024]{3,2,1,0:T(8,128)(2,1)}, f32[2,2,512,1024]{3,2,1,0:T(8,128)}, bf1...) custom-call(bf16[24,64,1024]{2,1,0:T(8,128)(2,1)} %bitcast.68, ...), custom_call_target="tpu_custom_call" | custom-call | tf_op jit(solution)/shard_map/gather_and_forward/pallas_call | solution.py:478
  400.7 0.8 fusion.1.used_ref
  401.4 358.2 %backward_and_reduce.1 = (bf16[24,4,2,2,64,1024]{5,4,3,2,1,0:T(8,128)(2,1)}, f32[24,64,1024]{2,1,0:T(8,128)}, bf16[512,1024]{1,0:T(8,128)(2,1)}, f32[32,128]{1,0:T(8,128)}) custom-call(bf16[24,1024,1024]{2,1,0:T(8,128)(2,1)} %bitcast.65, bf16[2,16,512,1024]{3,2,1,0:T(8,128)(2,1)} %get-tuple-element.21.saved_ref, ...), custom_call_target="tpu_custom_call" | custom-call | tf_op jit(solution)/shard_map/backward_and_reduce/pallas_call | solution.py:1003
  759.6 1.5 slice.72
  761.1 0.2 reverse_bitcast_fusion
  761.3 1.3 copy.48
  762.6 1.9 copy-done
  764.5 0.8 reverse_bitcast_fusion.1
  765.4 2.2 slice.74
  767.6 4.7 slice.65
  772.3 4.0 fusion.8
  776.3 2.5 reshape_squeeze.6
  778.8 6.9 copy.47
  785.7 5.6 reshape.286
  791.2 0.6 fusion.10
  791.9 0.6 reshape.287
  792.6 0.6 reshape.288
  793.2 1.0 copy.52
  794.1 1.0 copy.53
  (58 shorter events, 1.3 us)
Async XLA Ops:
  10.6 3.1 copy-start.3
  13.7 2.0 copy-start.8
  13.7 2.0 copy-start.9
  13.7 2.0 copy-start.11
  13.7 2.0 copy-start.12
  13.7 2.2 copy-start.6
  13.7 2.4 copy-start.7
  13.8 2.6 copy-start.10
  15.9 4.3 copy-start.4
  761.1 3.4 copy-start
  785.7 5.6 copy-start.5
  785.7 7.5 copy-start.1
  791.2 2.9 copy-start.2

commit v3 on v2

--- a/solution.py
+++ b/solution.py
@@ -20,9 +20,9 @@
         self.outers = outer_count
         self.role = lax.axis_index("role")
         dp = lax.axis_index("dp")
-        self.core = dp % 2
-        self.pair = (dp // 2) % 2
-        self.outer = dp // 4
+        self.core = lax.rem(dp, 2)
+        self.pair = lax.rem(lax.div(dp, 2), 2)
+        self.outer = lax.div(dp, 4)
         self.dp = dp
 
     def at(self, role, outer, pair, core):
@@ -38,10 +38,10 @@
         return self.at(1 - self.role, self.outer, self.pair, self.core)
 
     def along(self, by):
-        return self.at(self.role, (self.outer + by) % self.outers, self.pair, self.core)
+        return self.at(self.role, lax.rem(self.outer + by, self.outers), self.pair, self.core)
 
     def around(self, by):
-        return (self.role, (self.dp + by) % (4 * self.outers))
+        return (self.role, lax.rem(self.dp + by, 4 * self.outers))
 
     def greet(self):
         barrier = pltpu.get_barrier_semaphore()
@@ -107,7 +107,7 @@
 
 
 class Gather:
-    lag = 4
+    lag = 7
 
     def __init__(self, me, part_ref, full_ref, split, sems):
         self.me, self.part, self.full, self.split = me, part_ref, full_ref, split
@@ -120,16 +120,16 @@
     def semaphores(many):
         dma = pltpu.SemaphoreType.DMA
         return [
-            dma((SLOTS,)),
-            dma((SLOTS, many)), dma((SLOTS, many)),
-            dma((SLOTS,)), dma((SLOTS,)),
-            dma((2 * SLOTS, many)), dma((2 * SLOTS, many)),
-            dma((SLOTS,)), dma((SLOTS,)),
-            dma((SLOTS,)), dma((SLOTS,)),
+            dma((8,)),
+            dma((8, many)), dma((8, many)),
+            dma((8,)), dma((8,)),
+            dma((12, many)), dma((12, many)),
+            dma((8,)), dma((8,)),
+            dma((8,)), dma((8,)),
         ]
 
     def cols(self, h, offset, size):
-        return pl.ds(pl.multiple_of((h % 2) * self.half + offset, 128), size)
+        return pl.ds(pl.multiple_of(lax.rem(h, 2) * self.half + offset, 128), size)
 
     def main_cols(self, h):
         return self.cols(h, self.me.role * self.split, self.main)
@@ -141,45 +141,45 @@
         return self.cols(h, (1 - self.me.role) * self.main, self.split)
 
     def before(self, by):
-        return (self.me.outer - by + self.me.outers) % self.me.outers
+        return lax.rem(self.me.outer - by + self.me.outers, self.me.outers)
 
     def own(self, h):
         me, cols = self.me, self.cols(h, 0, self.half)
         return pltpu.make_async_copy(
-            self.part.at[h // 2, :, cols], self.full.at[h // 2, me.outer, me.pair, me.core, :, cols], self.own_sem.at[h % SLOTS]
+            self.part.at[lax.div(h, 2), :, cols], self.full.at[lax.div(h, 2), me.outer, me.pair, me.core, :, cols], self.own_sem.at[lax.rem(h, 8)]
         )
 
     def z_copy(self, h, by):
-        me, cols, s = self.me, self.main_cols(h), h % SLOTS
+        me, cols, s = self.me, self.main_cols(h), lax.rem(h, 8)
         return remote(
-            self.part.at[h // 2, :, cols],
-            self.full.at[h // 2, me.outer, me.pair, me.core, :, cols],
+            self.part.at[lax.div(h, 2), :, cols],
+            self.full.at[lax.div(h, 2), me.outer, me.pair, me.core, :, cols],
             self.zs.at[s, by - 1], self.zr.at[s, by - 1], me.along(by),
         )
 
     def z_wait(self, h, by):
-        me, s = self.me, h % SLOTS
-        dst = self.full.at[h // 2, self.before(by), me.pair, me.core, :, self.main_cols(h)]
+        me, s = self.me, lax.rem(h, 8)
+        dst = self.full.at[lax.div(h, 2), self.before(by), me.pair, me.core, :, self.main_cols(h)]
         remote(dst, dst, self.zs.at[s, by - 1], self.zr.at[s, by - 1], me.along(by)).wait_recv()
 
     def x_copy(self, h, pair):
-        me, s = self.me, h % SLOTS
-        ref = self.full.at[h // 2, :, pair, me.core, :, self.main_cols(h)]
+        me, s = self.me, lax.rem(h, 8)
+        ref = self.full.at[lax.div(h, 2), :, pair, me.core, :, self.main_cols(h)]
         return remote(ref, ref, self.xs.at[s], self.xr.at[s], me.across())
 
     def u_copy(self, h, by, cols):
-        me, s = self.me, h % (2 * SLOTS)
-        ref = self.full.at[h // 2, self.before(by), me.pair, me.core, :, cols]
+        me, s = self.me, lax.rem(h, 12)
+        ref = self.full.at[lax.div(h, 2), self.before(by), me.pair, me.core, :, cols]
         return remote(ref, ref, self.us.at[s, by - 1], self.ur.at[s, by - 1], me.other_role())
 
     def v_copy(self, h, cols):
-        me, s = self.me, h % SLOTS
-        ref = self.full.at[h // 2, :, 1 - me.pair, me.core, :, cols]
+        me, s = self.me, lax.rem(h, 8)
+        ref = self.full.at[lax.div(h, 2), :, 1 - me.pair, me.core, :, cols]
         return remote(ref, ref, self.vs.at[s], self.vr.at[s], me.other_role())
 
     def c_copy(self, h, core):
-        s = h % SLOTS
-        ref = self.full.at[h // 2, :, :, core, :, self.cols(h, 0, self.half)]
+        s = lax.rem(h, 8)
+        ref = self.full.at[lax.div(h, 2), :, :, core, :, self.cols(h, 0, self.half)]
         return remote(ref, ref, self.cs.at[s], self.cr.at[s], self.me.sibling())
 
     def step(self, t):
@@ -192,9 +192,9 @@
             for by in others:
                 self.z_copy(t, by).start()
 
-        @pl.when((t >= 1) & (t < count + 1))
-        def _():
-            h = t - 1
+        @pl.when((t >= 2) & (t < count + 2))
+        def _():
+            h = t - 2
             self.own(h).wait()
             for by in others:
                 self.z_wait(h, by)
@@ -202,28 +202,29 @@
             for by in others:
                 self.u_copy(h, by, self.give_cols(h)).start()
 
-        @pl.when((t >= 2) & (t < count + 2))
-        def _():
-            h = t - 2
+        @pl.when((t >= 4) & (t < count + 4))
+        def _():
+            h = t - 4
             self.x_copy(h, 1 - me.pair).wait_recv()
             self.v_copy(h, self.give_cols(h)).start()
-
-        @pl.when((t >= 3) & (t < count + 3))
-        def _():
-            h = t - 3
+            for by in others:
+                self.z_copy(h, by).wait_send()
+
+        @pl.when((t >= 6) & (t < count + 6))
+        def _():
+            h = t - 6
             for by in others:
                 self.u_copy(h, by, self.take_cols(h)).wait_recv()
             self.v_copy(h, self.take_cols(h)).wait_recv()
             self.c_copy(h, me.core).start()
             for by in others:
-                self.z_copy(h, by).wait_send()
                 self.u_copy(h, by, self.give_cols(h)).wait_send()
             self.x_copy(h, me.pair).wait_send()
             self.v_copy(h, self.give_cols(h)).wait_send()
 
-        @pl.when((t >= 4) & (t < count + 4))
-        def _():
-            h = t - 4
+        @pl.when((t >= 7) & (t < count + 7))
+        def _():
+            h = t - 7
             self.c_copy(h, 1 - me.core).wait_recv()
             self.c_copy(h, me.core).wait_send()
 
@@ -247,7 +248,7 @@
     layers, outers, split,
     part_ref, frames_ref, piece_ref, pick_ref, bias_ref,
     full_ref, saved_ref, hidden_ref, probs_ref, mixed_ref, table_ref,
-    tab_in, h_buf, a_buf, qkv_buf, far_buf, mix_buf, f_buf, lift_buf, slope_buf, w_buf, p_buf,
+    tab_in, h_buf, a_buf, qkv_buf, far_in, far_buf, mix_buf, f_buf, lift_buf, slope_buf, w_buf, p_buf,
     ts, tr, w_sem, save_sem, h_sem, p_sem, out_sem, ks, kr, *gather_sems,
 ):
     me = Place(outers)
@@ -274,8 +275,10 @@
     @pl.when(me.role == 0)
     def _():
         far_buf[...] = jnp.zeros_like(far_buf)
-
-    loop(6, gather.step)
+        far_in[...] = jnp.zeros_like(far_in)
+
+    ahead = gather.lag - 4
+    loop(2, gather.step)
     loop(devices - 1, lambda i: piece_wait(i + 1))
     loop(devices - 1, lambda i: piece_copy(i + 1).wait_send())
     per = 128 * devices // width
@@ -292,14 +295,14 @@
     loop(rows_all // 64, load_rows)
 
     def load(k):
-        return pltpu.make_async_copy(full_ref.at[k], w_buf.at[k % 2], w_sem.at[k % 2])
+        return pltpu.make_async_copy(full_ref.at[k], w_buf.at[lax.rem(k, 2)], w_sem.at[lax.rem(k, 2)])
 
     def matmul(in_ref, k, finish):
         load(k).wait()
 
         def columns(n):
             cols = tile(n, WIDE)
-            w = w_buf[k % 2, :, :, :, :, cols].reshape(width, WIDE)
+            w = w_buf[lax.rem(k, 2), :, :, :, :, cols].reshape(width, WIDE)
             finish(cols, dot(in_ref[...], w))
 
         loop(width // WIDE, columns)
@@ -314,57 +317,84 @@
 
         loop(rows_all // 64, some)
 
+    def save_at(l, ref, slot):
+        return pltpu.make_async_copy(ref, saved_ref.at[l, slot], save_sem.at[slot])
+
+    def save_hidden_at(l, which):
+        return pltpu.make_async_copy(h_buf.at[which], hidden_ref.at[l, which], h_sem.at[which])
+
+    def far_copy(l):
+        return remote(a_buf, far_in.at[l], ks.at[l], kr.at[l], me.other_role())
+
+    def begin(l):
+        save_hidden_at(l, 0).start()
+        norm(0, 0, a_buf, l)
+        save_at(l, a_buf, 0).start()
+
+        @pl.when(me.role == 0)
+        def _():
+            far_copy(l).start()
+
+    begin(0)
+    loop(gather.lag, lambda i: gather.step(i + 2))
+
     def layer(l):
         base = l * per_layer
 
         def save(ref, slot):
-            return pltpu.make_async_copy(ref, saved_ref.at[l, slot], save_sem.at[slot])
+            return save_at(l, ref, slot)
 
         def save_hidden(which):
-            return pltpu.make_async_copy(h_buf.at[which], hidden_ref.at[l, which], h_sem.at[which])
+            return save_hidden_at(l, which)
 
         load(base).start()
-        save_hidden(0).start()
-        norm(0, 0, a_buf, l)
-        save(a_buf, 0).start()
 
         def project(i):
             def keep(cols, value):
                 qkv_buf[i, :, cols] = value.astype(BF16)
 
             matmul(a_buf, base + i, keep)
-            gather.step(2 * (base + i) + 6)
-            gather.step(2 * (base + i) + 7)
-            load(base + i + 1).start()
+            gather.step(2 * (base + i) + 6 + ahead)
+            gather.step(2 * (base + i) + 7 + ahead)
+
+            @pl.when(i < 2)
+            def _():
+                load(base + i + 1).start()
+
             save(qkv_buf.at[i], 1 + i).start()
 
         loop(3, project)
 
-        def far_copy():
-            return remote(qkv_buf.at[pl.ds(1, 2)], far_buf.at[l], ks.at[l], kr.at[l], me.other_role())
-
-        @pl.when(me.role == 0)
-        def _():
-            far_copy().start()
-
         @pl.when(me.role == 1)
         def _():
-            far_copy().wait_recv()
-
-        save(far_buf.at[l, 0], 4).start()
-        save(far_buf.at[l, 1], 5).start()
+            load(base + 1).start()
+            load(base + 2).start()
+            far_copy(l).wait_recv()
+
+            def project_far(i):
+                def keep(cols, value):
+                    far_buf[i, :, cols] = value.astype(BF16)
+
+                matmul(far_in.at[l], base + 1 + i, keep)
+
+            loop(2, project_far)
+
+        load(base + 3).start()
+        save(far_in.at[l], 8 + 2 * pieces).start()
+        save(far_buf.at[0], 4).start()
+        save(far_buf.at[1], 5).start()
 
         def save_probs(it):
-            return pltpu.make_async_copy(p_buf.at[it % 2], probs_ref.at[l, it], p_sem.at[it % 2])
+            return pltpu.make_async_copy(p_buf.at[lax.rem(it, 2)], probs_ref.at[l, it], p_sem.at[lax.rem(it, 2)])
 
         def attend(it):
-            m, p = it // pairs, it % pairs
+            m, p = lax.div(it, pairs), lax.rem(it, pairs)
             r, cols = tile(m, rows), tile(p, 128)
             first = lax.broadcasted_iota(jnp.int32, (rows, 128), 1) < HD
             q = qkv_buf[0, r, cols].astype(F32) * HD**-0.5
             both = jnp.concatenate([jnp.where(first, q, 0.0).astype(BF16), jnp.where(first, 0.0, q).astype(BF16)], axis=0)
-            keys = jnp.concatenate([far_buf[l, 0, r, cols], qkv_buf[1, r, cols]], axis=0)
-            values = jnp.concatenate([far_buf[l, 1, r, cols], qkv_buf[2, r, cols]], axis=0)
+            keys = jnp.concatenate([far_buf[0, r, cols], qkv_buf[1, r, cols]], axis=0)
+            values = jnp.concatenate([far_buf[1, r, cols], qkv_buf[2, r, cols]], axis=0)
             bias = bias_ref[l, m].astype(F32)
             scores = dot_t(keys, both) + jnp.concatenate([bias, bias], axis=1)
             exponent = jnp.exp(scores - jnp.max(scores, axis=0, keepdims=True))
@@ -374,7 +404,7 @@
             def _():
                 save_probs(it - 2).wait()
 
-            p_buf[it % 2] = soft
+            p_buf[lax.rem(it, 2)] = soft
             save_probs(it).start()
             out = t_dot(values, soft)
             out = jnp.concatenate([out[:HD, :rows], out[HD:, rows:]], axis=0)
@@ -384,7 +414,7 @@
 
         def attend_some(s):
             loop(segment, lambda i: attend(s * segment + i))
-            gather.step(2 * base + 12 + s)
+            gather.step(2 * base + 12 + s + ahead)
 
         loop(4, attend_some)
         save_probs(micro * pairs - 2).wait()
@@ -411,12 +441,12 @@
                 slope_buf[:, cols] = slope.astype(BF16)
 
             matmul(f_buf, base + 4 + 2 * j, raise_columns)
-            lift_save = pltpu.make_async_copy(lift_buf, saved_ref.at[l, 8 + j], save_sem.at[8])
-            slope_save = pltpu.make_async_copy(slope_buf, saved_ref.at[l, 8 + pieces + j], save_sem.at[9])
+            lift_save = pltpu.make_async_copy(lift_buf, saved_ref.at[l, 8 + j], save_sem.at[9 + 2 * pieces])
+            slope_save = pltpu.make_async_copy(slope_buf, saved_ref.at[l, 8 + pieces + j], save_sem.at[8])
             lift_save.start()
             slope_save.start()
-            gather.step(2 * base + 16 + 4 * j)
-            gather.step(2 * base + 17 + 4 * j)
+            gather.step(2 * base + 16 + 4 * j + ahead)
+            gather.step(2 * base + 17 + 4 * j + ahead)
 
             @pl.when(j < pieces - 1)
             def _():
@@ -429,8 +459,8 @@
 
             @pl.when(j < pieces - 1)
             def _():
-                gather.step(2 * base + 18 + 4 * j)
-                gather.step(2 * base + 19 + 4 * j)
+                gather.step(2 * base + 18 + 4 * j + ahead)
+                gather.step(2 * base + 19 + 4 * j + ahead)
 
             lift_save.wait()
             slope_save.wait()
@@ -440,14 +470,19 @@
         save(a_buf, 0).wait()
         for i in range(3):
             save(qkv_buf.at[i], 1 + i).wait()
-        save(far_buf.at[l, 0], 4).wait()
-        save(far_buf.at[l, 1], 5).wait()
+        save(far_buf.at[0], 4).wait()
+        save(far_buf.at[1], 5).wait()
         save(mix_buf, 6).wait()
         save(f_buf, 7).wait()
+        save(far_in.at[l], 8 + 2 * pieces).wait()
 
         @pl.when(me.role == 0)
         def _():
-            far_copy().wait_send()
+            far_copy(l).wait_send()
+
+        @pl.when(l < layers - 1)
+        def _():
+            begin(l + 1)
 
     loop(layers, layer)
 
@@ -479,7 +514,7 @@
         functools.partial(forward_kernel, layers, outers, split),
         out_shape=(
             jax.ShapeDtypeStruct((count, outers, 2, 2, shard, width), BF16),
-            jax.ShapeDtypeStruct((layers, 8 + 2 * pieces) + grid_rows, BF16),
+            jax.ShapeDtypeStruct((layers, 9 + 2 * pieces) + grid_rows, BF16),
             jax.ShapeDtypeStruct((layers, 2) + grid_rows, F32),
             jax.ShapeDtypeStruct((layers, micro * pairs, keys, 2 * rows), BF16),
             jax.ShapeDtypeStruct(grid_rows, BF16),
@@ -492,7 +527,8 @@
             pltpu.VMEM((2,) + grid_rows, F32),
             pltpu.VMEM(grid_rows, BF16),
             pltpu.VMEM((3,) + grid_rows, BF16),
-            pltpu.VMEM((layers, 2) + grid_rows, BF16),
+            pltpu.VMEM((layers,) + grid_rows, BF16),
+            pltpu.VMEM((2,) + grid_rows, BF16),
             pltpu.VMEM(grid_rows, BF16),
             pltpu.VMEM(grid_rows, BF16),
             pltpu.VMEM(grid_rows, BF16),
@@ -500,7 +536,7 @@
             pltpu.VMEM((2, outers, 2, 2, shard, width), BF16),
             pltpu.VMEM((2, keys, 2 * rows), BF16),
             dma((devices - 1,)), dma((devices - 1,)),
-            dma((2,)), dma((10,)), dma((2,)), dma((2,)), dma(()), dma((layers,)), dma((layers,)),
+            dma((2,)), dma((10 + 2 * pieces,)), dma((2,)), dma((2,)), dma(()), dma((layers,)), dma((layers,)),
         ]
         + Gather.semaphores(many),
         compiler_params=pltpu.CompilerParams(
@@ -511,7 +547,7 @@
 
 
 class Reduce:
-    lag = 5
+    lag = 8
 
     def __init__(self, me, grad_ref, out_ref, split, refs):
         self.me, self.grad, self.out, self.split = me, grad_ref, out_ref, split
@@ -520,33 +556,34 @@
             self.end_buf, self.fin_buf,
             self.own_sem, self.cs, self.cr, self.ys, self.yr, self.xs, self.xr, self.zs, self.zr, self.es, self.er, self.fs,
         ) = refs
-        self.width = grad_ref.shape[-1]
-        self.main = self.width - split
-        self.steps = grad_ref.shape[0]
+        self.half = grad_ref.shape[-1] // 2
+        self.main = self.half - split
+        self.steps = 2 * grad_ref.shape[0]
 
     @staticmethod
     def scratch(outers, rows, width, split):
         dma = pltpu.SemaphoreType.DMA
         many = outers - 1
-        main = width - split
+        half = width // 2
+        main = half - split
         return [
-            pltpu.VMEM((2, outers, 2, rows, width), BF16),
-            pltpu.VMEM((SLOTS, outers, 2, rows, width), BF16),
-            pltpu.VMEM((SLOTS, outers, 2, rows, split), BF16),
-            pltpu.VMEM((SLOTS, outers, rows, main), BF16),
-            pltpu.VMEM((SLOTS, many, rows, main), BF16),
-            pltpu.VMEM((SLOTS, rows, main), BF16),
-            pltpu.VMEM((SLOTS, outers, 2, rows, width), BF16),
-            pltpu.VMEM((SLOTS, outers, rows, main), BF16),
-            pltpu.VMEM((SLOTS, rows, main), BF16),
-            pltpu.VMEM((SLOTS, rows, width), F32),
+            pltpu.VMEM((2, outers, 2, rows, half), BF16),
+            pltpu.VMEM((4, outers, 2, rows, half), BF16),
+            pltpu.VMEM((6, outers, 2, rows, split), BF16),
+            pltpu.VMEM((6, outers, rows, main), BF16),
+            pltpu.VMEM((6, many, rows, main), BF16),
+            pltpu.VMEM((4, rows, main), BF16),
+            pltpu.VMEM((6, outers, 2, rows, half), BF16),
+            pltpu.VMEM((4, outers, rows, main), BF16),
+            pltpu.VMEM((4, rows, main), BF16),
+            pltpu.VMEM((4, rows, half), F32),
             dma((2,)),
-            dma((SLOTS,)), dma((SLOTS,)),
-            dma((SLOTS,)), dma((SLOTS,)),
-            dma((SLOTS,)), dma((SLOTS,)),
-            dma((SLOTS, many)), dma((SLOTS, many)),
-            dma((SLOTS,)), dma((SLOTS,)),
-            dma((SLOTS,)),
+            dma((4,)), dma((4,)),
+            dma((6,)), dma((6,)),
+            dma((6,)), dma((6,)),
+            dma((6, many)), dma((6, many)),
+            dma((4,)), dma((4,)),
+            dma((4,)),
         ]
 
     def cols(self, offset, size):
@@ -561,42 +598,46 @@
     def give_cols(self):
         return self.cols((1 - self.me.role) * self.main, self.split)
 
+    def part(self, k, core):
+        return self.grad.at[lax.div(k, 2), :, :, core, :, self.cols(lax.rem(k, 2) * self.half, self.half)]
+
     def own(self, k):
         s = lax.rem(k, 2)
-        return pltpu.make_async_copy(self.grad.at[k, :, :, self.me.core], self.own_buf.at[s], self.own_sem.at[s])
+        return pltpu.make_async_copy(self.part(k, self.me.core), self.own_buf.at[s], self.own_sem.at[s])
 
     def c_copy(self, k):
-        s = lax.rem(k, SLOTS)
-        return remote(self.grad.at[k, :, :, 1 - self.me.core], self.core_buf.at[s], self.cs.at[s], self.cr.at[s], self.me.sibling())
+        s = lax.rem(k, 4)
+        return remote(self.part(k, 1 - self.me.core), self.core_buf.at[s], self.cs.at[s], self.cr.at[s], self.me.sibling())
 
     def y_copy(self, k):
-        s = lax.rem(k, SLOTS)
+        s = lax.rem(k, 6)
         return remote(
             self.sum_buf.at[s, :, :, :, self.give_cols()], self.role_buf.at[s], self.ys.at[s], self.yr.at[s], self.me.other_role()
         )
 
     def x_copy(self, k):
-        s = lax.rem(k, SLOTS)
+        s = lax.rem(k, 6)
         return remote(
             self.sum_buf.at[s, :, 1 - self.me.pair, :, self.main_cols()],
             self.pair_buf.at[s], self.xs.at[s], self.xr.at[s], self.me.across(),
         )
 
     def z_copy(self, k, by):
-        s = lax.rem(k, SLOTS)
+        s = lax.rem(k, 6)
         me = self.me
         return remote(
-            self.low_buf.at[s, lax.rem(me.outer + by, me.outers)], self.outer_buf.at[s, by - 1],
+            self.low_buf.at[lax.rem(k, 4), lax.rem(me.outer + by, me.outers)], self.outer_buf.at[s, by - 1],
             self.zs.at[s, by - 1], self.zr.at[s, by - 1], me.along(by),
         )
 
     def e_copy(self, k):
-        s = lax.rem(k, SLOTS)
+        s = lax.rem(k, 4)
         return remote(self.end_buf.at[s], self.last_buf.at[s], self.es.at[s], self.er.at[s], self.me.other_role())
 
     def f_copy(self, k):
-        s = lax.rem(k, SLOTS)
-        return pltpu.make_async_copy(self.fin_buf.at[s], self.out.at[k], self.fs.at[s])
+        s = lax.rem(k, 4)
+        cols = self.cols(lax.rem(k, 2) * self.half, self.half)
+        return pltpu.make_async_copy(self.fin_buf.at[s], self.out.at[lax.div(k, 2), :, cols], self.fs.at[s])
 
     def step(self, t):
         me, count, split, main = self.me, self.steps, self.split, self.main
@@ -610,21 +651,20 @@
         @pl.when((t >= 1) & (t < count + 1))
         def _():
             k = t - 1
-            s = lax.rem(k, SLOTS)
             self.own(k).wait()
             self.c_copy(k).wait()
 
             def add(i):
                 o, p = lax.div(i, 2), lax.rem(i, 2)
-                self.sum_buf[s, o, p] = self.own_buf[lax.rem(k, 2), o, p] + self.core_buf[s, o, p]
+                self.sum_buf[lax.rem(k, 6), o, p] = self.own_buf[lax.rem(k, 2), o, p] + self.core_buf[lax.rem(k, 4), o, p]
 
             loop(2 * me.outers, add)
             self.y_copy(k).start()
 
-        @pl.when((t >= 2) & (t < count + 2))
-        def _():
-            k = t - 2
-            s = lax.rem(k, SLOTS)
+        @pl.when((t >= 3) & (t < count + 3))
+        def _():
+            k = t - 3
+            s = lax.rem(k, 6)
             self.y_copy(k).wait()
             keep = self.keep_cols()
 
@@ -635,41 +675,40 @@
             loop(2 * me.outers, add)
             self.x_copy(k).start()
 
-        @pl.when((t >= 3) & (t < count + 3))
-        def _():
-            k = t - 3
-            s = lax.rem(k, SLOTS)
+        @pl.when((t >= 5) & (t < count + 5))
+        def _():
+            k = t - 5
+            s = lax.rem(k, 6)
             self.x_copy(k).wait()
             cols = self.main_cols()
 
             def add(o):
-                self.low_buf[s, o] = self.sum_buf[s, o, me.pair, :, cols] + self.pair_buf[s, o]
+                self.low_buf[lax.rem(k, 4), o] = self.sum_buf[s, o, me.pair, :, cols] + self.pair_buf[s, o]
 
             loop(me.outers, add)
             for by in others:
                 self.z_copy(k, by).start()
 
-        @pl.when((t >= 4) & (t < count + 4))
-        def _():
-            k = t - 4
-            s = lax.rem(k, SLOTS)
+        @pl.when((t >= 7) & (t < count + 7))
+        def _():
+            k = t - 7
             for by in others:
                 self.z_copy(k, by).wait()
-            total = self.low_buf[s, me.outer].astype(F32)
+            total = self.low_buf[lax.rem(k, 4), me.outer].astype(F32)
             for by in others:
-                total = total + self.outer_buf[s, by - 1].astype(F32)
-            self.end_buf[s] = total.astype(BF16)
+                total = total + self.outer_buf[lax.rem(k, 6), by - 1].astype(F32)
+            self.end_buf[lax.rem(k, 4)] = total.astype(BF16)
             self.e_copy(k).start()
 
-        @pl.when((t >= 5) & (t < count + 5))
-        def _():
-            k = t - 5
-            s = lax.rem(k, SLOTS)
+        @pl.when((t >= 8) & (t < count + 8))
+        def _():
+            k = t - 8
+            s = lax.rem(k, 4)
             self.e_copy(k).wait()
 
-            @pl.when(k >= SLOTS)
+            @pl.when(k >= 4)
             def _():
-                self.f_copy(k - SLOTS).wait()
+                self.f_copy(k - 4).wait()
 
             mid = main - split
             mine = self.end_buf[s].astype(F32)
@@ -690,7 +729,7 @@
             self.f_copy(k).start()
 
     def finish(self):
-        for k in range(self.steps - SLOTS, self.steps):
+        for k in range(self.steps - 4, self.steps):
             self.f_copy(k).wait()
 
 
@@ -735,12 +774,15 @@
         s = lax.rem(n, 2)
         return pltpu.make_async_copy(stage_buf.at[s], grad_ref.at[n], stage_sem.at[s])
 
-    def produce(n, left, right):
+    def produce(n, left, right, far=None):
         s = lax.rem(n, 2)
 
         def some(i):
-            value = t_dot(left[:, tile(i, WIDE)], right[...]).astype(BF16)
-            stage_buf[s, pl.ds(i * tile_outers, tile_outers)] = value.reshape(tile_outers, 2, 2, shard, width)
+            cols = tile(i, WIDE)
+            value = t_dot(left[:, cols], right[...])
+            if far is not None:
+                value = value + t_dot(far[0][:, cols], far[1][...])
+            stage_buf[s, pl.ds(i * tile_outers, tile_outers)] = value.astype(BF16).reshape(tile_outers, 2, 2, shard, width)
 
         loop(width // WIDE, some)
         send_stage(n).start()
@@ -784,7 +826,7 @@
         n0 = turn * per_layer
 
         def service(index):
-            reduce.step(n0 + index - 1)
+            reduce.step(2 * (n0 - 1) + index)
 
         get(l, 7, 0).start()
         get(l, 8, 1).start()
@@ -807,6 +849,7 @@
                 get(l, 9 + pieces + j, 4 - s).start()
 
             produce(n0 + 2 * j, act_buf.at[1 + s], low_buf)
+            service(2 * j)
             get_w(base + 5 + 2 * j, 0).wait()
 
             def lift(cols, value):
@@ -818,7 +861,7 @@
             def _():
                 get_w(base + 7 + 2 * j, 0).start()
 
-            service(j)
+            service(2 * j + 1)
             produce(n0 + 2 * j + 1, act_buf.at[0], act_buf.at[5])
             get_w(base + 4 + 2 * j, 1).wait()
 
@@ -832,6 +875,7 @@
         get(l, 6, 0).start()
         for i in range(5):
             get(l, 1 + i, 1 + i).start()
+        get(l, 8 + 2 * pieces, 9).start()
 
         def get_probs(it):
             s = lax.rem(it, 2)
@@ -839,10 +883,11 @@
 
         get_probs(0).start()
         get_hidden(l, 1).wait()
+        service(2 * pieces)
         norm_back(1, l)
         lower(low_buf, g_buf)
-        service(pieces)
         get(l, 6, 0).wait()
+        service(2 * pieces + 1)
         produce(n0 + 2 * pieces, act_buf.at[0], low_buf)
         get_w(base + 3, 0).wait()
 
@@ -850,7 +895,7 @@
             act_buf[6, :, cols] = value.astype(BF16)
 
         through(low_buf, 0, keep_mixture)
-        get_w(base, 0).start()
+        get_w(base + 1, 0).start()
         get(l, 0, 8).start()
         for i in range(5):
             get(l, 1 + i, 1 + i).wait()
@@ -888,20 +933,73 @@
             out = jnp.concatenate([out[:HD, :rows], out[HD:, rows:]], axis=0)
             act_buf[7, r, cols] = out.T.astype(BF16)
 
-        segment = micro * pairs // 4
+        segment = micro * pairs // 8
 
         def attend_some(s):
             loop(segment, lambda i: attend(s * segment + i))
-            service(pieces + 1 + s)
-
-        loop(4, attend_some)
+            service(2 * pieces + 2 + s)
+
+        loop(8, attend_some)
+
+        def some_rows(i):
+            r = tile(i, block)
+            act_buf[1, r, :] = h_buf[r, :].astype(BF16)
+            act_buf[2, r, :] = acc_buf[r, :].astype(BF16)
+
+        loop(rows_all // block, some_rows)
+        acc_buf[...] = jnp.zeros_like(acc_buf)
+        get(l, 0, 8).wait()
+        get(l, 8 + 2 * pieces, 9).wait()
 
         def back_copy():
-            return remote(give_buf, back_buf.at[l], ks.at[l], kr.at[l], me.other_role())
-
-        @pl.when(me.role == 1)
-        def _():
-            back_copy().start()
+            return remote(low_buf, back_buf.at[l], ks.at[l], kr.at[l], me.other_role())
+
+        def add(cols, value):
+            acc_buf[:, cols] += value
+
+        def project(i):
+            get_w(base + lax.rem(2 + i, 3), 1 - i).start()
+            part = act_buf.at[1 + i]
+            n = n0 + 2 * pieces + 1 + i
+
+            @pl.when(me.role == 0)
+            def _():
+                produce(n, act_buf.at[8], part)
+
+            @pl.when(me.role == 1)
+            def _():
+                produce(n, act_buf.at[8], part, (act_buf.at[9], give_buf.at[i]))
+
+            service(2 * pieces + 10 + 2 * i)
+            get_w(base + 1 + i, i).wait()
+            through(part, i, add)
+
+            @pl.when(me.role == 1)
+            def _():
+                def first(cols, value):
+                    h_buf[:, cols] = value
+
+                def second(cols, value):
+                    low_buf[:, cols] = (h_buf[:, cols] + value).astype(BF16)
+
+                @pl.when(i == 0)
+                def _():
+                    through(give_buf.at[0], 0, first)
+
+                @pl.when(i == 1)
+                def _():
+                    through(give_buf.at[1], 1, second)
+                    back_copy().start()
+
+            service(2 * pieces + 11 + 2 * i)
+
+        loop(2, project)
+        get_hidden(l, 0).start()
+        produce(n0 + 2 * pieces + 3, act_buf.at[8], act_buf.at[7])
+        service(2 * pieces + 14)
+        get_w(base, 0).wait()
+        through(act_buf.at[7], 0, add)
+        service(2 * pieces + 15)
 
         @pl.when(me.role == 0)
         def _():
@@ -909,42 +1007,10 @@
 
             def some(i):
                 r = tile(i, block)
-                act_buf[1, r, :] = (h_buf[r, :] + back_buf[l, 0, r, :].astype(F32)).astype(BF16)
-                act_buf[2, r, :] = (acc_buf[r, :] + back_buf[l, 1, r, :].astype(F32)).astype(BF16)
+                acc_buf[r, :] += back_buf[l, r, :].astype(F32)
 
             loop(rows_all // block, some)
 
-        @pl.when(me.role == 1)
-        def _():
-            def some(i):
-                r = tile(i, block)
-                act_buf[1, r, :] = h_buf[r, :].astype(BF16)
-                act_buf[2, r, :] = acc_buf[r, :].astype(BF16)
-
-            loop(rows_all // block, some)
-
-        get_hidden(l, 0).start()
-        acc_buf[...] = jnp.zeros_like(acc_buf)
-        get(l, 0, 8).wait()
-
-        def project(i):
-            s = lax.rem(i, 2)
-
-            @pl.when(i < 2)
-            def _():
-                get_w(base + 1 + i, 1 - s).start()
-
-            part = act_buf.at[jnp.where(i == 0, 7, i)]
-            produce(n0 + 2 * pieces + 1 + i, act_buf.at[8], part)
-            get_w(base + i, s).wait()
-
-            def add(cols, value):
-                acc_buf[:, cols] += value
-
-            through(part, s, add)
-            service(pieces + 5 + i)
-
-        loop(3, project)
         get_hidden(l, 0).wait()
         norm_back(0, l)
 
@@ -973,7 +1039,7 @@
     tab_in[me.dp] = tab_role[lax.div(me.dp, per)]
     last = layers * per_layer - 1
     send_stage(last).wait()
-    loop(2, lambda i: reduce.step(last + i))
+    loop(4, lambda i: reduce.step(2 * last + i))
     loop(devices - 1, lambda i: tab_wait(i + 1))
     loop(devices - 1, lambda i: tab_copy(i + 1).wait_send())
     total = tab_in[0]
@@ -982,7 +1048,7 @@
     tab_back[0] = total
     swap = remote(tab_back.at[0], tab_back.at[1], rs_sem, rr_sem, me.other_role())
     swap.start()
-    loop(reduce.lag - 1, lambda i: reduce.step(last + 2 + i))
+    loop(reduce.lag - 2, lambda i: reduce.step(2 * last + 4 + i))
     swap.wait()
     table_out_ref[...] = tab_back[0] + tab_back[1]
     reduce.finish()
@@ -996,7 +1062,7 @@
     small = table.shape[0]
     dma = pltpu.SemaphoreType.DMA
     devices = 4 * outers
-    split = width // 4
+    split = width // 8
     any_space = pl.BlockSpec(memory_space=pl.ANY)
     vmem = pl.BlockSpec(memory_space=pltpu.VMEM)
     grid_rows = (rows_all, width)
@@ -1016,16 +1082,16 @@
             pltpu.VMEM(grid_rows, F32),
             pltpu.VMEM((2, width, width), BF16),
             pltpu.VMEM(grid_rows, BF16),
-            pltpu.VMEM((9,) + grid_rows, BF16),
+            pltpu.VMEM((10,) + grid_rows, BF16),
             pltpu.VMEM((2,) + grid_rows, BF16),
-            pltpu.VMEM((layers, 2) + grid_rows, BF16),
+            pltpu.VMEM((layers,) + grid_rows, BF16),
             pltpu.VMEM((2, keys, keys), BF16),
             pltpu.VMEM((2, outers, 2, 2, shard, width), BF16),
             pltpu.VMEM((small, width), F32),
             pltpu.VMEM((devices, small, 128), F32),
             pltpu.VMEM((width // 128, small, 128), F32),
             pltpu.VMEM((2, small, 128), F32),
-            dma((9,)), dma(()), dma((2,)), dma((2,)), dma((2,)), dma((layers,)), dma((layers,)),
+            dma((10,)), dma(()), dma((2,)), dma((2,)), dma((2,)), dma((layers,)), dma((layers,)),
             dma((devices - 1,)), dma((devices - 1,)), dma(()), dma(()), dma(()),
         ]
         + Reduce.scratch(outers, shard, width, split),
@@ -1111,7 +1177,7 @@
     )
     owned = owned.reshape(layers, -1, shard, width)[::-1]
     feed = owned[:, : 2 * pieces].reshape(layers, pieces, 2, shard, width)
-    inner_grad = owned[:, 2 * pieces + 1 :].transpose(0, 2, 1, 3).reshape(layers, shard, 3 * width)
+    inner_grad = jnp.concatenate([owned[:, 2 * pieces + i] for i in (3, 1, 2)], axis=2)
     outer_grad = owned[:, 2 * pieces]
     expand_grad = feed[:, :, 1].reshape(layers, pieces, shard, devices, shard).transpose(0, 2, 3, 1, 4).reshape(layers, shard, -1)
     shrink_grad = feed[:, :, 0].reshape(layers, pieces * shard, width)

time: 796 us -> 640 us (0.80)
  Pallas kernels: 739 us -> 583 us
    pallas_call x1, Pallas kernels: 380 us -> 271 us  [forward(): pl.pallas_call(functools.partial(forward_kernel, layers, outers, split),...]
    pallas_call x1, Pallas kernels: 358 us -> 312 us  [backward(): pl.pallas_call(functools.partial(backward_kernel, layers, outers, split),...]
where the time goes in v3:
time: 640 us; the launch traced here: 639 us
  Pallas kernels  583 us (91%)
  local copies, waits for them, and re-layouts  45.6 us (7%)
  other arithmetic  9.41 us (1%)
    pallas_call x1, Pallas kernels, backward(): pl.pallas_call(functools.partial(backward_kernel, layers, outers, split),...  312 us
    pallas_call x1, Pallas kernels, forward(): pl.pallas_call(functools.partial(forward_kernel, layers, outers, split),...  271 us

profile of v3, /device:TPU:0, one launch (start us, length us, event | category | flops | bytes accessed | tf_op | source)
XLA Modules:
  0.0 638.9 jit_solution(14990684745863743631)
XLA Ops:
  0.6 5.0 reshape.268
  5.6 1.9 copy.47
  7.5 1.5 reshape.269
  9.0 1.4 pad_maximum_fusion.1
  10.4 0.2 copy.48
  10.6 2.8 reshape.267
  13.4 0.3 copy.49
  13.8 1.9 pad_maximum_fusion
  15.8 0.2 dynamic_update_slice.3.piece_ref
  16.0 0.1 select_reduce_fusion.6
  16.9 1.5 fusion.pick_ref
  18.4 0.2 compare_and_fusion
  18.7 0.2 compare_and_fusion.2
  19.0 1.2 select_convert_fusion.bias_ref
  20.3 270.8 %gather_and_forward.1 = (bf16[24,4,2,2,64,1024]{5,4,3,2,1,0:T(8,128)(2,1)}, bf16[2,17,512,1024]{3,2,1,0:T(8,128)(2,1)}, f32[2,2,512,1024]{3,2,1,0:T(8,128)}, bf1...) custom-call(bf16[24,64,1024]{2,1,0:T(8,128)(2,1)} %bitcast.74, ...), custom_call_target="tpu_custom_call" | custom-call | tf_op jit(solution)/shard_map/gather_and_forward/pallas_call | solution.py:513
  291.0 0.8 fusion.1.used_ref
  291.8 312.1 %backward_and_reduce.1 = (bf16[24,4,2,2,64,1024]{5,4,3,2,1,0:T(8,128)(2,1)}, f32[24,64,1024]{2,1,0:T(8,128)}, bf16[512,1024]{1,0:T(8,128)(2,1)}, f32[32,128]{1,0:T(8,128)}) custom-call(bf16[24,1024,1024]{2,1,0:T(8,128)(2,1)} %bitcast.71, bf16[2,17,512,1024]{3,2,1,0:T(8,128)(2,1)} %get-tuple-element.21.saved_ref, ...), custom_call_target="tpu_custom_call" | custom-call | tf_op jit(solution)/shard_map/backward_and_reduce/pallas_call | solution.py:1069
  603.9 1.7 fusion.8
  605.7 1.3 pad_maximum_fusion.2
  607.0 0.8 reverse_bitcast_fusion
  607.8 1.4 copy-done
  609.1 2.2 slice.92
  611.4 4.7 slice.81
  616.1 4.0 fusion.9
  620.1 2.5 reshape_squeeze.6
  622.6 6.9 %copy.53 = f32[2,64,16,4,64]{4,3,2,1,0:T(4,128)} copy(f32[2,64,16,4,64]{4,2,1,3,0:T(8,128)} %bitcast.73) | data formatting | bytes 4194304 | tf_op jit(solution)/shard_map/transpose | solution.py:1182
  629.5 5.6 reshape.282
  635.0 0.6 fusion.11
  635.7 0.6 reshape.283
  636.3 0.6 reshape.284
  637.0 1.0 copy.59
  637.9 1.0 copy.60
  (59 shorter events, 1.2 us)
Async XLA Ops:
  10.6 3.1 copy-start.3
  13.7 2.0 copy-start.8
  13.7 2.0 copy-start.9
  13.7 2.0 copy-start.11
  13.7 2.0 copy-start.12
  13.7 2.2 copy-start.6
  13.7 2.4 copy-start.7
  13.8 2.6 copy-start.10
  15.9 4.3 copy-start.4
  605.6 3.5 copy-start
  629.5 5.6 copy-start.5
  629.5 7.5 %copy-start.1 = (bf16[512,1024]{1,0:T(8,128)(2,1)S(1)}, bf16[512,1024]{1,0:T(8,128)(2,1)}, u32[]{:S(2)}) copy-start(bf16[512,1024]{1,0:T(8,128)(2,1)} %get-tuple-element.19) | copy-start | bytes 3145732
  635.0 2.9 copy-start.2

commit v4 on v3

--- a/solution.py
+++ b/solution.py
@@ -241,25 +241,37 @@
     return pl.ds(pl.multiple_of(i * size, size), size)
 
 
-WIDE = 256
+WIDE = 1024
 
 
 def forward_kernel(
     layers, outers, split,
-    part_ref, frames_ref, piece_ref, pick_ref, bias_ref,
+    inner_ref, outer_ref, expand_ref, shrink_ref, frames_ref, piece_ref, pick_ref, bias_ref,
     full_ref, saved_ref, hidden_ref, probs_ref, mixed_ref, table_ref,
-    tab_in, h_buf, a_buf, qkv_buf, far_in, far_buf, mix_buf, f_buf, lift_buf, slope_buf, w_buf, p_buf,
-    ts, tr, w_sem, save_sem, h_sem, p_sem, out_sem, ks, kr, *gather_sems,
+    part_buf, e_buf, tab_in, h_buf, a_buf, qkv_buf, far_in, far_buf, mix_buf, f_buf, lift_buf, slope_buf, w_buf, p_buf,
+    pack_sem, ts, tr, w_sem, save_sem, h_sem, p_sem, out_sem, ks, kr, *gather_sems,
 ):
     me = Place(outers)
     devices = 4 * outers
     rows_all, width = frames_ref.shape
-    per_layer = part_ref.shape[0] // layers
+    count, shard, _ = part_buf.shape
+    per_layer = count // layers
     pieces = (per_layer - 4) // 2
     micro = bias_ref.shape[1]
     rows = rows_all // micro
     pairs = width // 128
-    gather = Gather(me, part_ref, full_ref, split, gather_sems)
+    gather = Gather(me, part_buf, full_ref, split, gather_sems)
+    early, late = [], []
+    for l in range(layers):
+        base = l * per_layer
+        sources = [(i, inner_ref.at[l, :, pl.ds(i * width, width)]) for i in range(3)] + [(3, outer_ref.at[l])]
+        sources += [(5 + 2 * j, shrink_ref.at[l, pl.ds(j * shard, shard)]) for j in range(pieces)]
+        for k, source in sources:
+            copy = pltpu.make_async_copy(source, part_buf.at[base + k], pack_sem.at[base + k])
+            (early if base + k < 4 else late).append(copy)
+        late.append(pltpu.make_async_copy(expand_ref.at[l], e_buf.at[l], pack_sem.at[count + l]))
+    for copy in early + late:
+        copy.start()
     me.greet()
 
     def piece_copy(by):
@@ -278,7 +290,29 @@
         far_in[...] = jnp.zeros_like(far_in)
 
     ahead = gather.lag - 4
+    for copy in early:
+        copy.wait()
     loop(2, gather.step)
+    for copy in late:
+        copy.wait()
+
+    def spread(index):
+        l, t = lax.div(index, width // 128), lax.rem(index, width // 128)
+        first = lax.broadcasted_iota(jnp.int32, (shard, 128), 1) < 64
+        for j in range(pieces):
+            to = part_buf.at[l * per_layer + 4 + 2 * j, :, tile(t, 128)]
+            if shard == 64:
+                even = e_buf[l, :, tile(t * pieces + j // 2, 128)].astype(F32)
+                odd = e_buf[l, :, tile(t * pieces + pieces // 2 + j // 2, 128)].astype(F32)
+                if j % 2 == 0:
+                    odd = pltpu.roll(odd, 64, 1)
+                else:
+                    even = pltpu.roll(even, 64, 1)
+                to[...] = jnp.where(first, even, odd).astype(BF16)
+            else:
+                to[...] = e_buf[l, :, tile(j * (width // 128) + t, 128)]
+
+    loop(layers * width // 128, spread)
     loop(devices - 1, lambda i: piece_wait(i + 1))
     loop(devices - 1, lambda i: piece_copy(i + 1).wait_send())
     per = 128 * devices // width
@@ -421,6 +455,7 @@
         save_probs(micro * pairs - 1).wait()
         save(mix_buf, 6).start()
         load(base + 4).start()
+        gather.step(2 * base + 16 + ahead)
 
         def keep_middle(cols, value):
             h_buf[1, :, cols] = h_buf[0, :, cols] + value
@@ -428,11 +463,13 @@
         matmul(mix_buf, base + 3, keep_middle)
         save_hidden(1).start()
         save_hidden(0).wait()
+        gather.step(2 * base + 17 + ahead)
         norm(1, 1, f_buf, l)
         save(f_buf, 7).start()
         h_buf[0] = h_buf[1]
 
         def feed(j):
+            gather.step(2 * base + 18 + 3 * j + ahead)
             load(base + 5 + 2 * j).start()
 
             def raise_columns(cols, value):
@@ -445,8 +482,7 @@
             slope_save = pltpu.make_async_copy(slope_buf, saved_ref.at[l, 8 + pieces + j], save_sem.at[8])
             lift_save.start()
             slope_save.start()
-            gather.step(2 * base + 16 + 4 * j + ahead)
-            gather.step(2 * base + 17 + 4 * j + ahead)
+            gather.step(2 * base + 19 + 3 * j + ahead)
 
             @pl.when(j < pieces - 1)
             def _():
@@ -456,12 +492,7 @@
                 h_buf[0, :, cols] += value
 
             matmul(lift_buf, base + 5 + 2 * j, add)
-
-            @pl.when(j < pieces - 1)
-            def _():
-                gather.step(2 * base + 18 + 4 * j + ahead)
-                gather.step(2 * base + 19 + 4 * j + ahead)
-
+            gather.step(2 * base + 20 + 3 * j + ahead)
             lift_save.wait()
             slope_save.wait()
 
@@ -496,10 +527,11 @@
     done.wait()
 
 
-def forward(parts, frames, piece, pick, bias, outers, layers, collective_id):
-    count, shard, width = parts.shape
+def forward(inner, outer, expand, shrink, frames, piece, pick, bias, outers, collective_id):
+    layers, shard, width = outer.shape
     rows_all = frames.shape[0]
-    pieces = (count // layers - 4) // 2
+    pieces = expand.shape[2] // width
+    count = layers * (4 + 2 * pieces)
     many = outers - 1
     dma = pltpu.SemaphoreType.DMA
     devices = 4 * outers
@@ -520,9 +552,11 @@
             jax.ShapeDtypeStruct(grid_rows, BF16),
             jax.ShapeDtypeStruct((piece.shape[0], width), BF16),
         ),
-        in_specs=[any_space, vmem, vmem, vmem, vmem],
+        in_specs=[any_space, any_space, any_space, any_space, vmem, vmem, vmem, vmem],
         out_specs=(any_space, any_space, any_space, any_space, any_space, vmem),
         scratch_shapes=[
+            pltpu.VMEM((count, shard, width), BF16),
+            pltpu.VMEM(expand.shape, BF16),
             pltpu.VMEM((devices,) + piece.shape, BF16),
             pltpu.VMEM((2,) + grid_rows, F32),
             pltpu.VMEM(grid_rows, BF16),
@@ -535,7 +569,7 @@
             pltpu.VMEM(grid_rows, BF16),
             pltpu.VMEM((2, outers, 2, 2, shard, width), BF16),
             pltpu.VMEM((2, keys, 2 * rows), BF16),
-            dma((devices - 1,)), dma((devices - 1,)),
+            dma((count + layers,)), dma((devices - 1,)), dma((devices - 1,)),
             dma((2,)), dma((10 + 2 * pieces,)), dma((2,)), dma((2,)), dma(()), dma((layers,)), dma((layers,)),
         ]
         + Gather.semaphores(many),
@@ -543,25 +577,30 @@
             collective_id=collective_id, has_side_effects=True, vmem_limit_bytes=58 * 2**20
         ),
         name="gather_and_forward",
-    )(parts, frames, piece, pick, bias)
+    )(inner, outer, expand, shrink, frames, piece, pick, bias)
 
 
 class Reduce:
     lag = 8
 
-    def __init__(self, me, grad_ref, out_ref, split, refs):
-        self.me, self.grad, self.out, self.split = me, grad_ref, out_ref, split
+    def __init__(self, me, layers, grad_ref, out_refs, split, refs):
+        self.me, self.grad, self.split = me, grad_ref, split
+        self.inner, self.outer, self.expand, self.shrink = out_refs
         (
             self.own_buf, self.core_buf, self.role_buf, self.pair_buf, self.outer_buf, self.last_buf, self.sum_buf, self.low_buf,
-            self.end_buf, self.fin_buf,
+            self.end_buf, self.fin_buf, self.spread_buf,
             self.own_sem, self.cs, self.cr, self.ys, self.yr, self.xs, self.xr, self.zs, self.zr, self.es, self.er, self.fs,
+            self.ps,
         ) = refs
         self.half = grad_ref.shape[-1] // 2
         self.main = self.half - split
         self.steps = 2 * grad_ref.shape[0]
+        self.layers = layers
+        self.per_layer = grad_ref.shape[0] // layers
+        self.pieces = (self.per_layer - 4) // 2
 
     @staticmethod
-    def scratch(outers, rows, width, split):
+    def scratch(layers, outers, rows, width, pieces, split):
         dma = pltpu.SemaphoreType.DMA
         many = outers - 1
         half = width // 2
@@ -577,13 +616,14 @@
             pltpu.VMEM((4, outers, rows, main), BF16),
             pltpu.VMEM((4, rows, main), BF16),
             pltpu.VMEM((4, rows, half), F32),
+            pltpu.VMEM((layers, rows, pieces * width), F32),
             dma((2,)),
             dma((4,)), dma((4,)),
             dma((6,)), dma((6,)),
             dma((6,)), dma((6,)),
             dma((6, many)), dma((6, many)),
             dma((4,)), dma((4,)),
-            dma((4,)),
+            dma((4,)), dma((layers,)),
         ]
 
     def cols(self, offset, size):
@@ -634,10 +674,79 @@
         s = lax.rem(k, 4)
         return remote(self.end_buf.at[s], self.last_buf.at[s], self.es.at[s], self.er.at[s], self.me.other_role())
 
-    def f_copy(self, k):
-        s = lax.rem(k, 4)
-        cols = self.cols(lax.rem(k, 2) * self.half, self.half)
-        return pltpu.make_async_copy(self.fin_buf.at[s], self.out.at[lax.div(k, 2), :, cols], self.fs.at[s])
+    def kind(self, k):
+        n = lax.div(k, 2)
+        return self.layers - 1 - lax.div(n, self.per_layer), lax.rem(n, self.per_layer)
+
+    def is_expand(self, k):
+        _, q = self.kind(k)
+        return (q < 2 * self.pieces) & (lax.rem(q, 2) == 1)
+
+    def store(self, k):
+        s, half = lax.rem(k, 4), lax.rem(k, 2)
+        layer, q = self.kind(k)
+        width, pieces = 2 * self.half, self.pieces
+        rows = self.fin_buf.shape[1]
+        cols = self.cols(half * self.half, self.half)
+        piece = lax.div(q, 2)
+
+        def put(dst):
+            pltpu.make_async_copy(self.fin_buf.at[s], dst, self.fs.at[s]).start()
+
+        @pl.when((q < 2 * pieces) & (lax.rem(q, 2) == 0))
+        def _():
+            put(self.shrink.at[layer, pl.ds(pl.multiple_of(piece * rows, rows), rows), cols])
+
+        @pl.when(q == 2 * pieces)
+        def _():
+            put(self.outer.at[layer, :, cols])
+
+        @pl.when(q > 2 * pieces)
+        def _():
+            put(self.inner.at[layer, :, self.cols(lax.rem(q - 2 * pieces, 3) * width + half * self.half, self.half)])
+
+        @pl.when(self.is_expand(k))
+        def _():
+            self.spread(layer, piece, half, s)
+
+            @pl.when((piece == pieces - 1) & (half == 1))
+            def _():
+                self.spread_copy(layer).start()
+
+    def spread_copy(self, layer):
+        return pltpu.make_async_copy(self.spread_buf.at[layer], self.expand.at[layer], self.ps.at[layer])
+
+    def spread(self, layer, piece, half, s):
+        rows, pieces = self.fin_buf.shape[1], self.pieces
+        tiles = self.half // 128
+        first = lax.broadcasted_iota(jnp.int32, (rows, 128), 1) < 64
+
+        def some(i):
+            value = self.fin_buf[s, :, tile(i, 128)]
+            if rows != 64:
+                self.spread_buf[layer, :, tile((2 * piece + half) * tiles + i, 128)] = value
+                return
+            moved = pltpu.roll(value, 64, 1)
+            at = (half * tiles + i) * pieces + lax.div(piece, 2)
+            even, odd = tile(at, 128), tile(at + pieces // 2, 128)
+
+            @pl.when(lax.rem(piece, 2) == 0)
+            def _():
+                self.spread_buf[layer, :, even] = jnp.where(first, value, self.spread_buf[layer, :, even])
+                self.spread_buf[layer, :, odd] = jnp.where(first, moved, self.spread_buf[layer, :, odd])
+
+            @pl.when(lax.rem(piece, 2) == 1)
+            def _():
+                self.spread_buf[layer, :, even] = jnp.where(first, self.spread_buf[layer, :, even], moved)
+                self.spread_buf[layer, :, odd] = jnp.where(first, self.spread_buf[layer, :, odd], value)
+
+        loop(tiles, some)
+
+    def stored(self, k):
+        @pl.when(jnp.logical_not(self.is_expand(k)))
+        def _():
+            s = lax.rem(k, 4)
+            pltpu.make_async_copy(self.fin_buf.at[s], self.outer.at[0, :, pl.ds(0, self.half)], self.fs.at[s]).wait()
 
     def step(self, t):
         me, count, split, main = self.me, self.steps, self.split, self.main
@@ -708,7 +817,7 @@
 
             @pl.when(k >= 4)
             def _():
-                self.f_copy(k - 4).wait()
+                self.stored(k - 4)
 
             mid = main - split
             mine = self.end_buf[s].astype(F32)
@@ -726,17 +835,18 @@
                 self.fin_buf[s, :, split:main] = theirs[:, split:] + mine[:, :mid]
                 self.fin_buf[s, :, main:] = mine[:, mid:]
 
-            self.f_copy(k).start()
+            self.store(k)
 
     def finish(self):
-        for k in range(self.steps - 4, self.steps):
-            self.f_copy(k).wait()
+        loop(4, lambda i: self.stored(self.steps - 4 + i))
+        for layer in range(self.layers):
+            self.spread_copy(layer).wait()
 
 
 def backward_kernel(
     layers, outers, split,
     full_ref, saved_ref, hidden_ref, probs_ref, cot_ref, table_ref, pick_ref, used_ref,
-    grad_ref, out_ref, frames_grad_ref, table_out_ref,
+    grad_ref, inner_ref, outer_ref, expand_ref, shrink_ref, frames_grad_ref, table_out_ref,
     g_buf, acc_buf, h_buf, w_buf, low_buf, act_buf, give_buf, back_buf, p_buf, stage_buf, tab_sum, tab_in, tab_role, tab_back,
     act_sem, h_sem, w_sem, p_sem, stage_sem, ks, kr, ts, tr, rs_sem, rr_sem, out_sem, *reduce_refs,
 ):
@@ -751,7 +861,7 @@
     shard = grad_ref.shape[-2]
     tile_outers = WIDE // (4 * shard)
     block = 128
-    reduce = Reduce(me, grad_ref, out_ref, split, reduce_refs)
+    reduce = Reduce(me, layers, grad_ref, (inner_ref, outer_ref, expand_ref, shrink_ref), split, reduce_refs)
     me.greet()
 
     def load_rows(i):
@@ -933,13 +1043,12 @@
             out = jnp.concatenate([out[:HD, :rows], out[HD:, rows:]], axis=0)
             act_buf[7, r, cols] = out.T.astype(BF16)
 
-        segment = micro * pairs // 8
-
         def attend_some(s):
-            loop(segment, lambda i: attend(s * segment + i))
+            loop(3, lambda i: attend(s * 3 + i))
             service(2 * pieces + 2 + s)
 
-        loop(8, attend_some)
+        loop(5, attend_some)
+        loop(micro * pairs - 15, lambda i: attend(15 + i))
 
         def some_rows(i):
             r = tile(i, block)
@@ -957,48 +1066,57 @@
         def add(cols, value):
             acc_buf[:, cols] += value
 
-        def project(i):
-            get_w(base + lax.rem(2 + i, 3), 1 - i).start()
-            part = act_buf.at[1 + i]
-            n = n0 + 2 * pieces + 1 + i
-
-            @pl.when(me.role == 0)
-            def _():
-                produce(n, act_buf.at[8], part)
-
-            @pl.when(me.role == 1)
-            def _():
-                produce(n, act_buf.at[8], part, (act_buf.at[9], give_buf.at[i]))
-
-            service(2 * pieces + 10 + 2 * i)
-            get_w(base + 1 + i, i).wait()
-            through(part, i, add)
-
-            @pl.when(me.role == 1)
-            def _():
-                def first(cols, value):
-                    h_buf[:, cols] = value
-
-                def second(cols, value):
-                    low_buf[:, cols] = (h_buf[:, cols] + value).astype(BF16)
-
-                @pl.when(i == 0)
-                def _():
-                    through(give_buf.at[0], 0, first)
-
-                @pl.when(i == 1)
-                def _():
-                    through(give_buf.at[1], 1, second)
-                    back_copy().start()
-
-            service(2 * pieces + 11 + 2 * i)
-
-        loop(2, project)
+        def first(cols, value):
+            h_buf[:, cols] = value
+
+        def second(cols, value):
+            low_buf[:, cols] = (h_buf[:, cols] + value).astype(BF16)
+
+        get_w(base + 2, 1).start()
+        get_w(base + 1, 0).wait()
+
+        @pl.when(me.role == 1)
+        def _():
+            through(give_buf.at[0], 0, first)
+
+        through(act_buf.at[1], 0, add)
+        service(2 * pieces + 7)
+        get_w(base, 0).start()
+        get_w(base + 2, 1).wait()
+
+        @pl.when(me.role == 1)
+        def _():
+            through(give_buf.at[1], 1, second)
+            back_copy().start()
+
         get_hidden(l, 0).start()
-        produce(n0 + 2 * pieces + 3, act_buf.at[8], act_buf.at[7])
-        service(2 * pieces + 14)
+        through(act_buf.at[2], 1, add)
+        service(2 * pieces + 8)
         get_w(base, 0).wait()
         through(act_buf.at[7], 0, add)
+        service(2 * pieces + 9)
+        n = n0 + 2 * pieces + 1
+
+        @pl.when(me.role == 0)
+        def _():
+            def some(i):
+                produce(n + i, act_buf.at[8], act_buf.at[1 + i])
+                service(2 * pieces + 10 + 2 * i)
+                service(2 * pieces + 11 + 2 * i)
+
+            loop(2, some)
+
+        @pl.when(me.role == 1)
+        def _():
+            def some(i):
+                produce(n + i, act_buf.at[8], act_buf.at[1 + i], (act_buf.at[9], give_buf.at[i]))
+                service(2 * pieces + 10 + 2 * i)
+                service(2 * pieces + 11 + 2 * i)
+
+            loop(2, some)
+
+        produce(n + 2, act_buf.at[8], act_buf.at[7])
+        service(2 * pieces + 14)
         service(2 * pieces + 15)
 
         @pl.when(me.role == 0)
@@ -1057,6 +1175,7 @@
 
 def backward(full, saved, hidden, probs, cotangent, table, pick, used, outers, layers, shard, collective_id):
     count = full.shape[0]
+    pieces = (count // layers - 4) // 2
     rows_all, width = cotangent.shape
     keys = probs.shape[2]
     small = table.shape[0]
@@ -1070,12 +1189,15 @@
         functools.partial(backward_kernel, layers, outers, split),
         out_shape=(
             jax.ShapeDtypeStruct((count, outers, 2, 2, shard, width), BF16),
-            jax.ShapeDtypeStruct((count, shard, width), F32),
+            jax.ShapeDtypeStruct((layers, shard, 3 * width), F32),
+            jax.ShapeDtypeStruct((layers, shard, width), F32),
+            jax.ShapeDtypeStruct((layers, shard, pieces * width), F32),
+            jax.ShapeDtypeStruct((layers, pieces * shard, width), F32),
             jax.ShapeDtypeStruct(grid_rows, BF16),
             jax.ShapeDtypeStruct((small, 128), F32),
         ),
         in_specs=[any_space, any_space, any_space, any_space, vmem, vmem, vmem, vmem],
-        out_specs=(any_space, any_space, any_space, vmem),
+        out_specs=(any_space,) * 6 + (vmem,),
         scratch_shapes=[
             pltpu.VMEM(grid_rows, F32),
             pltpu.VMEM(grid_rows, F32),
@@ -1094,7 +1216,7 @@
             dma((10,)), dma(()), dma((2,)), dma((2,)), dma((2,)), dma((layers,)), dma((layers,)),
             dma((devices - 1,)), dma((devices - 1,)), dma(()), dma(()), dma(()),
         ]
-        + Reduce.scratch(outers, shard, width, split),
+        + Reduce.scratch(layers, outers, shard, width, pieces, split),
         compiler_params=pltpu.CompilerParams(
             collective_id=collective_id, has_side_effects=True, vmem_limit_bytes=60 * 2**20
         ),
@@ -1103,24 +1225,11 @@
 
 
 def prepare(
-    inner_weight, outer_weight, expand_weight, shrink_weight, causal_gain, causal_shift,
-    section_scale, section_shift, prompt_lengths, target_lengths, sections, rows,
+    shard, causal_gain, causal_shift, section_scale, section_shift, prompt_lengths, target_lengths, sections, rows,
 ):
     is_target = lax.axis_index("role") == 1
-    layers, shard, _ = inner_weight.shape
-    width = outer_weight.shape[2]
-    devices = width // shard
-    pieces = expand_weight.shape[2] // width
     segs = section_scale.shape[0]
     micro = prompt_lengths.shape[0]
-    outer = outer_weight[:, None]
-    inner = inner_weight.reshape(layers, shard, 3, width).transpose(0, 2, 1, 3)
-    expand = expand_weight.reshape(layers, shard, devices, pieces, shard).transpose(0, 3, 1, 2, 4)
-    expand = expand.reshape(layers, pieces, 1, shard, width)
-    shrink = shrink_weight.reshape(layers, pieces, 1, shard, width)
-    feed = jnp.concatenate([expand, shrink], axis=2).reshape(layers, 2 * pieces, shard, width)
-    parts = jnp.concatenate([inner, outer, feed], axis=1).reshape(-1, shard, width)
-
     small = jnp.concatenate(
         [causal_gain, causal_shift, section_scale.reshape(2 * segs, -1), section_shift.reshape(2 * segs, -1)], axis=0
     )
@@ -1148,7 +1257,7 @@
     none = jnp.zeros_like(section)
     first, second = 4 + 2 * section, 4 + 2 * segs + 2 * section
     used = jnp.stack([none, none + 2, none + 1, none + 3, first, second, first + 1, second + 1])
-    return parts, piece, used, bias
+    return piece, used, bias
 
 
 def body(
@@ -1161,26 +1270,23 @@
     outers = devices // 4
     pieces = expand_weight.shape[2] // width
     segs = section_scale.shape[0]
-    parts, piece, used, bias = prepare(
-        inner_weight, outer_weight, expand_weight, shrink_weight, causal_gain, causal_shift,
-        section_scale, section_shift, prompt_lengths, target_lengths, sections, rows,
+    piece, used, bias = prepare(
+        shard, causal_gain, causal_shift, section_scale, section_shift, prompt_lengths, target_lengths, sections, rows
     )
+    if shard != 64:
+        expand_weight = expand_weight.reshape(layers, shard, devices, pieces, shard).transpose(0, 1, 3, 2, 4).reshape(layers, shard, -1)
     entries = jnp.arange(piece.shape[0], dtype=jnp.int32)
     pick = (used[:, :, None] == entries[None, None, :]).astype(BF16)
     pick_t = (used[:, None, :] == entries[None, :, None]).astype(BF16)
     full, saved, hidden, probs, mixed, table = forward(
-        parts, frames.reshape(micro * rows, width), piece, pick, bias, outers, layers, 0
+        inner_weight, outer_weight, expand_weight, shrink_weight, frames.reshape(micro * rows, width), piece, pick, bias, outers, 0
     )
-    _, owned, frames_grad, small = backward(
+    _, inner_grad, outer_grad, expand_grad, shrink_grad, frames_grad, small = backward(
         full.reshape(-1, width, width), saved, hidden, probs, cotangent.reshape(micro * rows, width),
         table, pick, pick_t, outers, layers, shard, 1,
     )
-    owned = owned.reshape(layers, -1, shard, width)[::-1]
-    feed = owned[:, : 2 * pieces].reshape(layers, pieces, 2, shard, width)
-    inner_grad = jnp.concatenate([owned[:, 2 * pieces + i] for i in (3, 1, 2)], axis=2)
-    outer_grad = owned[:, 2 * pieces]
-    expand_grad = feed[:, :, 1].reshape(layers, pieces, shard, devices, shard).transpose(0, 2, 3, 1, 4).reshape(layers, shard, -1)
-    shrink_grad = feed[:, :, 0].reshape(layers, pieces * shard, width)
+    if shard != 64:
+        expand_grad = expand_grad.reshape(layers, shard, pieces, devices, shard).transpose(0, 1, 3, 2, 4).reshape(layers, shard, -1)
     per = 128 // shard
     spot = (lax.axis_index("dp") % per) * shard
     small = lax.dynamic_slice(small, (0, spot), (small.shape[0], shard))

time: 640 us -> 583 us (0.911)
  local copies, waits for them, and re-layouts: 45.6 us -> 15.1 us
  Pallas kernels: 583 us -> 560 us
    reshape x4 -> x0, local copies, waits for them, and re-layouts: 14.8 us -> none  [the longest x1 5.56 us: body(): feed[:, :, 1].reshape(layers, pieces, shard, devices, shard)]
    slice x4 -> x0, local copies, waits for them, and re-layouts: 12.6 us -> none  [the longest x2 6.98 us: body(): feed = owned[:, :2 * pieces].reshape(layers, pieces, 2, shard, width)]
    pallas_call x1, Pallas kernels: 312 us -> 300 us  [backward(): pl.pallas_call(functools.partial(backward_kernel, layers, outers, split),...]
    pallas_call x1, Pallas kernels: 271 us -> 260 us  [forward(): pl.pallas_call(functools.partial(forward_kernel, layers, outers, split),...]
    transpose x3 -> x0, local copies, waits for them, and re-layouts: 9.02 us -> none  [the longest x1 6.85 us: body(): feed[:, :, 1].reshape(layers, pieces, shard, devices, shard)]
where the time goes in v4:
time: 583 us; the launch traced here: 582 us
  Pallas kernels  560 us (96%)
  local copies, waits for them, and re-layouts  15.1 us (3%)
  other arithmetic  6.23 us (1%)
    pallas_call x1, Pallas kernels, backward(): pl.pallas_call(functools.partial(backward_kernel, layers, outers, split),...  300 us
    pallas_call x1, Pallas kernels, forward(): pl.pallas_call(functools.partial(forward_kernel, layers, outers, split),...  260 us

profile of v4, /device:TPU:0, one launch (start us, length us, event | category | flops | bytes accessed | tf_op | source)
XLA Modules:
  0.0 582.0 jit_solution(14180786909900853880)
XLA Ops:
  0.6 0.7 reshape.242
  1.3 0.7 reshape.241
  2.0 0.7 pad_maximum_fusion
  2.8 0.2 dynamic_update_slice.3.piece_ref
  2.9 0.7 slice_bitcast_fusion.4
  3.6 0.1 select_reduce_fusion.6
  3.8 0.7 slice_bitcast_fusion.5
  4.4 0.1 select_reduce_fusion.7
  4.6 0.7 subtract_subtract_fusion.2
  5.4 0.7 slice_bitcast_fusion.3
  6.1 0.1 select_reduce_fusion.1
  6.4 0.1 select_reduce_fusion.3
  6.6 1.5 fusion.pick_ref
  8.1 0.2 compare_and_fusion
  8.4 0.2 compare_and_fusion.2
  8.7 1.2 select_convert_fusion.bias_ref
  9.9 260.2 %gather_and_forward.1 = (bf16[24,4,2,2,64,1024]{5,4,3,2,1,0:T(8,128)(2,1)}, bf16[2,17,512,1024]{3,2,1,0:T(8,128)(2,1)}, f32[2,2,512,1024]{3,2,1,0:T(8,128)}, bf1...) custom-call(bf16[2,64,3072]{2,1,0:T(8,128)(2,1)} %inner_ref.1, ...), custom_call_target="tpu_custom_call" | custom-call | tf_op jit(solution)/shard_map/gather_and_forward/pallas_call | solution.py:545
  270.2 0.8 fusion.1.used_ref
  270.9 299.7 %backward_and_reduce.1 = (bf16[24,4,2,2,64,1024]{5,4,3,2,1,0:T(8,128)(2,1)}, f32[2,64,3072]{2,1,0:T(8,128)}, f32[2,64,1024]{2,1,0:T(8,128)}, f32[2,64,4096]{2,1,...) custom-call(bf16[24,1024,1024]{2,1,0:T(8,128)(2,1)} %bitcast.43, ...), custom_call_target="tpu_custom_call" | custom-call | tf_op jit(solution)/shard_map/backward_and_reduce/pallas_call | solution.py:1188
  570.6 1.4 fusion.9
  572.0 0.9 fusion.8
  572.9 0.6 reshape.247
  573.5 0.6 reshape.248
  574.1 1.0 copy.30
  575.1 1.0 copy.31
  576.0 1.1 copy.32
  577.2 0.2 copy-done.5
  577.4 0.8 copy.33
  578.2 0.2 copy-done.1
  578.4 1.3 copy.34
  579.7 1.0 copy-done
  580.7 1.3 copy.35
  (31 shorter events, 0.6 us)
Async XLA Ops:
  2.9 7.0 %copy-start.6 = (bf16[32,128]{1,0:T(8,128)(2,1)}, bf16[32,128]{1,0:T(8,128)(2,1)S(1)}, u32[]{:S(2)}) copy-start(bf16[32,128]{1,0:T(8,128)(2,1)S(1)} %dynamic_update_slice.3.piece_ref) | copy-start | bytes 24580
  270.9 303.2 %copy-start.3 = (bf16[512,1024]{1,0:T(8,128)(2,1)S(1)}, bf16[512,1024]{1,0:T(8,128)(2,1)}, u32[]{:S(2)}) copy-start(bf16[512,1024]{1,0:T(8,128)(2,1)} %get-tuple-element.22) | copy-start | bytes 3145732
  570.6 4.5 copy-start.4
  574.1 1.9 copy-start.2
  576.0 1.4 copy-start.5
  576.0 2.3 copy-start.1
  578.4 2.3 copy-start

commit v5 on v4

--- a/solution.py
+++ b/solution.py
@@ -107,32 +107,42 @@
 
 
 class Gather:
-    lag = 7
+    lag = 9
 
     def __init__(self, me, part_ref, full_ref, split, sems):
         self.me, self.part, self.full, self.split = me, part_ref, full_ref, split
-        self.own_sem, self.zs, self.zr, self.xs, self.xr, self.us, self.ur, self.vs, self.vr, self.cs, self.cr = sems
+        (
+            self.own_sem, self.zs, self.zr, self.fs, self.xs, self.xr, self.us, self.ur, self.vs, self.vr, self.cs, self.cr,
+            self.qxs, self.qxr, self.qzs, self.qzr, self.qfs,
+        ) = sems
         self.half = part_ref.shape[-1] // 2
         self.main = self.half - split
         self.steps = 2 * part_ref.shape[0]
+        self.chain = me.outers == 4
 
     @staticmethod
     def semaphores(many):
         dma = pltpu.SemaphoreType.DMA
         return [
-            dma((8,)),
-            dma((8, many)), dma((8, many)),
-            dma((8,)), dma((8,)),
+            dma((4,)),
+            dma((6, many)), dma((6, many)), dma((6,)),
+            dma((6,)), dma((6,)),
             dma((12, many)), dma((12, many)),
-            dma((8,)), dma((8,)),
-            dma((8,)), dma((8,)),
+            dma((6,)), dma((6,)),
+            dma((4,)), dma((4,)),
+            dma((6,)), dma((6,)), dma((6, many)), dma((6, many)), dma((6,)),
         ]
 
     def cols(self, h, offset, size):
         return pl.ds(pl.multiple_of(lax.rem(h, 2) * self.half + offset, 128), size)
 
-    def main_cols(self, h):
+    def main_cols(self, h, odd):
+        if odd:
+            return self.cols(h, self.me.role * 2 * self.split, 2 * self.split)
         return self.cols(h, self.me.role * self.split, self.main)
+
+    def cross_cols(self, h):
+        return self.cols(h, (2 - self.me.role) * self.split, self.split)
 
     def give_cols(self, h):
         return self.cols(h, self.me.role * self.main, self.split)
@@ -142,30 +152,94 @@
 
     def before(self, by):
         return lax.rem(self.me.outer - by + self.me.outers, self.me.outers)
+
+    def sends(self, by, action):
+        self.unless(by, {1: 3, 3: 0}, action)
+
+    def takes(self, by, action):
+        self.unless(by, {1: 0, 3: 3}, action)
+
+    def unless(self, by, ends, action):
+        if self.chain and by in ends:
+            pl.when(self.me.outer != ends[by])(action)
+        else:
+            action()
+
+    def passes(self, action):
+        if self.chain:
+            z = self.me.outer
+
+            @pl.when((z == 1) | (z == 2))
+            def _():
+                action(6 - 3 * z, self.me.at(self.me.role, 3 * z - 3, self.me.pair, self.me.core), 2 * z - 2)
+
+    def gets(self, action):
+        if self.chain:
+            z = self.me.outer
+
+            @pl.when((z == 0) | (z == 3))
+            def _():
+                action(3 - z, jnp.where(z == 0, 0, 2))
 
     def own(self, h):
         me, cols = self.me, self.cols(h, 0, self.half)
         return pltpu.make_async_copy(
-            self.part.at[lax.div(h, 2), :, cols], self.full.at[lax.div(h, 2), me.outer, me.pair, me.core, :, cols], self.own_sem.at[lax.rem(h, 8)]
+            self.part.at[lax.div(h, 2), :, cols],
+            self.full.at[lax.div(h, 2), me.outer, me.pair, me.core, :, cols],
+            self.own_sem.at[lax.rem(h, 4)],
         )
 
-    def z_copy(self, h, by):
-        me, cols, s = self.me, self.main_cols(h), lax.rem(h, 8)
+    def z_copy(self, h, by, odd):
+        me, cols, s = self.me, self.main_cols(h, odd), lax.rem(h, 6)
         return remote(
             self.part.at[lax.div(h, 2), :, cols],
             self.full.at[lax.div(h, 2), me.outer, me.pair, me.core, :, cols],
             self.zs.at[s, by - 1], self.zr.at[s, by - 1], me.along(by),
         )
 
-    def z_wait(self, h, by):
-        me, s = self.me, lax.rem(h, 8)
-        dst = self.full.at[lax.div(h, 2), self.before(by), me.pair, me.core, :, self.main_cols(h)]
-        remote(dst, dst, self.zs.at[s, by - 1], self.zr.at[s, by - 1], me.along(by)).wait_recv()
-
-    def x_copy(self, h, pair):
-        me, s = self.me, lax.rem(h, 8)
-        ref = self.full.at[lax.div(h, 2), :, pair, me.core, :, self.main_cols(h)]
+    def z_block(self, h, block, odd):
+        return self.full.at[lax.div(h, 2), block, self.me.pair, self.me.core, :, self.main_cols(h, odd)]
+
+    def z_wait(self, h, block, index, odd):
+        dst, s = self.z_block(h, block, odd), lax.rem(h, 6)
+        remote(dst, dst, self.fs.at[s], self.zr.at[s, index], self.me.across()).wait_recv()
+
+    def f_copy(self, h, block, to, index, odd):
+        ref, s = self.z_block(h, block, odd), lax.rem(h, 6)
+        return remote(ref, ref, self.fs.at[s], self.zr.at[s, index], to)
+
+    def x_copy(self, h, pair, odd):
+        me, s = self.me, lax.rem(h, 6)
+        ref = self.full.at[lax.div(h, 2), :, pair, me.core, :, self.main_cols(h, odd)]
         return remote(ref, ref, self.xs.at[s], self.xr.at[s], me.across())
+
+    def qx_copy(self, h):
+        me, cols, s = self.me, self.cross_cols(h), lax.rem(h, 6)
+        return remote(
+            self.part.at[lax.div(h, 2), :, cols],
+            self.full.at[lax.div(h, 2), me.outer, me.pair, me.core, :, cols],
+            self.qxs.at[s], self.qxr.at[s], me.across(),
+        )
+
+    def qx_wait(self, h):
+        me, s = self.me, lax.rem(h, 6)
+        dst = self.full.at[lax.div(h, 2), me.outer, 1 - me.pair, me.core, :, self.cross_cols(h)]
+        remote(dst, dst, self.qxs.at[s], self.qxr.at[s], me.across()).wait_recv()
+
+    def q_block(self, h, block):
+        return self.full.at[lax.div(h, 2), block, :, self.me.core, :, self.cross_cols(h)]
+
+    def qz_copy(self, h, by):
+        ref, s = self.q_block(h, self.me.outer), lax.rem(h, 6)
+        return remote(ref, ref, self.qzs.at[s, by - 1], self.qzr.at[s, by - 1], self.me.along(by))
+
+    def qz_wait(self, h, block, index):
+        dst, s = self.q_block(h, block), lax.rem(h, 6)
+        remote(dst, dst, self.qfs.at[s], self.qzr.at[s, index], self.me.across()).wait_recv()
+
+    def qf_copy(self, h, block, to, index):
+        ref, s = self.q_block(h, block), lax.rem(h, 6)
+        return remote(ref, ref, self.qfs.at[s], self.qzr.at[s, index], to)
 
     def u_copy(self, h, by, cols):
         me, s = self.me, lax.rem(h, 12)
@@ -173,16 +247,26 @@
         return remote(ref, ref, self.us.at[s, by - 1], self.ur.at[s, by - 1], me.other_role())
 
     def v_copy(self, h, cols):
-        me, s = self.me, lax.rem(h, 8)
+        me, s = self.me, lax.rem(h, 6)
         ref = self.full.at[lax.div(h, 2), :, 1 - me.pair, me.core, :, cols]
         return remote(ref, ref, self.vs.at[s], self.vr.at[s], me.other_role())
 
     def c_copy(self, h, core):
-        s = lax.rem(h, 8)
+        s = lax.rem(h, 4)
         ref = self.full.at[lax.div(h, 2), :, :, core, :, self.cols(h, 0, self.half)]
         return remote(ref, ref, self.cs.at[s], self.cr.at[s], self.me.sibling())
 
     def step(self, t):
+        for odd in (False, True):
+            pl.when(lax.rem(t, 2) == int(odd))(functools.partial(self.stages, t, odd))
+
+        @pl.when((t >= 9) & (t < self.steps + 9))
+        def _():
+            h = t - 9
+            self.c_copy(h, 1 - self.me.core).wait_recv()
+            self.c_copy(h, self.me.core).wait_send()
+
+    def stages(self, t, odd):
         me, count = self.me, self.steps
         others = range(1, me.outers)
 
@@ -190,43 +274,60 @@
         def _():
             self.own(t).start()
             for by in others:
-                self.z_copy(t, by).start()
+                self.sends(by, lambda: self.z_copy(t, by, odd).start())
+            if odd:
+                self.qx_copy(t).start()
 
         @pl.when((t >= 2) & (t < count + 2))
         def _():
             h = t - 2
             self.own(h).wait()
             for by in others:
-                self.z_wait(h, by)
-            self.x_copy(h, me.pair).start()
+                self.takes(by, lambda: self.z_wait(h, self.before(by), by - 1, odd))
+            self.passes(lambda block, to, index: self.f_copy(h, block, to, index, odd).start())
+            if odd:
+                self.qx_wait(h)
+                for by in others:
+                    self.sends(by, lambda: self.qz_copy(h, by).start())
+
+        @pl.when((t >= 4) & (t < count + 4))
+        def _():
+            h = t - 4
+            self.gets(lambda block, index: self.z_wait(h, block, index, odd))
+            self.x_copy(h, me.pair, odd).start()
             for by in others:
                 self.u_copy(h, by, self.give_cols(h)).start()
-
-        @pl.when((t >= 4) & (t < count + 4))
-        def _():
-            h = t - 4
-            self.x_copy(h, 1 - me.pair).wait_recv()
+            for by in others:
+                self.sends(by, lambda: self.z_copy(h, by, odd).wait_send())
+            self.passes(lambda block, to, index: self.f_copy(h, block, to, index, odd).wait_send())
+            if odd:
+                for by in others:
+                    self.takes(by, lambda: self.qz_wait(h, self.before(by), by - 1))
+                self.passes(lambda block, to, index: self.qf_copy(h, block, to, index).start())
+                self.qx_copy(h).wait_send()
+
+        @pl.when((t >= 6) & (t < count + 6))
+        def _():
+            h = t - 6
+            self.x_copy(h, 1 - me.pair, odd).wait_recv()
             self.v_copy(h, self.give_cols(h)).start()
-            for by in others:
-                self.z_copy(h, by).wait_send()
-
-        @pl.when((t >= 6) & (t < count + 6))
-        def _():
-            h = t - 6
+            if odd:
+                self.gets(lambda block, index: self.qz_wait(h, block, index))
+                for by in others:
+                    self.sends(by, lambda: self.qz_copy(h, by).wait_send())
+                self.passes(lambda block, to, index: self.qf_copy(h, block, to, index).wait_send())
+
+        @pl.when((t >= 8) & (t < count + 8))
+        def _():
+            h = t - 8
             for by in others:
                 self.u_copy(h, by, self.take_cols(h)).wait_recv()
             self.v_copy(h, self.take_cols(h)).wait_recv()
             self.c_copy(h, me.core).start()
             for by in others:
                 self.u_copy(h, by, self.give_cols(h)).wait_send()
-            self.x_copy(h, me.pair).wait_send()
+            self.x_copy(h, me.pair, odd).wait_send()
             self.v_copy(h, self.give_cols(h)).wait_send()
-
-        @pl.when((t >= 7) & (t < count + 7))
-        def _():
-            h = t - 7
-            self.c_copy(h, 1 - me.core).wait_recv()
-            self.c_copy(h, me.core).wait_send()
 
 
 def loop(count, action):
@@ -581,16 +682,16 @@
 
 
 class Reduce:
-    lag = 8
+    lag = 10
 
     def __init__(self, me, layers, grad_ref, out_refs, split, refs):
         self.me, self.grad, self.split = me, grad_ref, split
-        self.inner, self.outer, self.expand, self.shrink = out_refs
+        self.inner_out, self.outer_out, self.expand_out, self.shrink_out = out_refs
         (
-            self.own_buf, self.core_buf, self.role_buf, self.pair_buf, self.outer_buf, self.last_buf, self.sum_buf, self.low_buf,
-            self.end_buf, self.fin_buf, self.spread_buf,
-            self.own_sem, self.cs, self.cr, self.ys, self.yr, self.xs, self.xr, self.zs, self.zr, self.es, self.er, self.fs,
-            self.ps,
+            self.own_buf, self.core_buf, self.role_buf, self.pair_buf, self.outer_buf, self.end_in, self.last_buf, self.sum_buf,
+            self.low_buf, self.cross_end, self.cross_in, self.cross_sum, self.cross_pair, self.end_buf, self.fin_buf, self.spread_buf,
+            self.own_sem, self.cs, self.cr, self.ys, self.yr, self.xs, self.xr, self.zs, self.zr, self.ns, self.nr,
+            self.qas, self.qar, self.qzs, self.qzr, self.qxs, self.qxr, self.es, self.er, self.fs, self.ps,
         ) = refs
         self.half = grad_ref.shape[-1] // 2
         self.main = self.half - split
@@ -598,6 +699,7 @@
         self.layers = layers
         self.per_layer = grad_ref.shape[0] // layers
         self.pieces = (self.per_layer - 4) // 2
+        self.chain = me.outers == 4
 
     @staticmethod
     def scratch(layers, outers, rows, width, pieces, split):
@@ -608,29 +710,73 @@
         return [
             pltpu.VMEM((2, outers, 2, rows, half), BF16),
             pltpu.VMEM((4, outers, 2, rows, half), BF16),
-            pltpu.VMEM((6, outers, 2, rows, split), BF16),
+            pltpu.VMEM((8, outers, 2, rows, split), BF16),
             pltpu.VMEM((6, outers, rows, main), BF16),
-            pltpu.VMEM((6, many, rows, main), BF16),
-            pltpu.VMEM((4, rows, main), BF16),
+            pltpu.VMEM((10, many, rows, main), BF16),
+            pltpu.VMEM((8, rows, main), BF16),
+            pltpu.VMEM((4, rows, half), BF16),
             pltpu.VMEM((6, outers, 2, rows, half), BF16),
-            pltpu.VMEM((4, outers, rows, main), BF16),
-            pltpu.VMEM((4, rows, main), BF16),
+            pltpu.VMEM((6, outers, rows, main), BF16),
+            pltpu.VMEM((8, 2, rows, split), BF16),
+            pltpu.VMEM((8, many, 2, rows, split), BF16),
+            pltpu.VMEM((6, 2, rows, split), BF16),
+            pltpu.VMEM((6, rows, split), BF16),
+            pltpu.VMEM((4, rows, half), BF16),
             pltpu.VMEM((4, rows, half), F32),
             pltpu.VMEM((layers, rows, pieces * width), F32),
             dma((2,)),
             dma((4,)), dma((4,)),
+            dma((8,)), dma((8,)),
             dma((6,)), dma((6,)),
+            dma((10, many)), dma((10, many)),
+            dma((8,)), dma((8,)),
+            dma((8,)), dma((8,)),
+            dma((8, many)), dma((8, many)),
             dma((6,)), dma((6,)),
-            dma((6, many)), dma((6, many)),
             dma((4,)), dma((4,)),
             dma((4,)), dma((layers,)),
         ]
 
+    def sends(self, by, action):
+        self.unless(by, {1: 3, 3: 0}, action)
+
+    def takes(self, by, action):
+        self.unless(by, {1: 0, 3: 3}, action)
+
+    def unless(self, by, ends, action):
+        if self.chain and by in ends:
+            pl.when(self.me.outer != ends[by])(action)
+        else:
+            action()
+
+    def ends(self, action):
+        if self.chain:
+            z = self.me.outer
+
+            @pl.when((z == 0) | (z == 3))
+            def _():
+                action(3 - z, self.me.at(self.me.role, 1 + lax.div(z, 3), self.me.pair, self.me.core))
+
+    def inner(self, action):
+        if self.chain:
+            z = self.me.outer
+
+            @pl.when((z == 1) | (z == 2))
+            def _():
+                action(6 - 3 * z)
+
+    def early(self, by, action):
+        if self.chain and by == 2:
+            z = self.me.outer
+            pl.when((z == 0) | (z == 3))(action)
+        else:
+            self.sends(by, action)
+
     def cols(self, offset, size):
         return pl.ds(pl.multiple_of(offset, 128), size)
 
-    def main_cols(self):
-        return self.cols(self.me.role * self.split, self.main)
+    def main_cols(self, odd):
+        return pl.ds(0, self.main) if odd else self.cols(self.me.role * self.split, self.main)
 
     def keep_cols(self):
         return self.cols(self.me.role * self.main, self.split)
@@ -650,29 +796,54 @@
         return remote(self.part(k, 1 - self.me.core), self.core_buf.at[s], self.cs.at[s], self.cr.at[s], self.me.sibling())
 
     def y_copy(self, k):
+        s = lax.rem(k, 8)
+        return remote(
+            self.sum_buf.at[lax.rem(k, 6), :, :, :, self.give_cols()], self.role_buf.at[s], self.ys.at[s], self.yr.at[s],
+            self.me.other_role(),
+        )
+
+    def x_copy(self, k, odd):
         s = lax.rem(k, 6)
         return remote(
-            self.sum_buf.at[s, :, :, :, self.give_cols()], self.role_buf.at[s], self.ys.at[s], self.yr.at[s], self.me.other_role()
-        )
-
-    def x_copy(self, k):
-        s = lax.rem(k, 6)
-        return remote(
-            self.sum_buf.at[s, :, 1 - self.me.pair, :, self.main_cols()],
+            self.sum_buf.at[s, :, 1 - self.me.pair, :, self.main_cols(odd)],
             self.pair_buf.at[s], self.xs.at[s], self.xr.at[s], self.me.across(),
         )
 
+    def toward(self, by):
+        return lax.rem(self.me.outer + by, self.me.outers)
+
     def z_copy(self, k, by):
+        s = lax.rem(k, 10)
+        return remote(
+            self.low_buf.at[lax.rem(k, 6), self.toward(by)], self.outer_buf.at[s, by - 1],
+            self.zs.at[s, by - 1], self.zr.at[s, by - 1], self.me.along(by),
+        )
+
+    def n_copy(self, k, block, to):
+        s = lax.rem(k, 8)
+        return remote(self.low_buf.at[lax.rem(k, 6), block], self.end_in.at[s], self.ns.at[s], self.nr.at[s], to)
+
+    def cross(self, k, block):
+        return self.sum_buf.at[lax.rem(k, 6), block, :, :, pl.ds(self.main, self.split)]
+
+    def qa_copy(self, k, block, to):
+        s = lax.rem(k, 8)
+        return remote(self.cross(k, block), self.cross_end.at[s], self.qas.at[s], self.qar.at[s], to)
+
+    def qz_copy(self, k, by):
+        s = lax.rem(k, 8)
+        return remote(
+            self.cross(k, self.toward(by)), self.cross_in.at[s, by - 1], self.qzs.at[s, by - 1], self.qzr.at[s, by - 1], self.me.along(by)
+        )
+
+    def qx_copy(self, k):
         s = lax.rem(k, 6)
-        me = self.me
-        return remote(
-            self.low_buf.at[lax.rem(k, 4), lax.rem(me.outer + by, me.outers)], self.outer_buf.at[s, by - 1],
-            self.zs.at[s, by - 1], self.zr.at[s, by - 1], me.along(by),
-        )
-
-    def e_copy(self, k):
+        return remote(self.cross_sum.at[s, 1 - self.me.pair], self.cross_pair.at[s], self.qxs.at[s], self.qxr.at[s], self.me.across())
+
+    def e_copy(self, k, odd):
         s = lax.rem(k, 4)
-        return remote(self.end_buf.at[s], self.last_buf.at[s], self.es.at[s], self.er.at[s], self.me.other_role())
+        cols = pl.ds(0, self.half if odd else self.main)
+        return remote(self.end_buf.at[s, :, cols], self.last_buf.at[s, :, cols], self.es.at[s], self.er.at[s], self.me.other_role())
 
     def kind(self, k):
         n = lax.div(k, 2)
@@ -695,15 +866,15 @@
 
         @pl.when((q < 2 * pieces) & (lax.rem(q, 2) == 0))
         def _():
-            put(self.shrink.at[layer, pl.ds(pl.multiple_of(piece * rows, rows), rows), cols])
+            put(self.shrink_out.at[layer, pl.ds(pl.multiple_of(piece * rows, rows), rows), cols])
 
         @pl.when(q == 2 * pieces)
         def _():
-            put(self.outer.at[layer, :, cols])
+            put(self.outer_out.at[layer, :, cols])
 
         @pl.when(q > 2 * pieces)
         def _():
-            put(self.inner.at[layer, :, self.cols(lax.rem(q - 2 * pieces, 3) * width + half * self.half, self.half)])
+            put(self.inner_out.at[layer, :, self.cols(lax.rem(q - 2 * pieces, 3) * width + half * self.half, self.half)])
 
         @pl.when(self.is_expand(k))
         def _():
@@ -714,7 +885,7 @@
                 self.spread_copy(layer).start()
 
     def spread_copy(self, layer):
-        return pltpu.make_async_copy(self.spread_buf.at[layer], self.expand.at[layer], self.ps.at[layer])
+        return pltpu.make_async_copy(self.spread_buf.at[layer], self.expand_out.at[layer], self.ps.at[layer])
 
     def spread(self, layer, piece, half, s):
         rows, pieces = self.fin_buf.shape[1], self.pieces
@@ -746,20 +917,25 @@
         @pl.when(jnp.logical_not(self.is_expand(k)))
         def _():
             s = lax.rem(k, 4)
-            pltpu.make_async_copy(self.fin_buf.at[s], self.outer.at[0, :, pl.ds(0, self.half)], self.fs.at[s]).wait()
+            pltpu.make_async_copy(self.fin_buf.at[s], self.outer_out.at[0, :, pl.ds(0, self.half)], self.fs.at[s]).wait()
 
     def step(self, t):
+        for odd in (False, True):
+            pl.when((lax.rem(t, 2) == int(odd)) & (t >= 0))(functools.partial(self.stages, t, odd))
+
+    def stages(self, t, same):
         me, count, split, main = self.me, self.steps, self.split, self.main
         others = range(1, me.outers)
-
-        @pl.when((t >= 0) & (t < count))
+        low = self.low_buf
+
+        @pl.when(t < count)
         def _():
             self.own(t).start()
             self.c_copy(t).start()
 
         @pl.when((t >= 1) & (t < count + 1))
         def _():
-            k = t - 1
+            k, odd = t - 1, not same
             self.own(k).wait()
             self.c_copy(k).wait()
 
@@ -768,72 +944,126 @@
                 self.sum_buf[lax.rem(k, 6), o, p] = self.own_buf[lax.rem(k, 2), o, p] + self.core_buf[lax.rem(k, 4), o, p]
 
             loop(2 * me.outers, add)
-            self.y_copy(k).start()
+            if odd:
+                self.ends(lambda block, to: self.qa_copy(k, block, to).start())
+            else:
+                self.y_copy(k).start()
 
         @pl.when((t >= 3) & (t < count + 3))
         def _():
-            k = t - 3
+            k, odd = t - 3, not same
             s = lax.rem(k, 6)
-            self.y_copy(k).wait()
-            keep = self.keep_cols()
-
-            def add(i):
-                o, p = lax.div(i, 2), lax.rem(i, 2)
-                self.sum_buf[s, o, p, :, keep] = self.sum_buf[s, o, p, :, keep] + self.role_buf[s, o, p]
-
-            loop(2 * me.outers, add)
-            self.x_copy(k).start()
+            if odd:
+                self.x_copy(k, odd).start()
+
+                def take(block):
+                    self.qa_copy(k, block, me.across()).wait_recv()
+                    for p in range(2):
+                        self.sum_buf[s, block, p, :, main:] = self.sum_buf[s, block, p, :, main:] + self.cross_end[lax.rem(k, 8), p]
+
+                self.inner(take)
+                self.ends(lambda block, to: self.qa_copy(k, block, to).wait_send())
+                for by in others:
+                    self.sends(by, lambda: self.qz_copy(k, by).start())
+            else:
+                self.y_copy(k).wait()
+                keep = self.keep_cols()
+
+                def add(i):
+                    o, p = lax.div(i, 2), lax.rem(i, 2)
+                    self.sum_buf[s, o, p, :, keep] = self.sum_buf[s, o, p, :, keep] + self.role_buf[lax.rem(k, 8), o, p]
+
+                loop(2 * me.outers, add)
+                self.x_copy(k, odd).start()
 
         @pl.when((t >= 5) & (t < count + 5))
         def _():
-            k = t - 5
+            k, odd = t - 5, not same
             s = lax.rem(k, 6)
-            self.x_copy(k).wait()
-            cols = self.main_cols()
+            self.x_copy(k, odd).wait()
+            cols = self.main_cols(odd)
 
             def add(o):
-                self.low_buf[lax.rem(k, 4), o] = self.sum_buf[s, o, me.pair, :, cols] + self.pair_buf[s, o]
+                low[s, o] = self.sum_buf[s, o, me.pair, :, cols] + self.pair_buf[s, o]
 
             loop(me.outers, add)
+            self.ends(lambda block, to: self.n_copy(k, block, to).start())
             for by in others:
-                self.z_copy(k, by).start()
+                self.early(by, lambda: self.z_copy(k, by).start())
+            if odd:
+                self.cross_sum[s] = self.sum_buf[s, me.outer, :, :, main:]
+                for by in others:
+
+                    def take():
+                        self.qz_copy(k, by).wait_recv()
+                        self.cross_sum[s] = self.cross_sum[s] + self.cross_in[lax.rem(k, 8), by - 1]
+
+                    self.takes(by, take)
+                    self.sends(by, lambda: self.qz_copy(k, by).wait_send())
+                self.qx_copy(k).start()
 
         @pl.when((t >= 7) & (t < count + 7))
         def _():
-            k = t - 7
-            for by in others:
-                self.z_copy(k, by).wait()
-            total = self.low_buf[lax.rem(k, 4), me.outer].astype(F32)
-            for by in others:
-                total = total + self.outer_buf[lax.rem(k, 6), by - 1].astype(F32)
-            self.end_buf[lax.rem(k, 4)] = total.astype(BF16)
-            self.e_copy(k).start()
-
-        @pl.when((t >= 8) & (t < count + 8))
-        def _():
-            k = t - 8
-            s = lax.rem(k, 4)
-            self.e_copy(k).wait()
+            k, odd = t - 7, not same
+            s = lax.rem(k, 6)
+
+            def take(block):
+                self.n_copy(k, block, me.across()).wait_recv()
+                low[s, block] = low[s, block] + self.end_in[lax.rem(k, 8)]
+                self.z_copy(k, 2).start()
+
+            self.inner(take)
+            self.ends(lambda block, to: self.n_copy(k, block, to).wait_send())
+            if odd:
+                self.qx_copy(k).wait()
+                cross = self.cross_sum[s, me.pair].astype(F32) + self.cross_pair[s].astype(F32)
+                self.end_buf[lax.rem(k, 4), :, main:] = cross.astype(BF16)
+
+        @pl.when((t >= 9) & (t < count + 9))
+        def _():
+            k, odd = t - 9, not same
+            e = lax.rem(k, 4)
 
             @pl.when(k >= 4)
             def _():
                 self.stored(k - 4)
 
-            mid = main - split
-            mine = self.end_buf[s].astype(F32)
-            theirs = self.last_buf[s].astype(F32)
-
-            @pl.when(me.role == 0)
-            def _():
-                self.fin_buf[s, :, :split] = mine[:, :split]
-                self.fin_buf[s, :, split:main] = mine[:, split:] + theirs[:, :mid]
-                self.fin_buf[s, :, main:] = theirs[:, mid:]
-
-            @pl.when(me.role == 1)
-            def _():
-                self.fin_buf[s, :, :split] = theirs[:, :split]
-                self.fin_buf[s, :, split:main] = theirs[:, split:] + mine[:, :mid]
-                self.fin_buf[s, :, main:] = mine[:, mid:]
+            self.fin_buf[e, :, :main] = low[lax.rem(k, 6), me.outer].astype(F32)
+            for by in others:
+
+                def take():
+                    self.z_copy(k, by).wait_recv()
+                    self.fin_buf[e, :, :main] = self.fin_buf[e, :, :main] + self.outer_buf[lax.rem(k, 10), by - 1].astype(F32)
+
+                self.takes(by, take)
+                self.sends(by, lambda: self.z_copy(k, by).wait_send())
+            self.end_buf[e, :, :main] = self.fin_buf[e, :, :main].astype(BF16)
+            self.e_copy(k, odd).start()
+
+        @pl.when((t >= 10) & (t < count + 10))
+        def _():
+            k, odd = t - 10, same
+            s = lax.rem(k, 4)
+            self.e_copy(k, odd).wait()
+
+            if odd:
+                self.fin_buf[s] = self.end_buf[s].astype(F32) + self.last_buf[s].astype(F32)
+            else:
+                mid = main - split
+                mine = self.end_buf[s, :, :main].astype(F32)
+                theirs = self.last_buf[s, :, :main].astype(F32)
+
+                @pl.when(me.role == 0)
+                def _():
+                    self.fin_buf[s, :, :split] = mine[:, :split]
+                    self.fin_buf[s, :, split:main] = mine[:, split:] + theirs[:, :mid]
+                    self.fin_buf[s, :, main:] = theirs[:, mid:]
+
+                @pl.when(me.role == 1)
+                def _():
+                    self.fin_buf[s, :, :split] = theirs[:, :split]
+                    self.fin_buf[s, :, split:main] = theirs[:, split:] + mine[:, :mid]
+                    self.fin_buf[s, :, main:] = mine[:, mid:]
 
             self.store(k)
 
@@ -862,14 +1092,10 @@
     tile_outers = WIDE // (4 * shard)
     block = 128
     reduce = Reduce(me, layers, grad_ref, (inner_ref, outer_ref, expand_ref, shrink_ref), split, reduce_refs)
-    me.greet()
-
     def load_rows(i):
         r = tile(i, block)
         g_buf[r, :] = cot_ref[r, :].astype(F32)
 
-    loop(rows_all // block, load_rows)
-    tab_sum[...] = jnp.zeros_like(tab_sum)
 
     def get(l, item, slot):
         return pltpu.make_async_copy(saved_ref.at[l, item], act_buf.at[slot], act_sem.at[slot])
@@ -915,7 +1141,7 @@
 
         loop(rows_all // block, some)
 
-    def norm_back(index, l):
+    def norm_back(index, l, between):
         def some(i):
             r = tile(i, block)
             unit, inverse = normalize(h_buf[r, :])
@@ -928,7 +1154,20 @@
                 rest = (values - high.astype(F32)).astype(BF16)
                 tab_sum[...] += dot(picked, high) + dot(picked, rest)
 
-        loop(rows_all // block, some)
+        loop(rows_all // block // 2, some)
+        between()
+        loop(rows_all // block // 2, lambda i: some(i + rows_all // block // 2))
+
+    def prefetch(l):
+        get(l, 7, 0).start()
+        get(l, 8, 1).start()
+        get(l, 8 + pieces, 3).start()
+        get_w(l * per_layer + 5, 0).start()
+
+    prefetch(layers - 1)
+    loop(rows_all // block, load_rows)
+    tab_sum[...] = jnp.zeros_like(tab_sum)
+    me.greet()
 
     def layer(turn):
         l = layers - 1 - turn
@@ -938,10 +1177,6 @@
         def service(index):
             reduce.step(2 * (n0 - 1) + index)
 
-        get(l, 7, 0).start()
-        get(l, 8, 1).start()
-        get(l, 8 + pieces, 3).start()
-        get_w(base + 5, 0).start()
         get_hidden(l, 1).start()
         lower(low_buf, g_buf)
         acc_buf[...] = jnp.zeros_like(acc_buf)
@@ -993,8 +1228,7 @@
 
         get_probs(0).start()
         get_hidden(l, 1).wait()
-        service(2 * pieces)
-        norm_back(1, l)
+        norm_back(1, l, lambda: service(2 * pieces))
         lower(low_buf, g_buf)
         get(l, 6, 0).wait()
         service(2 * pieces + 1)
@@ -1101,8 +1335,7 @@
         def _():
             def some(i):
                 produce(n + i, act_buf.at[8], act_buf.at[1 + i])
-                service(2 * pieces + 10 + 2 * i)
-                service(2 * pieces + 11 + 2 * i)
+                service(2 * pieces + 10 + i)
 
             loop(2, some)
 
@@ -1110,14 +1343,18 @@
         def _():
             def some(i):
                 produce(n + i, act_buf.at[8], act_buf.at[1 + i], (act_buf.at[9], give_buf.at[i]))
-                service(2 * pieces + 10 + 2 * i)
-                service(2 * pieces + 11 + 2 * i)
+                service(2 * pieces + 10 + i)
 
             loop(2, some)
 
         produce(n + 2, act_buf.at[8], act_buf.at[7])
-        service(2 * pieces + 14)
-        service(2 * pieces + 15)
+        service(2 * pieces + 12)
+
+        @pl.when(turn < layers - 1)
+        def _():
+            prefetch(l - 1)
+
+        service(2 * pieces + 13)
 
         @pl.when(me.role == 0)
         def _():
@@ -1130,7 +1367,8 @@
             loop(rows_all // block, some)
 
         get_hidden(l, 0).wait()
-        norm_back(0, l)
+        norm_back(0, l, lambda: service(2 * pieces + 14))
+        service(2 * pieces + 15)
 
         @pl.when(me.role == 1)
         def _():

time: 583 us -> 584 us (level); the launches traced: 582 us -> 573 us
  Pallas kernels: 560 us -> 551 us
    pallas_call x1, Pallas kernels: 260 us -> 241 us  [forward(): pl.pallas_call(functools.partial(forward_kernel, layers, outers, split),...]
    pallas_call x1, Pallas kernels: 300 us -> 309 us  [backward(): pl.pallas_call(functools.partial(backward_kernel, layers, outers, split),...]
where the time goes in v5:
time: 584 us; the launch traced here: 573 us
  Pallas kernels  551 us (94%)
  local copies, waits for them, and re-layouts  15.1 us (3%)
  other arithmetic  6.23 us (1%)
    pallas_call x1, Pallas kernels, backward(): pl.pallas_call(functools.partial(backward_kernel, layers, outers, split),...  309 us
    pallas_call x1, Pallas kernels, forward(): pl.pallas_call(functools.partial(forward_kernel, layers, outers, split),...  241 us

profile of v5, /device:TPU:0, one launch (start us, length us, event | category | flops | bytes accessed | tf_op | source)
XLA Modules:
  0.0 573.0 jit_solution(8087016627811974767)
XLA Ops:
  0.6 0.7 reshape.242
  1.3 0.7 reshape.241
  2.0 0.7 pad_maximum_fusion
  2.8 0.2 dynamic_update_slice.3.piece_ref
  2.9 0.7 slice_bitcast_fusion.4
  3.6 0.1 select_reduce_fusion.6
  3.8 0.7 slice_bitcast_fusion.5
  4.4 0.1 select_reduce_fusion.7
  4.6 0.7 subtract_subtract_fusion.2
  5.4 0.7 slice_bitcast_fusion.3
  6.1 0.1 select_reduce_fusion.1
  6.4 0.1 select_reduce_fusion.3
  6.6 1.5 fusion.pick_ref
  8.1 0.2 compare_and_fusion
  8.4 0.2 compare_and_fusion.2
  8.7 1.2 select_convert_fusion.bias_ref
  9.9 241.1 %gather_and_forward.1 = (bf16[24,4,2,2,64,1024]{5,4,3,2,1,0:T(8,128)(2,1)}, bf16[2,17,512,1024]{3,2,1,0:T(8,128)(2,1)}, f32[2,2,512,1024]{3,2,1,0:T(8,128)}, bf1...) custom-call(bf16[2,64,3072]{2,1,0:T(8,128)(2,1)} %inner_ref.1, ...), custom_call_target="tpu_custom_call" | custom-call | tf_op jit(solution)/shard_map/gather_and_forward/pallas_call | solution.py:646
  251.0 0.8 fusion.1.used_ref
  251.8 309.4 %backward_and_reduce.1 = (bf16[24,4,2,2,64,1024]{5,4,3,2,1,0:T(8,128)(2,1)}, f32[2,64,3072]{2,1,0:T(8,128)}, f32[2,64,1024]{2,1,0:T(8,128)}, f32[2,64,4096]{2,1,...) custom-call(bf16[24,1024,1024]{2,1,0:T(8,128)(2,1)} %bitcast.43, ...), custom_call_target="tpu_custom_call" | custom-call | tf_op jit(solution)/shard_map/backward_and_reduce/pallas_call | solution.py:1426
  561.2 1.4 fusion.9
  562.6 0.9 fusion.8
  563.5 0.6 reshape.247
  564.1 0.6 reshape.248
  564.7 1.0 copy.30
  565.7 1.0 copy.31
  566.7 1.1 copy.32
  567.8 0.2 copy-done.5
  568.0 0.8 copy.33
  568.8 0.2 copy-done.1
  569.0 1.3 copy.34
  570.3 1.0 copy-done
  571.3 1.3 copy.35
  (31 shorter events, 0.6 us)
Async XLA Ops:
  2.9 7.0 %copy-start.6 = (bf16[32,128]{1,0:T(8,128)(2,1)}, bf16[32,128]{1,0:T(8,128)(2,1)S(1)}, u32[]{:S(2)}) copy-start(bf16[32,128]{1,0:T(8,128)(2,1)S(1)} %dynamic_update_slice.3.piece_ref) | copy-start | bytes 24580
  251.8 312.9 %copy-start.3 = (bf16[512,1024]{1,0:T(8,128)(2,1)S(1)}, bf16[512,1024]{1,0:T(8,128)(2,1)}, u32[]{:S(2)}) copy-start(bf16[512,1024]{1,0:T(8,128)(2,1)} %get-tuple-element.22) | copy-start | bytes 3145732
  561.2 4.5 copy-start.4
  564.7 1.9 copy-start.2
  566.7 1.4 copy-start.5
  566.7 2.3 copy-start.1
  569.0 2.3 copy-start
